TPU v7x, 32 devices: a whole 2x2x4 slice. The times are simulated.
32 devices in a mesh: frame: 4 (over y, x), pix: 8 (over z, core).
Axes of the slice: x: 2, y: 2, z: 4, core: 2. Of those that a mesh axis runs over, the one named last changes fastest.
Arguments:
- frames: bfloat16 [128, 4, 128, 512], P('frame', None, 'pix'), may hold values from -26 to 26
- prev_fg: bfloat16 [128, 4, 128, 512], P('frame', None, 'pix'), may hold values from -3 to 3
- depth_valid: int32 [128, 128, 512], P('frame', 'pix'), may hold values 0 or 1
- sketch: float32 [128, 64], replicated, may hold values from -0.5 to 0.5
- tv_weight: float32 [4], replicated, may hold values from 0.1 to 1
Outputs:
- background: bfloat16 [128, 4, 128, 512], P('frame', None, 'pix')
- foreground: bfloat16 [128, 4, 128, 512], P('frame', None, 'pix')
All inputs are finite; a program needn't handle non-finite values. No bound on the sum of `depth_valid` on one device may be relied on, other than what follows from the above.
Results may differ from a plain program's by a relative error of at most 0.012.
The roundings to bfloat16 on the way count: a program that leaves them out, or rounds other values in their place, can miss the bound.
Values may be sent and summed in bfloat16 or wider, within the bound.
No kernel may reach another device: no remote copies, remote signals or barrier semaphores. Data moves between devices by JAX's collectives and lax.ppermute only.
A program may use at most 64 MiB of HBM per device.

v0:
```python
import functools

import jax
import jax.numpy as jnp
from jax import lax
from jax.experimental import pallas as pl
from jax.experimental.pallas import tpu as pltpu
from jax.sharding import PartitionSpec as P

POWER = 3
NSWEEP = 5
STEP_SIZE = 0.125
SUB = 8
LANE = 128
PACK = 16
VMEM_BYTES = 32 * 1024 * 1024


def from_behind(value, axis, steps):
    count = lax.axis_size(axis)
    leading, last = (max(0, -steps), min(count, count - steps))
    return lax.ppermute(value, axis, [(source, source + steps) for source in range(leading, last)])


def power_of_two(count):
    return count & (count - 1) == 0


def partner(index, offset, count, back=False):
    if power_of_two(count):
        return index ^ offset
    return (index + (count - offset if back else offset)) % count


def swap(value, axis, offset):
    count = lax.axis_size(axis)
    pairs = [(source, partner(source, offset, count)) for source in range(count)]
    return lax.ppermute(value, axis, pairs)


def all_sum(value, axis):
    count = lax.axis_size(axis)
    if not power_of_two(count):
        return lax.psum(value, axis)
    bit = 1
    while bit < count:
        fours = (count // bit).bit_length() % 2 == 1
        offsets = (bit, 2 * bit, 3 * bit) if fours else (bit,)
        others = [swap(value, axis, offset) for offset in offsets]
        for other in others:
            value = value + other
        bit *= len(offsets) + 1
    return value


def exact_dot(left, right, left_dim, right_dim):
    return lax.dot_general(
        left,
        right,
        (((left_dim,), (right_dim,)), ((), ())),
        precision=lax.Precision.HIGHEST,
        preferred_element_type=jnp.float32,
    )


def short_dot(left, right, left_dim, right_dim):
    return lax.dot_general(
        left,
        right,
        (((left_dim,), (right_dim,)), ((), ())),
        preferred_element_type=jnp.float32,
    )


def eliminate(square, sides):
    rank = square.shape[0]
    width = sides[0].shape[1]
    blocks = rank // SUB
    sub_ids = lax.broadcasted_iota(jnp.int32, (SUB, width), 0)
    square = jnp.concatenate([square, jnp.zeros((rank, width - rank), jnp.float32)], axis=1)

    def in_blocks(rows):
        return [rows[SUB * b : SUB * (b + 1)] for b in range(blocks)]

    def row_of(rows, j):
        return jnp.broadcast_to(rows[j : j + 1], (SUB, width))

    def col_of(rows, j):
        return jnp.broadcast_to(rows[:, j : j + 1], (SUB, width))

    square = in_blocks(square)
    sides = [in_blocks(side) for side in sides]
    solved = [[] for _ in sides]
    for k in range(blocks):
        below = range(k, blocks)
        cols = {b: [col_of(square[b], SUB * k + j) for j in range(SUB)] for b in below}
        pivots = jnp.ones((SUB, width), jnp.float32)
        for j in range(SUB):
            pivot = row_of(cols[k][j], j)
            inverse = 1.0 / pivot
            pivots = jnp.where(sub_ids == j, pivot, pivots)
            col_rows = {i: row_of(cols[k][i], j) for i in range(j + 1, SUB)}
            square_row = row_of(square[k], j)
            side_rows = [row_of(side[k], j) for side in sides]
            for b in below:
                ratio = cols[b][j] * inverse
                if b == k:
                    ratio = jnp.where(sub_ids > j, ratio, 0.0)
                for i in range(j + 1, SUB):
                    cols[b][i] = cols[b][i] - ratio * col_rows[i]
                square[b] = square[b] - ratio * square_row
                for side, side_row in zip(sides, side_rows):
                    side[b] = side[b] - ratio * side_row
        scale = lax.rsqrt(pivots)
        for rows, side in zip(solved, sides):
            rows.append(side[k] * scale)
    return [jnp.concatenate(rows, axis=0) for rows in solved]


def mixing_kernel(gram_ref, sketch_ref, mixing_ref):
    gram = gram_ref[...]
    basis = sketch_ref[...]
    for turn in range(POWER):
        image = exact_dot(basis, gram, 1, 1)
        (basis,) = eliminate(exact_dot(basis, image, 1, 1), [image])
    image = exact_dot(basis, gram, 1, 1)
    left, right = eliminate(exact_dot(basis, image, 1, 1), [basis, image])
    mixing_ref[...] = exact_dot(right, left, 0, 0).astype(mixing_ref.dtype)


def mixing_matrix(gram, sketch):
    return pl.pallas_call(
        mixing_kernel,
        out_shape=jax.ShapeDtypeStruct(gram.shape, jnp.bfloat16),
        name="mixing",
    )(gram, sketch.T)


def tile(j):
    return pl.ds(LANE * j, LANE)


def vmem():
    return pl.BlockSpec(memory_space=pltpu.VMEM)


def smem():
    return pl.BlockSpec(memory_space=pltpu.SMEM)


def anywhere():
    return pl.BlockSpec(memory_space=pl.ANY)


def residual_kernel(last, picks, channel_ref, frames_ref, prev_ref, valid_ref, *refs):
    outs, (now, before, ok, sems) = refs[: len(picks)], refs[len(picks) :]
    _, _, count, rows, cols = now.shape
    each = now.shape[1]
    valid_copy = pltpu.make_async_copy(valid_ref, ok, sems.at[0])
    copies = []
    for n, pick in enumerate(picks):
        for c in range(each):
            chan = channel_ref[pick] + c
            at = 1 + 2 * (n * each + c)
            copies.append(
                (
                    pltpu.make_async_copy(frames_ref.at[:, chan], now.at[n, c], sems.at[at]),
                    pltpu.make_async_copy(prev_ref.at[:, chan], before.at[n, c], sems.at[at + 1]),
                )
            )
    for copy in copies[0]:
        copy.start()
    valid_copy.start()
    for pair in copies[1:]:
        for copy in pair:
            copy.start()
    valid_copy.wait()
    for n, pick in enumerate(picks):
        for c in range(each):
            for copy in copies[n * each + c]:
                copy.wait()
            keep = jnp.where(channel_ref[pick] + c == last, 0.0, 1.0)
            for g in range(count // PACK):
                some = pl.ds(g * PACK, PACK)
                for j in range(cols // LANE):
                    valid = jnp.where(ok[some, :, tile(j)] != 0, 1.0, keep)
                    diff = now[n, c, some, :, tile(j)].astype(jnp.float32)
                    diff = diff - before[n, c, some, :, tile(j)].astype(jnp.float32)
                    turned = jnp.swapaxes(diff * valid, 0, 1)
                    outs[n][c, :, some, tile(j)] = turned.astype(jnp.bfloat16)


def residual(channels, picks, each, frames, prev_fg, depth_valid):
    count, chans, rows, cols = frames.shape
    held = pltpu.VMEM((len(picks), each, count, rows, cols), jnp.bfloat16)
    return pl.pallas_call(
        functools.partial(residual_kernel, chans - 1, picks),
        in_specs=[smem(), anywhere(), anywhere(), anywhere()],
        out_specs=[vmem()] * len(picks),
        out_shape=[jax.ShapeDtypeStruct((each, rows, count, cols), jnp.bfloat16)] * len(picks),
        scratch_shapes=[
            held,
            held,
            pltpu.VMEM((count, rows, cols), jnp.int32),
            pltpu.SemaphoreType.DMA((1 + 2 * each * len(picks),)),
        ],
        compiler_params=pltpu.CompilerParams(vmem_limit_bytes=VMEM_BYTES),
        name="residual",
    )(channels, frames, prev_fg, depth_valid)


def interleave_kernel(frames_ref, valid_ref, order_ref, out_ref, top_ref, bottom_ref):
    count, chans, rows, cols = frames_ref.shape
    edge = NSWEEP
    for c in range(chans + 1):
        for g in range(count // PACK):
            some = pl.ds(g * PACK, PACK)
            if c < chans:
                lines = frames_ref[some, c]
            else:
                lines = valid_ref[some].astype(jnp.float32).astype(jnp.bfloat16)
            lines = short_dot(lines.reshape(PACK * rows, cols), order_ref[...], 1, 0)
            for j in range(cols // LANE):
                turned = lines[:, LANE * j : LANE * (j + 1)].reshape(PACK, rows, LANE)
                turned = jnp.swapaxes(turned, 0, 1).astype(jnp.bfloat16)
                out_ref[c, :, some, tile(j)] = turned
                top_ref[c, :, some, tile(j)] = turned[:edge]
                bottom_ref[c, :, some, tile(j)] = turned[rows - edge :]


def interleaved(frames, depth_valid, order):
    count, chans, rows, cols = frames.shape
    return pl.pallas_call(
        interleave_kernel,
        in_specs=[vmem()] * 3,
        out_specs=[vmem()] * 3,
        out_shape=[
            jax.ShapeDtypeStruct((chans + 1, height, count, cols), jnp.bfloat16)
            for height in (rows, NSWEEP, NSWEEP)
        ],
        compiler_params=pltpu.CompilerParams(vmem_limit_bytes=VMEM_BYTES),
        name="interleave",
    )(frames, depth_valid, order)


def gram_kernel(groups, nval, ids_ref, *refs):
    blocks, (gram_ref, all_ref) = refs[:groups], refs[-2:]
    lines, count, cols = blocks[0].shape
    for k, block in enumerate(blocks):
        start = pl.multiple_of(ids_ref[groups + k] * count, count)
        all_ref[:, pl.ds(start, count), :] = block[...]
    total = jnp.zeros(gram_ref.shape, jnp.float32)
    for r in range(lines):
        total = total + short_dot(all_ref[r], all_ref[r], 1, 1)
    gram_ref[...] = total / nval


def gram_terms(ids, blocks, nval, after):
    groups = len(blocks)
    lines, count, cols = blocks[0].shape
    every = groups * count
    return pl.pallas_call(
        functools.partial(gram_kernel, groups, nval),
        in_specs=[smem()] + [vmem()] * groups + [anywhere()] * len(after),
        out_specs=[vmem()] * 2,
        out_shape=[
            jax.ShapeDtypeStruct((every, every), jnp.float32),
            jax.ShapeDtypeStruct((lines, every, cols), jnp.bfloat16),
        ],
        compiler_params=pltpu.CompilerParams(vmem_limit_bytes=VMEM_BYTES),
        name="gram",
    )(ids, *blocks, *after)


def spread_kernel(picks, edges, n_after, ids_ref, mixing_ref, all_ref, *refs):
    refs = refs[n_after:]
    pieces, weights = refs[: len(picks)], refs[-1]
    lines, count, cols = pieces[0].shape
    for n, pick in enumerate(picks):
        start = pl.multiple_of(ids_ref[pick] * count, count)
        weights[pl.ds(n * count, count), :] = mixing_ref[pl.ds(start, count), :]
    chosen = weights[...]
    for r in range(lines):
        back = short_dot(chosen, all_ref[r], 1, 0).astype(jnp.bfloat16)
        for n, piece in enumerate(pieces):
            piece[r] = back[n * count : (n + 1) * count]
    if edges:
        each, edge = refs[len(picks)].shape[:2]
        rows = lines // each
        for c in range(each):
            refs[len(picks)][c] = pieces[0][c * rows : c * rows + edge]
            refs[len(picks) + 1][c] = pieces[0][(c + 1) * rows - edge : (c + 1) * rows]


def spread(ids, picks, mixing, pixels, groups, each, edges=False, after=()):
    lines, every, cols = pixels.shape
    count = every // groups
    piece = jax.ShapeDtypeStruct((lines, count, cols), jnp.bfloat16)
    rim = jax.ShapeDtypeStruct((each, NSWEEP, count, cols), jnp.bfloat16)
    shapes = [piece] * len(picks) + [rim] * (2 if edges else 0)
    return pl.pallas_call(
        functools.partial(spread_kernel, picks, edges, len(after)),
        in_specs=[smem(), vmem(), vmem()] + [anywhere()] * len(after),
        out_specs=[vmem()] * len(shapes),
        out_shape=shapes,
        scratch_shapes=[pltpu.VMEM((len(picks) * count, every), jnp.bfloat16)],
        compiler_params=pltpu.CompilerParams(vmem_limit_bytes=VMEM_BYTES),
        name="spread",
    )(ids, mixing, pixels, *after)


def rims_kernel(count, *refs):
    pieces, (top_ref, bottom_ref) = refs[:count], refs[-2:]
    edge = top_ref.shape[1]
    at = 0
    for piece in pieces:
        for c in range(piece.shape[0]):
            top_ref[at] = piece[c, :edge]
            bottom_ref[at] = piece[c, piece.shape[1] - edge :]
            at += 1


def rims(pieces, after):
    each, _, count, cols = pieces[0].shape
    rim = jax.ShapeDtypeStruct((each * len(pieces), NSWEEP, count, cols), jnp.bfloat16)
    return pl.pallas_call(
        functools.partial(rims_kernel, len(pieces)),
        in_specs=[vmem()] * len(pieces) + [anywhere()] * len(after),
        out_specs=[vmem()] * 2,
        out_shape=[rim, rim],
        name="rims",
    )(*pieces, *after)


def variation_kernel(n_after, scale_ref, at_ref, order_ref, *refs):
    own, above, below = refs[0:2], refs[2:4], refs[4:6]
    fg_out, bg_out, token_ref, source, first, second, flat_fg, flat_bg, fg_held, bg_held, sems = refs[
        6 + n_after :
    ]
    chan, rim, each_at = at_ref[0], at_ref[1], at_ref[2]
    edge = NSWEEP
    nf = PACK
    _, rows, count, cols = own[1].shape
    chans = own[0].shape[0] - 1
    tiles = cols // LANE
    lines = rows + 2 * edge
    lam, up_flag, down_flag = scale_ref[0], scale_ref[1], scale_ref[2]
    step = STEP_SIZE / lam
    end = lax.broadcasted_iota(jnp.int32, (nf, LANE), 1) == LANE - 1
    strips = ((0, above, rim), (edge, own, each_at), (edge + rows, below, rim))
    token_ref[...] = jnp.zeros_like(token_ref)

    def load(ref, i):
        return [ref[i, :, tile(j)] for j in range(tiles)]

    def divergence(over, here, beside):
        left = [pltpu.roll(beside[-1], 1, 1)] + beside[:-1]
        return [(here[j] - over[j]) + (beside[j] - left[j]) for j in range(tiles)]

    def smooth(i, over, here, beside):
        div = divergence(over, here, beside)
        image = load(source, i)
        return [image[j] - STEP_SIZE * div[j] for j in range(tiles)]

    @pl.loop(0, count // nf)
    def some_frames(g):
        some = pl.ds(pl.multiple_of(g * nf, nf), nf)
        copies = [
            pltpu.make_async_copy(held.at[g], out.at[some, chan], sems.at[n, g])
            for n, (held, out) in enumerate(((fg_held, fg_out), (bg_held, bg_out)))
        ]
        for h in range(rows):
            for j in range(tiles):
                back = own[1][each_at, h, some, tile(j)].astype(jnp.float32)
                flat_bg[j, pl.ds(h, nf, stride=rows), :] = back
        for j in range(tiles):
            bg_held[g, :, :, tile(j)] = flat_bg[j].astype(jnp.bfloat16).reshape(nf, rows, LANE)
        copies[1].start()

        for start, (frames, back), at in strips:
            height = back.shape[1]
            moved = back[at, :, some, :].reshape(height * nf, cols)
            moved = short_dot(moved, order_ref[...], 1, 0)
            for h in range(height):
                image = frames[chan, h, some, :].astype(jnp.float32)
                source[start + h] = (image - moved[h * nf : (h + 1) * nf]) * step

        @pl.when(chan == chans - 1)
        def mask():
            for start, (frames, back), at in strips:
                for h in range(back.shape[1]):
                    valid = frames[chans, h, some, :].astype(jnp.float32)
                    source[start + h] = source[start + h] * valid

        for sweep in range(NSWEEP):
            here = beside = None
            if sweep:
                here, beside = load(first, sweep), load(second, sweep)
                now = smooth(sweep, load(first, sweep - 1), here, beside)
            else:
                now = load(source, 0)
            for i in range(sweep, lines - 1 - sweep):
                next_here = next_beside = None
                if sweep:
                    next_here, next_beside = load(first, i + 1), load(second, i + 1)
                    later = smooth(i + 1, here, next_here, next_beside)
                else:
                    later = load(source, i + 1)
                right = now[1:] + [jnp.where(end, now[-1], pltpu.roll(now[0], LANE - 1, 1))]
                for j in range(tiles):
                    down = later[j] - now[j]
                    if i == edge - 1:
                        down = down * up_flag
                    if i == edge + rows - 1:
                        down = down * down_flag
                    across = right[j] - now[j]
                    square = down * down + across * across
                    size = square * lax.rsqrt(jnp.maximum(square, 1e-30))
                    scale = pl.reciprocal(1.0 + size, approx=True)
                    first[i, :, tile(j)] = (here[j] - down if sweep else -down) * scale
                    second[i, :, tile(j)] = (beside[j] - across if sweep else -across) * scale
                now, here, beside = later, next_here, next_beside

        over = load(first, edge - 1)
        for h in range(rows):
            here, beside = load(first, edge + h), load(second, edge + h)
            image = smooth(edge + h, over, here, beside)
            for j in range(tiles):
                flat_fg[j, pl.ds(h, nf, stride=rows), :] = image[j] * (lam / STEP_SIZE)
            over = here
        fg = jnp.concatenate([flat_fg[j].astype(jnp.bfloat16) for j in range(tiles)], axis=1)
        fg = short_dot(fg, order_ref[...], 1, 1).astype(jnp.bfloat16)
        fg_held[g] = fg.reshape(nf, rows, cols)
        copies[0].start()

    for g in range(count // nf):
        for n, (held, out) in enumerate(((fg_held, fg_out), (bg_held, bg_out))):
            pltpu.make_async_copy(held.at[g], out.at[pl.ds(g * nf, nf), chan], sems.at[n, g]).wait()


def variation(scales, at, order, own, above, below, outs, after, shape):
    count, chans, rows, cols = shape
    lines = rows + 2 * NSWEEP
    flat = pltpu.VMEM((cols // LANE, PACK * rows, LANE), jnp.float32)
    field = pltpu.VMEM((lines, PACK, cols), jnp.float32)
    held = pltpu.VMEM((count // PACK, PACK, rows, cols), jnp.bfloat16)
    work = count * rows * cols
    return pl.pallas_call(
        functools.partial(variation_kernel, len(outs) + len(after)),
        in_specs=[smem(), smem()] + [vmem()] * 7 + [anywhere()] * (len(outs) + len(after)),
        out_specs=[anywhere(), anywhere(), vmem()],
        out_shape=[jax.ShapeDtypeStruct(shape, jnp.bfloat16)] * 2
        + [jax.ShapeDtypeStruct((SUB, LANE), jnp.float32)],
        scratch_shapes=[
            field,
            field,
            field,
            flat,
            flat,
            held,
            held,
            pltpu.SemaphoreType.DMA((2, count // PACK)),
        ],
        input_output_aliases={9 + n: n for n in range(len(outs))},
        compiler_params=pltpu.CompilerParams(vmem_limit_bytes=VMEM_BYTES),
        cost_estimate=pl.CostEstimate(
            flops=work * 250, bytes_accessed=work * 12, transcendentals=work * 12
        ),
        name="variation",
    )(scales, at, order, *own, *above, *below, *outs, *after)


def body(frames, prev_fg, depth_valid, sketch, tv_weight):
    count, chans, rows, cols = frames.shape
    groups = lax.axis_size("frame")
    strips = lax.axis_size("pix")
    each = chans // groups
    nval = chans * rows * strips * cols
    tiles = cols // LANE
    me = lax.axis_index("frame")
    targets = [partner(me, k, groups) for k in range(groups)]
    sources = [partner(me, k, groups, back=True) for k in range(groups)]
    ids = jnp.stack(targets + sources).astype(jnp.int32)
    near = [k for k in range(1, groups) if power_of_two(k)]
    far = [k for k in range(1, groups) if not power_of_two(k)]

    first_channels = ids * each
    resid = {}
    for picks in (near, far + [0]):
        parts = residual(first_channels, picks, each, frames, prev_fg, depth_valid)
        resid.update(zip(picks, parts))
    blocks = [resid[0]] + [swap(resid[k], "frame", k) for k in range(1, groups)]
    blocks = [block.reshape(each * rows, count, cols) for block in blocks]

    places = lax.broadcasted_iota(jnp.int32, (cols, cols), 1)
    places = places % LANE * tiles + places // LANE
    order = (places == lax.broadcasted_iota(jnp.int32, (cols, cols), 0)).astype(jnp.bfloat16)
    lined, top, bottom = interleaved(frames, depth_valid, order)
    lined_above = from_behind(bottom, "pix", 1)
    lined_below = from_behind(top, "pix", -1)

    terms, pixels = gram_terms(ids, blocks, nval, (lined_above, lined_below))
    gram = all_sum(all_sum(terms, "frame"), "pix")
    mixing = mixing_matrix(gram, sketch)

    strip = lax.axis_index("pix")
    flags = [(strip > 0).astype(jnp.float32), (strip < strips - 1).astype(jnp.float32)]
    outs, token = [], None

    def strips_of(piece):
        return piece.reshape(each, rows, count, cols)

    def around(top, bottom):
        return from_behind(bottom, "pix", 1), from_behind(top, "pix", -1)

    def work_on(k, piece, from_above, from_below, at, after, outs):
        for c in range(each):
            chan = sources[k] * each + c
            lam = lax.dynamic_index_in_dim(tv_weight, chan, keepdims=False)
            *outs, token = variation(
                jnp.stack([lam] + flags),
                jnp.stack([chan, at + c, c]).astype(jnp.int32),
                order,
                (lined, piece),
                (lined_above, from_above),
                (lined_below, from_below),
                outs,
                after,
                frames.shape,
            )
        return outs, token

    *pieces, top, bottom = spread(ids, [0] + near, mixing, pixels, groups, each, edges=True)
    arrived = {k: swap(pieces[1 + n], "frame", k) for n, k in enumerate(near)}
    own = around(top, bottom)
    outs, token = work_on(0, strips_of(pieces[0]), *own, 0, (), outs)
    for stage in (near, far):
        if not stage:
            continue
        if stage is far:
            pieces = spread(ids, far, mixing, pixels, groups, each, after=tuple(arrived.values()))
            arrived = {k: swap(piece, "frame", k) for k, piece in zip(far, pieces)}
        held = [strips_of(arrived[k]) for k in stage]
        from_above, from_below = around(*rims(held, (token,)))
        for n, k in enumerate(stage):
            outs, done = work_on(k, held[n], from_above, from_below, n * each, (), outs)
            token = done if n == 0 else token
    foreground, background = outs
    return (background, foreground)


def solution(mesh):
    placed = (
        P("frame", None, "pix", None),
        P("frame", None, "pix", None),
        P("frame", "pix", None),
        P(),
        P(),
    )
    return jax.shard_map(
        body,
        mesh=mesh,
        in_specs=placed,
        out_specs=(P("frame", None, "pix", None), P("frame", None, "pix", None)),
        check_vma=False,
    )
```

profile of v0, /device:TPU:0, one launch (start us, length us, event | category | flops | bytes accessed | tf_op | source)
XLA Modules:
  0.0 173.1 jit_solution(7389170970085981736)
XLA Ops:
  0.8 1.6 copy-done
  2.4 1.2 copy-done.6
  3.6 3.3 %interleave.1 = (bf16[5,16,32,512]{3,2,1,0:T(8,128)(2,1)S(1)}, bf16[5,5,32,512]{3,2,1,0:T(8,128)(2,1)}, bf16[5,5,32,512]{3,2,1,0:T(8,128)(2,1)}) custom-call(bf16[32,4,16,512]{3,2,1,0:T(8,128)(2,1)S(1)} %copy-done, s32[32,16,512]{2,1,0:T(8,128)S(1)} %copy-done.6, bf16[512,512]{1,0:T(8,128)(2,1)S(1)} %fusion.order_ref), custom_call_target="tpu_custom_call" | custom-call | tf_op jit(solution)/shard_map/interleave/pallas_call | solution.py:233
  6.9 2.4 %collective-permute-start.3 = (bf16[5,5,32,512]{3,2,1,0:T(8,128)(2,1)}, bf16[5,5,32,512]{3,2,1,0:T(8,128)(2,1)S(1)}, u32[]{:S(2)}, u32[]{:S(2)}) collective-permute-start(bf16[5,5,32,512]{3,2,1,0:T(8,128)(2,1)} %get-tuple-element.35), channel_id=1, source_target_pairs={{0,1},{1,2},{2,3},{3,4},{4,5},{5,6},{6,7},{8,9},{9,10},{10,11},{11... | collective-permute-start | bytes 2457608 | tf_op jit(solution)/shard_map/ppermute | solution.py:22
  9.3 1.3 collective-permute-start.4
  10.7 1.6 copy-done.1
  12.3 1.2 copy-done.7
  13.5 1.6 copy-done.8
  15.1 1.7 residual.3
  16.8 2.4 %collective-permute-start = (bf16[1,16,32,512]{3,2,1,0:T(8,128)(2,1)S(1)}, bf16[1,16,32,512]{3,2,1,0:T(8,128)(2,1)S(1)}, u32[]{:S(2)}, u32[]{:S(2)}) collective-permute-start(bf16[1,16,32,512]{3,2,1,0:T(8,128)(2,1)S(1)} %get-tuple-element.32), channel_id=1, source_target_pairs={{0,8},{8,0},{16,24},{24,16},{1,9},{9,1},{17,25},{25,17},{2,10},{10... | collective-permute-start | bytes 1572872 | tf_op jit(solution)/shard_map/ppermute | solution.py:38
  19.2 1.5 collective-permute-start.1
  20.7 1.7 residual.2
  22.5 7.5 %collective-permute-done = bf16[1,16,32,512]{3,2,1,0:T(8,128)(2,1)S(1)} collective-permute-done((bf16[1,16,32,512]{3,2,1,0:T(8,128)(2,1)S(1)}, bf16[1,16,32,512]{3,2,1,0:T(8,128)(2,1)S(1)}, u32[]{:S(2)}, u32[]{:S(2)}) %collective-permute-start) | collective-permute-done | bytes 524320 | tf_op jit(solution)/shard_map/ppermute | solution.py:38
  30.0 12.9 %collective-permute-done.1 = bf16[1,16,32,512]{3,2,1,0:T(8,128)(2,1)S(1)} collective-permute-done((bf16[1,16,32,512]{3,2,1,0:T(8,128)(2,1)S(1)}, bf16[1,16,32,512]{3,2,1,0:T(8,128)(2,1)S(1)}, u32[]{:S(2)}, u32[]{:S(2)}) %collective-permute-start.1) | collective-permute-done | bytes 524320 | tf_op jit(solution)/shard_map/ppermute | solution.py:38
  43.3 1.4 gram.1
  44.7 1.3 copy-done.9
  46.0 1.4 collective-permute-start.7
  47.4 1.4 collective-permute-start.6
  49.7 1.4 collective-permute-done.7
  51.1 1.9 %collective-permute-done.6 = f32[128,128]{1,0:T(8,128)S(1)} collective-permute-done((f32[128,128]{1,0:T(8,128)S(1)}, f32[128,128]{1,0:T(8,128)S(1)}, u32[]{:S(2)}, u32[]{:S(2)}) %collective-permute-start.6) | collective-permute-done | bytes 65568 | tf_op jit(solution)/shard_map/ppermute | solution.py:38
  54.3 1.1 collective-permute-done.8
  55.4 5.5 %collective-permute-start.11 = (f32[128,128]{1,0:T(8,128)S(1)}, f32[128,128]{1,0:T(8,128)S(1)}, u32[]{:S(2)}, u32[]{:S(2)}) collective-permute-start(f32[128,128]{1,0:T(8,128)S(1)} %add.74), channel_id=1, source_target_pairs={{0,6},{1,7},{2,4},{3,5},{4,2},{5,3},{6,0},{7,1},{8,14},{9,15},{10,... | collective-permute-start | bytes 196616 | tf_op jit(solution)/shard_map/ppermute | solution.py:38
  61.5 1.9 %collective-permute-done.11 = f32[128,128]{1,0:T(8,128)S(1)} collective-permute-done((f32[128,128]{1,0:T(8,128)S(1)}, f32[128,128]{1,0:T(8,128)S(1)}, u32[]{:S(2)}, u32[]{:S(2)}) %collective-permute-start.11) | collective-permute-done | bytes 65568 | tf_op jit(solution)/shard_map/ppermute | solution.py:38
  63.4 3.5 %collective-permute-done.10 = f32[128,128]{1,0:T(8,128)S(1)} collective-permute-done((f32[128,128]{1,0:T(8,128)S(1)}, f32[128,128]{1,0:T(8,128)S(1)}, u32[]{:S(2)}, u32[]{:S(2)}) %collective-permute-start.10) | collective-permute-done | bytes 65568 | tf_op jit(solution)/shard_map/ppermute | solution.py:38
  67.6 10.6 %mixing.1.mixing_ref = bf16[128,128]{1,0:T(8,128)(2,1)} custom-call(f32[128,128]{1,0:T(8,128)} %add_add_fusion.gram_ref, f32[64,128]{1,0:T(8,128)} %bitcast.24), custom_call_target="tpu_custom_call" | custom-call | tf_op jit(solution)/shard_map/mixing/pallas_call | solution.py:132
  78.2 1.6 copy-done.10
  80.6 1.8 %spread.2 = (bf16[16,32,512]{2,1,0:T(8,128)(2,1)S(1)}, bf16[16,32,512]{2,1,0:T(8,128)(2,1)S(1)}, bf16[16,32,512]{2,1,0:T(8,128)(2,1)S(1)}, bf16[1,5,32,512]{3,2,1,0:T(8,128)(2,1)}, bf16[1,5,32,512]{3,2,1,0:T(8,128)(2,1)}) custom-call(s32[8]{0:T(128)S(1)} %stack.79.channel_ref.ids_ref, bf16[128,128]{1,0:T(8,128)(2,1)S(1)} %copy-done.19, ...), custom_call_target="tpu_custom_call" | custom-call | tf_op jit(solution)/shard_map/spread/pallas_call | solution.py:301
  83.1 1.5 collective-permute-start.13
  84.7 11.1 %collective-permute-done.12.refs_0_ = bf16[16,32,512]{2,1,0:T(8,128)(2,1)S(1)} collective-permute-done((bf16[16,32,512]{2,1,0:T(8,128)(2,1)S(1)}, bf16[16,32,512]{2,1,0:T(8,128)(2,1)S(1)}, u32[]{:S(2)}, u32[]{:S(2)}) %collective-permute-start.12) | collective-permute-done | bytes 524320 | tf_op jit(solution)/shard_map/ppermute | solution.py:38
  96.2 1.8 %spread.3 = bf16[16,32,512]{2,1,0:T(8,128)(2,1)} custom-call(s32[8]{0:T(128)S(1)} %stack.79.channel_ref.ids_ref, bf16[128,128]{1,0:T(8,128)(2,1)S(1)} %copy-done.19, bf16[16,128,512]{2,1,0:T(8,128)(2,1)S(1)} %copy-done.10, bf16[16,32,512]{2,1,0:T(8,128)(2,1)S(1)} %collective-permute-done.12.refs_0_, bf16[16,32,512]{2,1,0:T(8,128)(2,1)S(1)} %collective-permute-done.13.refs_1_), custom_call_target="tpu_custom_call" | custom-call | tf_op jit(solution)/shard_map/spread/pallas_call | solution.py:301
  98.0 1.5 collective-permute-start.14
  99.5 2.1 %collective-permute-start.15 = (bf16[1,5,32,512]{3,2,1,0:T(8,128)(2,1)}, bf16[1,5,32,512]{3,2,1,0:T(8,128)(2,1)}, u32[]{:S(2)}, u32[]{:S(2)}) collective-permute-start(bf16[1,5,32,512]{3,2,1,0:T(8,128)(2,1)} %get-tuple-element.42), channel_id=1, source_target_pairs={{0,1},{1,2},{2,3},{3,4},{4,5},{5,6},{6,7},{8,9},{9,10},{10,11},{11... | collective-permute-start | bytes 491528 | tf_op jit(solution)/shard_map/ppermute | solution.py:22
  101.6 1.3 collective-permute-start.16
  105.3 1.0 copy-done.3
  106.3 1.0 copy-done.23
  107.4 8.6 %variation.4 = (bf16[32,4,16,512]{3,2,1,0:T(8,128)(2,1)}, bf16[32,4,16,512]{3,2,1,0:T(8,128)(2,1)}, f32[8,128]{1,0:T(8,128)S(1)}) custom-call(f32[3]{0:T(128)S(1)} %maximum_maximum_fusion.2.scale_ref, s32[3]{0:T(128)S(1)} %stack.83.at_ref, bf16[512,512]{1,0:T(8,128)(2,1)S(1)} %copy-done.3, bf16[5,16,32,512]{3,2,1,0:T(8,128)(2,1)S(1)} %get-tuple-element.30.refs_0_, ...), custom_call_target="tpu_custom_call" | custom-call | flops 65536000 | bytes 3145728 | tf_op jit(solution)/shard_map/variation/pallas_call | solution.py:448
  116.5 2.1 %rims.2 = (bf16[2,5,32,512]{3,2,1,0:T(8,128)(2,1)}, bf16[2,5,32,512]{3,2,1,0:T(8,128)(2,1)}) custom-call(bf16[1,16,32,512]{3,2,1,0:T(8,128)(2,1)} %bitcast.17, bf16[1,16,32,512]{3,2,1,0:T(8,128)(2,1)} %bitcast.15, f32[8,128]{1,0:T(8,128)} %copy-done.21), custom_call_target="tpu_custom_call" | custom-call | tf_op jit(solution)/shard_map/rims/pallas_call | solution.py:326
  118.6 6.0 %collective-permute-start.17 = (bf16[2,5,32,512]{3,2,1,0:T(8,128)(2,1)}, bf16[2,5,32,512]{3,2,1,0:T(8,128)(2,1)S(1)}, u32[]{:S(2)}, u32[]{:S(2)}) collective-permute-start(bf16[2,5,32,512]{3,2,1,0:T(8,128)(2,1)} %get-tuple-element.45), channel_id=1, source_target_pairs={{0,1},{1,2},{2,3},{3,4},{4,5},{5,6},{6,7},{8,9},{9,10},{10,11},{11... | collective-permute-start | bytes 983048 | tf_op jit(solution)/shard_map/ppermute | solution.py:22
  124.6 1.3 collective-permute-start.18
  128.4 1.2 copy-done.4
  129.5 1.0 copy-done.14
  130.6 8.4 %variation.5 = (bf16[32,4,16,512]{3,2,1,0:T(8,128)(2,1)}, bf16[32,4,16,512]{3,2,1,0:T(8,128)(2,1)}, f32[8,128]{1,0:T(8,128)S(1)}) custom-call(f32[3]{0:T(128)S(1)} %maximum_maximum_fusion.1.scale_ref, s32[3]{0:T(128)S(1)} %stack.81.at_ref, bf16[512,512]{1,0:T(8,128)(2,1)S(1)} %copy-done.4, ...), custom_call_target="tpu_custom_call", output_to_operand_aliasing={{0}: (9, {}), {1}: (10, {})} | custom-call | flops 65536000 | bytes 3145728 | tf_op jit(solution)/shard_map/variation/pallas_call | solution.py:448
  139.6 1.8 %rims.3 = (bf16[1,5,32,512]{3,2,1,0:T(8,128)(2,1)}, bf16[1,5,32,512]{3,2,1,0:T(8,128)(2,1)}) custom-call(bf16[1,16,32,512]{3,2,1,0:T(8,128)(2,1)} %bitcast.11.refs_0_.refs_1_, f32[8,128]{1,0:T(8,128)} %copy-done.20), custom_call_target="tpu_custom_call" | custom-call | tf_op jit(solution)/shard_map/rims/pallas_call | solution.py:326
  141.4 6.8 %collective-permute-start.19 = (bf16[1,5,32,512]{3,2,1,0:T(8,128)(2,1)}, bf16[1,5,32,512]{3,2,1,0:T(8,128)(2,1)S(1)}, u32[]{:S(2)}, u32[]{:S(2)}) collective-permute-start(bf16[1,5,32,512]{3,2,1,0:T(8,128)(2,1)} %get-tuple-element.50), channel_id=1, source_target_pairs={{0,1},{1,2},{2,3},{3,4},{4,5},{5,6},{6,7},{8,9},{9,10},{10,11},{11... | collective-permute-start | bytes 491528 | tf_op jit(solution)/shard_map/ppermute | solution.py:22
  148.2 1.5 collective-permute-start.20
  150.5 1.0 copy-done.5
  154.5 9.0 %variation.6 = (bf16[32,4,16,512]{3,2,1,0:T(8,128)(2,1)}, bf16[32,4,16,512]{3,2,1,0:T(8,128)(2,1)}, f32[8,128]{1,0:T(8,128)}) custom-call(f32[3]{0:T(128)S(1)} %maximum_maximum_fusion.3.scale_ref, s32[3]{0:T(128)S(1)} %pad_add_fusion.at_ref, bf16[512,512]{1,0:T(8,128)(2,1)S(1)} %copy-done.5, ...), custom_call_target="tpu_custom_call", output_to_operand_aliasing={{0}: (9, {}), {1}: (10, {})} | custom-call | flops 65536000 | bytes 3145728 | tf_op jit(solution)/shard_map/variation/pallas_call | solution.py:448
  163.6 9.3 %variation.7 = (bf16[32,4,16,512]{3,2,1,0:T(8,128)(2,1)}, bf16[32,4,16,512]{3,2,1,0:T(8,128)(2,1)}, f32[8,128]{1,0:T(8,128)}) custom-call(f32[3]{0:T(128)S(1)} %maximum_maximum_fusion.scale_ref, s32[3]{0:T(128)S(1)} %stack.75.at_ref, bf16[512,512]{1,0:T(8,128)(2,1)S(1)} %copy-done.5, ...), custom_call_target="tpu_custom_call", output_to_operand_aliasing={{0}: (9, {}), {1}: (10, {})} | custom-call | flops 65536000 | bytes 3145728 | tf_op jit(solution)/shard_map/variation/pallas_call | solution.py:448
  (74 shorter events, 15.8 us)
Async XLA Ops:
  0.8 1.6 copy-start
  2.4 1.2 copy-start.6
  3.6 3.3 %copy-start.2 = (bf16[512,512]{1,0:T(8,128)(2,1)}, bf16[512,512]{1,0:T(8,128)(2,1)S(1)}, u32[]{:S(2)}) copy-start(bf16[512,512]{1,0:T(8,128)(2,1)S(1)} %fusion.order_ref) | copy-start | bytes 1572868
  6.9 36.4 %collective-permute-start.3 = (bf16[5,5,32,512]{3,2,1,0:T(8,128)(2,1)}, bf16[5,5,32,512]{3,2,1,0:T(8,128)(2,1)S(1)}, u32[]{:S(2)}, u32[]{:S(2)}) collective-permute-start(bf16[5,5,32,512]{3,2,1,0:T(8,128)(2,1)} %get-tuple-element.35), channel_id=1, source_target_pairs={{0,1},{1,2},{2,3},{3,4},{4,5},{5,6},{6,7},{8,9},{9,10},{10,11},{11... | collective-permute-start | bytes 2457608 | tf_op jit(solution)/shard_map/ppermute | solution.py:22
  9.3 34.0 %collective-permute-start.4 = (bf16[5,5,32,512]{3,2,1,0:T(8,128)(2,1)}, bf16[5,5,32,512]{3,2,1,0:T(8,128)(2,1)}, u32[]{:S(2)}, u32[]{:S(2)}) collective-permute-start(bf16[5,5,32,512]{3,2,1,0:T(8,128)(2,1)} %get-tuple-element.36), channel_id=1, source_target_pairs={{1,0},{2,1},{3,2},{4,3},{5,4},{6,5},{7,6},{9,8},{10,9},{11,10},{12... | collective-permute-start | bytes 2457608 | tf_op jit(solution)/shard_map/ppermute | solution.py:22
  10.7 1.6 copy-start.1
  12.3 1.2 copy-start.7
  13.5 1.6 copy-start.8
  16.8 13.2 %collective-permute-start = (bf16[1,16,32,512]{3,2,1,0:T(8,128)(2,1)S(1)}, bf16[1,16,32,512]{3,2,1,0:T(8,128)(2,1)S(1)}, u32[]{:S(2)}, u32[]{:S(2)}) collective-permute-start(bf16[1,16,32,512]{3,2,1,0:T(8,128)(2,1)S(1)} %get-tuple-element.32), channel_id=1, source_target_pairs={{0,8},{8,0},{16,24},{24,16},{1,9},{9,1},{17,25},{25,17},{2,10},{10... | collective-permute-start | bytes 1572872 | tf_op jit(solution)/shard_map/ppermute | solution.py:38
  19.2 23.7 %collective-permute-start.1 = (bf16[1,16,32,512]{3,2,1,0:T(8,128)(2,1)S(1)}, bf16[1,16,32,512]{3,2,1,0:T(8,128)(2,1)S(1)}, u32[]{:S(2)}, u32[]{:S(2)}) collective-permute-start(bf16[1,16,32,512]{3,2,1,0:T(8,128)(2,1)S(1)} %get-tuple-element.33), channel_id=1, source_target_pairs={{0,16},{8,24},{16,0},{24,8},{1,17},{9,25},{17,1},{25,9},{2,18},{10... | collective-permute-start | bytes 1572872 | tf_op jit(solution)/shard_map/ppermute | solution.py:38
  22.4 20.8 %collective-permute-start.2 = (bf16[1,16,32,512]{3,2,1,0:T(8,128)(2,1)S(1)}, bf16[1,16,32,512]{3,2,1,0:T(8,128)(2,1)S(1)}, u32[]{:S(2)}, u32[]{:S(2)}) collective-permute-start(bf16[1,16,32,512]{3,2,1,0:T(8,128)(2,1)S(1)} %get-tuple-element.34), channel_id=1, source_target_pairs={{0,24},{8,16},{16,8},{24,0},{1,25},{9,17},{17,9},{25,1},{2,26},{10... | collective-permute-start | bytes 1572872 | tf_op jit(solution)/shard_map/ppermute | solution.py:38
  44.7 1.3 copy-start.9
  46.0 5.2 %collective-permute-start.7 = (f32[128,128]{1,0:T(8,128)S(1)}, f32[128,128]{1,0:T(8,128)S(1)}, u32[]{:S(2)}, u32[]{:S(2)}) collective-permute-start(f32[128,128]{1,0:T(8,128)S(1)} %get-tuple-element.37), channel_id=1, source_target_pairs={{0,24},{8,16},{16,8},{24,0},{1,25},{9,17},{17,9},{25,1},{2,26},{10... | collective-permute-start | bytes 196616 | tf_op jit(solution)/shard_map/ppermute | solution.py:38
  47.4 5.6 %collective-permute-start.6 = (f32[128,128]{1,0:T(8,128)S(1)}, f32[128,128]{1,0:T(8,128)S(1)}, u32[]{:S(2)}, u32[]{:S(2)}) collective-permute-start(f32[128,128]{1,0:T(8,128)S(1)} %get-tuple-element.37), channel_id=1, source_target_pairs={{0,16},{8,24},{16,0},{24,8},{1,17},{9,25},{17,1},{25,9},{2,18},{10... | collective-permute-start | bytes 196616 | tf_op jit(solution)/shard_map/ppermute | solution.py:38
  48.8 5.2 %collective-permute-start.5 = (f32[128,128]{1,0:T(8,128)S(1)}, f32[128,128]{1,0:T(8,128)S(1)}, u32[]{:S(2)}, u32[]{:S(2)}) collective-permute-start(f32[128,128]{1,0:T(8,128)S(1)} %get-tuple-element.37), channel_id=1, source_target_pairs={{0,8},{8,0},{16,24},{24,16},{1,9},{9,1},{17,25},{25,17},{2,10},{10... | collective-permute-start | bytes 196616 | tf_op jit(solution)/shard_map/ppermute | solution.py:38
  54.1 1.3 collective-permute-start.8
  55.4 8.0 %collective-permute-start.11 = (f32[128,128]{1,0:T(8,128)S(1)}, f32[128,128]{1,0:T(8,128)S(1)}, u32[]{:S(2)}, u32[]{:S(2)}) collective-permute-start(f32[128,128]{1,0:T(8,128)S(1)} %add.74), channel_id=1, source_target_pairs={{0,6},{1,7},{2,4},{3,5},{4,2},{5,3},{6,0},{7,1},{8,14},{9,15},{10,... | collective-permute-start | bytes 196616 | tf_op jit(solution)/shard_map/ppermute | solution.py:38
  60.9 6.0 %collective-permute-start.10 = (f32[128,128]{1,0:T(8,128)S(1)}, f32[128,128]{1,0:T(8,128)S(1)}, u32[]{:S(2)}, u32[]{:S(2)}) collective-permute-start(f32[128,128]{1,0:T(8,128)S(1)} %add.74), channel_id=1, source_target_pairs={{0,4},{1,5},{2,6},{3,7},{4,0},{5,1},{6,2},{7,3},{8,12},{9,13},{10,... | collective-permute-start | bytes 196616 | tf_op jit(solution)/shard_map/ppermute | solution.py:38
  60.9 6.0 %collective-permute-start.9 = (f32[128,128]{1,0:T(8,128)S(1)}, f32[128,128]{1,0:T(8,128)S(1)}, u32[]{:S(2)}, u32[]{:S(2)}) collective-permute-start(f32[128,128]{1,0:T(8,128)S(1)} %add.74), channel_id=1, source_target_pairs={{0,2},{1,3},{2,0},{3,1},{4,6},{5,7},{6,4},{7,5},{8,10},{9,11},{10,... | collective-permute-start | bytes 196616 | tf_op jit(solution)/shard_map/ppermute | solution.py:38
  78.2 1.6 copy-start.10
  79.8 0.8 copy-start.19
  82.3 17.1 %copy-start.22 = (bf16[16,32,512]{2,1,0:T(8,128)(2,1)}, bf16[16,32,512]{2,1,0:T(8,128)(2,1)S(1)}, u32[]{:S(2)}) copy-start(bf16[16,32,512]{2,1,0:T(8,128)(2,1)S(1)} %get-tuple-element.41) | copy-start | bytes 1572868
  82.3 20.6 %copy-start.24 = (f32[4]{0:T(128)S(1)}, f32[4]{0:T(128)}, u32[]{:S(2)}) copy-start(f32[4]{0:T(128)} %param.9) | copy-start | bytes 52
  82.3 13.4 %collective-permute-start.12 = (bf16[16,32,512]{2,1,0:T(8,128)(2,1)S(1)}, bf16[16,32,512]{2,1,0:T(8,128)(2,1)S(1)}, u32[]{:S(2)}, u32[]{:S(2)}) collective-permute-start(bf16[16,32,512]{2,1,0:T(8,128)(2,1)S(1)} %get-tuple-element.39), channel_id=1, source_target_pairs={{0,8},{8,0},{16,24},{24,16},{1,9},{9,1},{17,25},{25,17},{2,10},{10... | collective-permute-start | bytes 1572872 | tf_op jit(solution)/shard_map/ppermute | solution.py:38
  83.1 13.1 %collective-permute-start.13 = (bf16[16,32,512]{2,1,0:T(8,128)(2,1)S(1)}, bf16[16,32,512]{2,1,0:T(8,128)(2,1)S(1)}, u32[]{:S(2)}, u32[]{:S(2)}) collective-permute-start(bf16[16,32,512]{2,1,0:T(8,128)(2,1)S(1)} %get-tuple-element.40), channel_id=1, source_target_pairs={{0,16},{8,24},{16,0},{24,8},{1,17},{9,25},{17,1},{25,9},{2,18},{10... | collective-permute-start | bytes 1572872 | tf_op jit(solution)/shard_map/ppermute | solution.py:38
  95.7 3.8 %copy-start.13 = (bf16[16,32,512]{2,1,0:T(8,128)(2,1)}, bf16[16,32,512]{2,1,0:T(8,128)(2,1)S(1)}, u32[]{:S(2)}) copy-start(bf16[16,32,512]{2,1,0:T(8,128)(2,1)S(1)} %collective-permute-done.12.refs_0_) | copy-start | bytes 1572868
  96.2 1.8 %copy-start.11 = (bf16[16,32,512]{2,1,0:T(8,128)(2,1)}, bf16[16,32,512]{2,1,0:T(8,128)(2,1)S(1)}, u32[]{:S(2)}) copy-start(bf16[16,32,512]{2,1,0:T(8,128)(2,1)S(1)} %collective-permute-done.13.refs_1_) | copy-start | bytes 1572868
  98.0 41.6 %collective-permute-start.14 = (bf16[16,32,512]{2,1,0:T(8,128)(2,1)}, bf16[16,32,512]{2,1,0:T(8,128)(2,1)}, u32[]{:S(2)}, u32[]{:S(2)}) collective-permute-start(bf16[16,32,512]{2,1,0:T(8,128)(2,1)} %spread.3), channel_id=1, source_target_pairs={{0,24},{8,16},{16,8},{24,0},{1,25},{9,17},{17,9},{25,1},{2,26},{10... | collective-permute-start | bytes 1572872 | tf_op jit(solution)/shard_map/ppermute | solution.py:38
  99.5 4.9 %collective-permute-start.15 = (bf16[1,5,32,512]{3,2,1,0:T(8,128)(2,1)}, bf16[1,5,32,512]{3,2,1,0:T(8,128)(2,1)}, u32[]{:S(2)}, u32[]{:S(2)}) collective-permute-start(bf16[1,5,32,512]{3,2,1,0:T(8,128)(2,1)} %get-tuple-element.42), channel_id=1, source_target_pairs={{0,1},{1,2},{2,3},{3,4},{4,5},{5,6},{6,7},{8,9},{9,10},{10,11},{11... | collective-permute-start | bytes 491528 | tf_op jit(solution)/shard_map/ppermute | solution.py:22
  101.6 3.6 %collective-permute-start.16 = (bf16[1,5,32,512]{3,2,1,0:T(8,128)(2,1)}, bf16[1,5,32,512]{3,2,1,0:T(8,128)(2,1)}, u32[]{:S(2)}, u32[]{:S(2)}) collective-permute-start(bf16[1,5,32,512]{3,2,1,0:T(8,128)(2,1)} %get-tuple-element.43), channel_id=1, source_target_pairs={{1,0},{2,1},{3,2},{4,3},{5,4},{6,5},{7,6},{9,8},{10,9},{11,10},{12... | collective-permute-start | bytes 491528 | tf_op jit(solution)/shard_map/ppermute | solution.py:22
  105.3 1.0 copy-start.3
  106.3 1.0 copy-start.23
  115.9 0.6 copy-start.21
  118.6 8.8 %collective-permute-start.17 = (bf16[2,5,32,512]{3,2,1,0:T(8,128)(2,1)}, bf16[2,5,32,512]{3,2,1,0:T(8,128)(2,1)S(1)}, u32[]{:S(2)}, u32[]{:S(2)}) collective-permute-start(bf16[2,5,32,512]{3,2,1,0:T(8,128)(2,1)} %get-tuple-element.45), channel_id=1, source_target_pairs={{0,1},{1,2},{2,3},{3,4},{4,5},{5,6},{6,7},{8,9},{9,10},{10,11},{11... | collective-permute-start | bytes 983048 | tf_op jit(solution)/shard_map/ppermute | solution.py:22
  124.6 3.7 %collective-permute-start.18 = (bf16[2,5,32,512]{3,2,1,0:T(8,128)(2,1)}, bf16[2,5,32,512]{3,2,1,0:T(8,128)(2,1)S(1)}, u32[]{:S(2)}, u32[]{:S(2)}) collective-permute-start(bf16[2,5,32,512]{3,2,1,0:T(8,128)(2,1)} %get-tuple-element.46), channel_id=1, source_target_pairs={{1,0},{2,1},{3,2},{4,3},{5,4},{6,5},{7,6},{9,8},{10,9},{11,10},{12... | collective-permute-start | bytes 983048 | tf_op jit(solution)/shard_map/ppermute | solution.py:22
  127.4 11.7 %copy-start.15 = (bf16[2,5,32,512]{3,2,1,0:T(8,128)(2,1)}, bf16[2,5,32,512]{3,2,1,0:T(8,128)(2,1)S(1)}, u32[]{:S(2)}) copy-start(bf16[2,5,32,512]{3,2,1,0:T(8,128)(2,1)S(1)} %collective-permute-done.17.refs_3_) | copy-start | bytes 983044
  128.4 10.7 %copy-start.17 = (bf16[2,5,32,512]{3,2,1,0:T(8,128)(2,1)}, bf16[2,5,32,512]{3,2,1,0:T(8,128)(2,1)S(1)}, u32[]{:S(2)}) copy-start(bf16[2,5,32,512]{3,2,1,0:T(8,128)(2,1)S(1)} %collective-permute-done.18.refs_5_) | copy-start | bytes 983044
  128.4 1.2 copy-start.4
  129.5 1.0 copy-start.14
  139.0 0.6 copy-start.20
  141.4 22.2 %collective-permute-start.19 = (bf16[1,5,32,512]{3,2,1,0:T(8,128)(2,1)}, bf16[1,5,32,512]{3,2,1,0:T(8,128)(2,1)S(1)}, u32[]{:S(2)}, u32[]{:S(2)}) collective-permute-start(bf16[1,5,32,512]{3,2,1,0:T(8,128)(2,1)} %get-tuple-element.50), channel_id=1, source_target_pairs={{0,1},{1,2},{2,3},{3,4},{4,5},{5,6},{6,7},{8,9},{9,10},{10,11},{11... | collective-permute-start | bytes 491528 | tf_op jit(solution)/shard_map/ppermute | solution.py:22
  148.2 15.4 %collective-permute-start.20 = (bf16[1,5,32,512]{3,2,1,0:T(8,128)(2,1)}, bf16[1,5,32,512]{3,2,1,0:T(8,128)(2,1)S(1)}, u32[]{:S(2)}, u32[]{:S(2)}) collective-permute-start(bf16[1,5,32,512]{3,2,1,0:T(8,128)(2,1)} %get-tuple-element.51), channel_id=1, source_target_pairs={{1,0},{2,1},{3,2},{4,3},{5,4},{6,5},{7,6},{9,8},{10,9},{11,10},{12... | collective-permute-start | bytes 491528 | tf_op jit(solution)/shard_map/ppermute | solution.py:22
  150.5 1.0 copy-start.5
  151.5 1.0 copy-start.12
  152.6 1.0 copy-start.16
  153.6 1.0 copy-start.18
where the time goes:
time: 175 us; the launch traced here: 173 us
  Pallas kernels  61.5 us (35%)
  waiting for transfers between devices  45 us (26%)
  starting transfers between devices  40.5 us (23%)
  local copies, waits for them, and re-layouts  21.2 us (12%)
  other arithmetic  3.78 us (2%)
    ppermute x13, waiting for transfers between devices, swap(): return lax.ppermute(value, axis, pairs)  43.2 us
    pallas_call x4, Pallas kernels, variation(): pl.pallas_call(functools.partial(variation_kernel, len(outs) + len(after)...  35.4 us
    ppermute x8, starting transfers between devices, from_behind(): lax.ppermute(value, axis, [(source, source + steps) for source in range(l...  22.7 us
    unnamed x50, local copies, waits for them, and re-layouts  20.4 us
    ppermute x13, starting transfers between devices, swap(): return lax.ppermute(value, axis, pairs)  17.9 us
    pallas_call x1, Pallas kernels, mixing_matrix(): pl.pallas_call(mixing_kernel, out_shape=jax.ShapeDtypeStruct(gram.shape,...  10.6 us
    pallas_call x2, Pallas kernels, rims(): pl.pallas_call(functools.partial(rims_kernel, len(pieces)), in_specs=[vme...  3.86 us
    pallas_call x2, Pallas kernels, spread(): pl.pallas_call(functools.partial(spread_kernel, picks, edges, len(after))...  3.52 us
  transfers between devices with their start and end apart: 21, of which 13 were waited for; matrix products, arithmetic and copies ran while one was open for 2% of the time, Pallas kernels for 18%

commit v1 on v0

v1 whole, which is shorter than its diff:
```python
import functools
import math

import jax
import jax.numpy as jnp
from jax import lax
from jax.experimental import pallas as pl
from jax.experimental.pallas import tpu as pltpu
from jax.sharding import PartitionSpec as P

POWER = 3
NSWEEP = 5
STEP_SIZE = 0.125
SUB = 8
LANE = 128
PACK = 16
SPARE_BYTES = 12 * 1024 * 1024


def from_behind(value, axis, steps):
    count = lax.axis_size(axis)
    leading, last = (max(0, -steps), min(count, count - steps))
    return lax.ppermute(value, axis, [(source, source + steps) for source in range(leading, last)])


def power_of_two(count):
    return count & (count - 1) == 0


def partner(index, offset, count, back=False):
    if power_of_two(count):
        return index ^ offset
    return (index + (count - offset if back else offset)) % count


def swap(value, axis, offset):
    count = lax.axis_size(axis)
    pairs = [(source, partner(source, offset, count)) for source in range(count)]
    return lax.ppermute(value, axis, pairs)


def all_sum(value, axis):
    count = lax.axis_size(axis)
    if not power_of_two(count):
        return lax.psum(value, axis)
    bit = 1
    while bit < count:
        fours = (count // bit).bit_length() % 2 == 1
        offsets = (bit, 2 * bit, 3 * bit) if fours else (bit,)
        others = [swap(value, axis, offset) for offset in offsets]
        for other in others:
            value = value + other
        bit *= len(offsets) + 1
    return value


def exact_dot(left, right, left_dim, right_dim):
    return lax.dot_general(
        left,
        right,
        (((left_dim,), (right_dim,)), ((), ())),
        precision=lax.Precision.HIGHEST,
        preferred_element_type=jnp.float32,
    )


def short_dot(left, right, left_dim, right_dim):
    return lax.dot_general(
        left,
        right,
        (((left_dim,), (right_dim,)), ((), ())),
        preferred_element_type=jnp.float32,
    )


def eliminate(square, sides):
    rank = square.shape[0]
    width = sides[0].shape[1]
    blocks = rank // SUB
    sub_ids = lax.broadcasted_iota(jnp.int32, (SUB, width), 0)
    square = jnp.concatenate([square, jnp.zeros((rank, width - rank), jnp.float32)], axis=1)

    def in_blocks(rows):
        return [rows[SUB * b : SUB * (b + 1)] for b in range(blocks)]

    def row_of(rows, j):
        return jnp.broadcast_to(rows[j : j + 1], (SUB, width))

    def col_of(rows, j):
        return jnp.broadcast_to(rows[:, j : j + 1], (SUB, width))

    square = in_blocks(square)
    sides = [in_blocks(side) for side in sides]
    solved = [[] for _ in sides]
    for k in range(blocks):
        below = range(k, blocks)
        cols = {b: [col_of(square[b], SUB * k + j) for j in range(SUB)] for b in below}
        pivots = jnp.ones((SUB, width), jnp.float32)
        for j in range(SUB):
            pivot = row_of(cols[k][j], j)
            inverse = 1.0 / pivot
            pivots = jnp.where(sub_ids == j, pivot, pivots)
            col_rows = {i: row_of(cols[k][i], j) for i in range(j + 1, SUB)}
            square_row = row_of(square[k], j)
            side_rows = [row_of(side[k], j) for side in sides]
            for b in below:
                ratio = cols[b][j] * inverse
                if b == k:
                    ratio = jnp.where(sub_ids > j, ratio, 0.0)
                for i in range(j + 1, SUB):
                    cols[b][i] = cols[b][i] - ratio * col_rows[i]
                square[b] = square[b] - ratio * square_row
                for side, side_row in zip(sides, side_rows):
                    side[b] = side[b] - ratio * side_row
        scale = lax.rsqrt(pivots)
        for rows, side in zip(solved, sides):
            rows.append(side[k] * scale)
    return [jnp.concatenate(rows, axis=0) for rows in solved]


def mixing_kernel(gram_ref, sketch_ref, mixing_ref):
    gram = gram_ref[...]
    basis = sketch_ref[...]
    for turn in range(POWER):
        image = exact_dot(basis, gram, 1, 1)
        (basis,) = eliminate(exact_dot(basis, image, 1, 1), [image])
    image = exact_dot(basis, gram, 1, 1)
    left, right = eliminate(exact_dot(basis, image, 1, 1), [basis, image])
    mixing_ref[...] = exact_dot(right, left, 0, 0).astype(mixing_ref.dtype)


def mixing_matrix(gram, sketch):
    return pl.pallas_call(
        mixing_kernel,
        out_shape=jax.ShapeDtypeStruct(gram.shape, jnp.bfloat16),
        cost_estimate=cost(10.6),
        name="mixing",
    )(gram, sketch.T)


def tile(j):
    return pl.ds(LANE * j, LANE)


def vmem():
    return pl.BlockSpec(memory_space=pltpu.VMEM)


def smem():
    return pl.BlockSpec(memory_space=pltpu.SMEM)


def anywhere():
    return pl.BlockSpec(memory_space=pl.ANY)


def room(*scratch):
    held = sum(math.prod(ref.shape) * jnp.dtype(ref.dtype).itemsize for ref in scratch)
    return pltpu.CompilerParams(vmem_limit_bytes=SPARE_BYTES + held)


def cost(micros):
    return pl.CostEstimate(flops=0, bytes_accessed=int(micros * 3.6e6), transcendentals=0)


def residual_kernel(last, channel_ref, frames_ref, prev_ref, valid_ref, *outs):
    pick, c = pl.program_id(0), pl.program_id(1)
    cols = frames_ref.shape[-1]
    keep = jnp.where(channel_ref[pick] + c == last, 0.0, 1.0)
    for j in range(cols // LANE):
        valid = jnp.where(valid_ref[:, :, tile(j)] != 0, 1.0, keep)
        diff = frames_ref[:, 0, :, tile(j)].astype(jnp.float32)
        diff = diff - prev_ref[:, 0, :, tile(j)].astype(jnp.float32)
        turned = jnp.swapaxes(diff * valid, 0, 1).astype(jnp.bfloat16)
        for n, out in enumerate(outs):

            @pl.when(pick == n)
            def write(out=out, turned=turned, j=j):
                out[0, :, :, tile(j)] = turned


def residual(channels, each, frames, prev_fg, depth_valid):
    count, chans, rows, cols = frames.shape
    picks = channels.shape[0]
    halves = count // PACK

    def image_at(p, c, g, first):
        return (g, first[p] + c, 0, 0)

    def valid_at(p, c, g, first):
        return (jnp.where(first[p] + c == chans - 1, g, 0), 0, 0)

    def out_at(n, p, c, g, first):
        early, late = p < n, p > n
        c = jnp.where(early, 0, jnp.where(late, each - 1, c))
        g = jnp.where(early, 0, jnp.where(late, halves - 1, g))
        return (c, 0, g, 0)

    image = pl.BlockSpec((PACK, 1, rows, cols), image_at)
    return pl.pallas_call(
        functools.partial(residual_kernel, chans - 1),
        grid_spec=pltpu.PrefetchScalarGridSpec(
            num_scalar_prefetch=1,
            grid=(picks, each, halves),
            in_specs=[image, image, pl.BlockSpec((PACK, rows, cols), valid_at)],
            out_specs=[
                pl.BlockSpec((1, rows, PACK, cols), functools.partial(out_at, n)) for n in range(picks)
            ],
        ),
        out_shape=[jax.ShapeDtypeStruct((each, rows, count, cols), jnp.bfloat16)] * picks,
        cost_estimate=cost(1.5),
        name="residual",
    )(channels, frames, prev_fg, depth_valid)


def interleave_kernel(frames_ref, valid_ref, order_ref, *refs):
    out_ref, top_ref, bottom_ref = refs[-3:]
    count, chans, rows, cols = frames_ref.shape
    edge = NSWEEP
    for c in range(chans + 1):
        for g in range(count // PACK):
            some = pl.ds(g * PACK, PACK)
            if c < chans:
                lines = frames_ref[some, c]
            else:
                lines = valid_ref[some].astype(jnp.float32).astype(jnp.bfloat16)
            lines = short_dot(lines.reshape(PACK * rows, cols), order_ref[...], 1, 0)
            for j in range(cols // LANE):
                turned = lines[:, LANE * j : LANE * (j + 1)].reshape(PACK, rows, LANE)
                turned = jnp.swapaxes(turned, 0, 1).astype(jnp.bfloat16)
                out_ref[c, :, some, tile(j)] = turned
                top_ref[c, :, some, tile(j)] = turned[:edge]
                bottom_ref[c, :, some, tile(j)] = turned[rows - edge :]


def interleaved(frames, depth_valid, order, after):
    count, chans, rows, cols = frames.shape
    return pl.pallas_call(
        interleave_kernel,
        in_specs=[vmem()] * 3 + [anywhere()] * len(after),
        out_specs=[vmem()] * 3,
        out_shape=[
            jax.ShapeDtypeStruct((chans + 1, height, count, cols), jnp.bfloat16)
            for height in (rows, NSWEEP, NSWEEP)
        ],
        compiler_params=room(),
        cost_estimate=cost(3.3),
        name="interleave",
    )(frames, depth_valid, order, *after)


def gram_kernel(groups, each, nval, ids_ref, *refs):
    blocks, (gram_ref, all_ref, top_ref, bottom_ref) = refs[:groups], refs[-4:]
    lines, count, cols = blocks[0].shape
    for k, block in enumerate(blocks):
        start = pl.multiple_of(ids_ref[groups + k] * count, count)
        all_ref[:, pl.ds(start, count), :] = block[...]
    rows = lines // each
    for c in range(each):
        top_ref[c] = all_ref[c * rows : c * rows + NSWEEP]
        bottom_ref[c] = all_ref[(c + 1) * rows - NSWEEP : (c + 1) * rows]
    total = jnp.zeros(gram_ref.shape, jnp.float32)
    for r in range(lines):
        total = total + short_dot(all_ref[r], all_ref[r], 1, 1)
    gram_ref[...] = total / nval


def gram_terms(ids, blocks, each, nval, after):
    groups = len(blocks)
    lines, count, cols = blocks[0].shape
    every = groups * count
    return pl.pallas_call(
        functools.partial(gram_kernel, groups, each, nval),
        in_specs=[smem()] + [vmem()] * groups + [anywhere()] * len(after),
        out_specs=[vmem()] * 4,
        out_shape=[
            jax.ShapeDtypeStruct((every, every), jnp.float32),
            jax.ShapeDtypeStruct((lines, every, cols), jnp.bfloat16),
            jax.ShapeDtypeStruct((each, NSWEEP, every, cols), jnp.bfloat16),
            jax.ShapeDtypeStruct((each, NSWEEP, every, cols), jnp.bfloat16),
        ],
        compiler_params=room(),
        cost_estimate=cost(1.4),
        name="gram",
    )(ids, *blocks, *after)


def spread_kernel(ids_ref, mixing_ref, all_ref, above_ref, below_ref, *refs):
    pieces, weights = refs[:-1], refs[-1]
    each, lines, count, cols = pieces[0].shape
    rows = lines - 2 * NSWEEP
    for k in range(len(pieces)):
        start = pl.multiple_of(ids_ref[k] * count, count)
        weights[pl.ds(k * count, count), :] = mixing_ref[pl.ds(start, count), :]
    chosen = weights[...]
    for c in range(each):
        for at in range(lines):
            if at < NSWEEP:
                pixels = above_ref[c, at]
            elif at < NSWEEP + rows:
                pixels = all_ref[c * rows + at - NSWEEP]
            else:
                pixels = below_ref[c, at - NSWEEP - rows]
            back = short_dot(chosen, pixels, 1, 0).astype(jnp.bfloat16)
            for k, piece in enumerate(pieces):
                piece[c, at] = back[k * count : (k + 1) * count]


def spread(ids, mixing, pixels, above, below, groups):
    lines, every, cols = pixels.shape
    each = above.shape[0]
    count = every // groups
    piece = jax.ShapeDtypeStruct((each, lines // each + 2 * NSWEEP, count, cols), jnp.bfloat16)
    return pl.pallas_call(
        spread_kernel,
        in_specs=[smem()] + [vmem()] * 4,
        out_specs=[vmem()] * groups,
        out_shape=[piece] * groups,
        scratch_shapes=[pltpu.VMEM((every, every), jnp.bfloat16)],
        compiler_params=room(),
        cost_estimate=cost(2.5),
        name="spread",
    )(ids, mixing, pixels, above, below)


def gate_kernel(*refs):
    pass


def gate(value, after):
    return pl.pallas_call(
        gate_kernel,
        in_specs=[anywhere()] * (1 + len(after)),
        out_specs=anywhere(),
        out_shape=jax.ShapeDtypeStruct(value.shape, value.dtype),
        input_output_aliases={0: 0},
        name="gate",
    )(value, *after)


def variation_kernel(n_after, scale_ref, at_ref, order_ref, *refs):
    own, above, below, back_ref = refs[:4]
    fg_out, bg_out, token_ref, source, first, second, flat_fg, flat_bg, fg_held, bg_held, sems = refs[
        4 + n_after :
    ]
    chan, at = at_ref[0], at_ref[1]
    edge = NSWEEP
    nf = PACK
    chans, rows, count, cols = own.shape
    chans -= 1
    tiles = cols // LANE
    lines = rows + 2 * edge
    lam, up_flag, down_flag = scale_ref[0], scale_ref[1], scale_ref[2]
    step = STEP_SIZE / lam
    end = lax.broadcasted_iota(jnp.int32, (nf, LANE), 1) == LANE - 1
    strips = ((0, above), (edge, own), (edge + rows, below))
    token_ref[...] = jnp.zeros_like(token_ref)

    def load(ref, i):
        return [ref[i, :, tile(j)] for j in range(tiles)]

    def divergence(over, here, beside):
        left = [pltpu.roll(beside[-1], 1, 1)] + beside[:-1]
        return [(here[j] - over[j]) + (beside[j] - left[j]) for j in range(tiles)]

    def smooth(i, over, here, beside):
        div = divergence(over, here, beside)
        image = load(source, i)
        return [image[j] - STEP_SIZE * div[j] for j in range(tiles)]

    @pl.loop(0, count // nf)
    def some_frames(g):
        some = pl.ds(pl.multiple_of(g * nf, nf), nf)
        copies = [
            pltpu.make_async_copy(held.at[g], out.at[some, chan], sems.at[n, g])
            for n, (held, out) in enumerate(((fg_held, fg_out), (bg_held, bg_out)))
        ]
        for h in range(rows):
            for j in range(tiles):
                back = back_ref[at, edge + h, some, tile(j)].astype(jnp.float32)
                flat_bg[j, pl.ds(h, nf, stride=rows), :] = back
        for j in range(tiles):
            bg_held[g, :, :, tile(j)] = flat_bg[j].astype(jnp.bfloat16).reshape(nf, rows, LANE)
        copies[1].start()

        moved = back_ref[at, :, some, :].reshape(lines * nf, cols)
        moved = short_dot(moved, order_ref[...], 1, 0)
        for start, frames in strips:
            for h in range(frames.shape[1]):
                image = frames[chan, h, some, :].astype(jnp.float32)
                source[start + h] = (image - moved[(start + h) * nf : (start + h + 1) * nf]) * step

        @pl.when(chan == chans - 1)
        def mask():
            for start, frames in strips:
                for h in range(frames.shape[1]):
                    valid = frames[chans, h, some, :].astype(jnp.float32)
                    source[start + h] = source[start + h] * valid

        for sweep in range(NSWEEP):
            here = beside = None
            if sweep:
                here, beside = load(first, sweep), load(second, sweep)
                now = smooth(sweep, load(first, sweep - 1), here, beside)
            else:
                now = load(source, 0)
            for i in range(sweep, lines - 1 - sweep):
                next_here = next_beside = None
                if sweep:
                    next_here, next_beside = load(first, i + 1), load(second, i + 1)
                    later = smooth(i + 1, here, next_here, next_beside)
                else:
                    later = load(source, i + 1)
                right = now[1:] + [jnp.where(end, now[-1], pltpu.roll(now[0], LANE - 1, 1))]
                for j in range(tiles):
                    down = later[j] - now[j]
                    if i == edge - 1:
                        down = down * up_flag
                    if i == edge + rows - 1:
                        down = down * down_flag
                    across = right[j] - now[j]
                    square = down * down + across * across
                    size = square * lax.rsqrt(jnp.maximum(square, 1e-30))
                    scale = pl.reciprocal(1.0 + size, approx=True)
                    first[i, :, tile(j)] = (here[j] - down if sweep else -down) * scale
                    second[i, :, tile(j)] = (beside[j] - across if sweep else -across) * scale
                now, here, beside = later, next_here, next_beside

        over = load(first, edge - 1)
        for h in range(rows):
            here, beside = load(first, edge + h), load(second, edge + h)
            image = smooth(edge + h, over, here, beside)
            for j in range(tiles):
                flat_fg[j, pl.ds(h, nf, stride=rows), :] = image[j] * (lam / STEP_SIZE)
            over = here
        fg = jnp.concatenate([flat_fg[j].astype(jnp.bfloat16) for j in range(tiles)], axis=1)
        fg = short_dot(fg, order_ref[...], 1, 1).astype(jnp.bfloat16)
        fg_held[g] = fg.reshape(nf, rows, cols)
        copies[0].start()

    for g in range(count // nf):
        for n, (held, out) in enumerate(((fg_held, fg_out), (bg_held, bg_out))):
            pltpu.make_async_copy(held.at[g], out.at[pl.ds(g * nf, nf), chan], sems.at[n, g]).wait()


def variation(scales, at, order, own, above, below, back, outs, after, shape):
    count, chans, rows, cols = shape
    lines = rows + 2 * NSWEEP
    flat = pltpu.VMEM((cols // LANE, PACK * rows, LANE), jnp.float32)
    field = pltpu.VMEM((lines, PACK, cols), jnp.float32)
    held = pltpu.VMEM((count // PACK, PACK, rows, cols), jnp.bfloat16)
    return pl.pallas_call(
        functools.partial(variation_kernel, len(outs) + len(after)),
        in_specs=[smem(), smem()] + [vmem()] * 5 + [anywhere()] * (len(outs) + len(after)),
        out_specs=[anywhere(), anywhere(), vmem()],
        out_shape=[jax.ShapeDtypeStruct(shape, jnp.bfloat16)] * 2
        + [jax.ShapeDtypeStruct((SUB, LANE), jnp.float32)],
        scratch_shapes=[
            field,
            field,
            field,
            flat,
            flat,
            held,
            held,
            pltpu.SemaphoreType.DMA((2, count // PACK)),
        ],
        input_output_aliases={7 + n: n for n in range(len(outs))},
        compiler_params=room(field, field, field, flat, flat, held, held),
        cost_estimate=cost(8.5),
        name="variation",
    )(scales, at, order, own, above, below, back, *outs, *after)


def body(frames, prev_fg, depth_valid, sketch, tv_weight):
    count, chans, rows, cols = frames.shape
    groups = lax.axis_size("frame")
    strips = lax.axis_size("pix")
    each = chans // groups
    nval = chans * rows * strips * cols
    tiles = cols // LANE
    me = lax.axis_index("frame")
    targets = [partner(me, k, groups) for k in range(groups)]
    sources = [partner(me, k, groups, back=True) for k in range(groups)]
    ids = jnp.stack(targets + sources).astype(jnp.int32)
    near = [k for k in range(1, groups) if power_of_two(k)]
    far = [k for k in range(1, groups) if not power_of_two(k)]

    resid = {}
    for picks in (near, far + [0]):
        channels = jnp.stack([targets[k] * each for k in picks]).astype(jnp.int32)
        resid.update(zip(picks, residual(channels, each, frames, prev_fg, depth_valid)))
    blocks = [resid[0]] + [swap(resid[k], "frame", k) for k in range(1, groups)]
    blocks = [block.reshape(each * rows, count, cols) for block in blocks]

    places = lax.broadcasted_iota(jnp.int32, (cols, cols), 1)
    places = places % LANE * tiles + places // LANE
    order = (places == lax.broadcasted_iota(jnp.int32, (cols, cols), 0)).astype(jnp.bfloat16)
    lined, top, bottom = interleaved(frames, depth_valid, order, tuple(resid.values()))
    got = tuple(blocks[k] for k in near)
    lined_above = from_behind(gate(bottom, got), "pix", 1)
    lined_below = from_behind(gate(top, got), "pix", -1)

    after = (lined_above, lined_below)
    terms, pixels, top, bottom = gram_terms(ids, blocks, each, nval, after)
    above = from_behind(bottom, "pix", 1)
    below = from_behind(top, "pix", -1)
    gram = all_sum(all_sum(terms, "frame"), "pix")
    mixing = mixing_matrix(gram, sketch)
    pieces = spread(ids, mixing, pixels, above, below, groups)
    arrived = {0: pieces[0]}
    for k in near:
        arrived[k] = swap(pieces[k], "frame", k)

    strip = lax.axis_index("pix")
    flags = [(strip > 0).astype(jnp.float32), (strip < strips - 1).astype(jnp.float32)]
    outs = []
    for k in [0] + near + far:
        for c in range(each):
            chan = sources[k] * each + c
            lam = lax.dynamic_index_in_dim(tv_weight, chan, keepdims=False)
            *outs, token = variation(
                jnp.stack([lam] + flags),
                jnp.stack([chan, c]).astype(jnp.int32),
                order,
                lined,
                lined_above,
                lined_below,
                arrived[k],
                outs,
                (),
                frames.shape,
            )
        if k == 0:
            for other in far:
                held = gate(pieces[other], (token,) + tuple(arrived[one] for one in near))
                arrived[other] = swap(held, "frame", other)
    foreground, background = outs
    return (background, foreground)


def solution(mesh):
    placed = (
        P("frame", None, "pix", None),
        P("frame", None, "pix", None),
        P("frame", "pix", None),
        P(),
        P(),
    )
    return jax.shard_map(
        body,
        mesh=mesh,
        in_specs=placed,
        out_specs=(P("frame", None, "pix", None), P("frame", None, "pix", None)),
        check_vma=False,
    )
```

time: 175 us -> 158 us (0.903)
  starting transfers between devices: 40.5 us -> 25.8 us
  waiting for transfers between devices: 45 us -> 37.1 us
  Pallas kernels: 61.5 us -> 65.6 us
    ppermute x8 -> x4, starting transfers between devices: 22.7 us -> 8.64 us  [from_behind(): lax.ppermute(value, axis, [(source, source + steps) for source in range(l...]
    ppermute x13, waiting for transfers between devices: 43.2 us -> 37.1 us  [swap(): return lax.ppermute(value, axis, pairs)]
    pallas_call x8, Pallas kernels: 15.5 us -> 18.8 us  [the longest x2 10.4 us: residual(): pl.pallas_call(functools.partial(residual_kernel, chans - 1), grid_spec=p...]
    ppermute x8 -> x4, waiting for transfers between devices: 1.87 us -> 0.01 us  [from_behind(): lax.ppermute(value, axis, [(source, source + steps) for source in range(l...]
    another operation x5 -> x10, other arithmetic: 2.96 us -> 4.24 us  [the longest x4 2.77 us: body(): jnp.stack([lam] + flags)]
    unnamed x50 -> x44, local copies, waits for them, and re-layouts: 20.4 us -> 21.1 us
  transfers between devices with their start and end apart: 21 -> 17, of which waited for: 13 -> 6; matrix products, arithmetic and copies ran while one was open for 2% -> 3% of each run, Pallas kernels for 18% -> 29%
where the time goes in v1:
time: 158 us; the launch traced here: 156 us
  Pallas kernels  65.6 us (42%)
  waiting for transfers between devices  37.1 us (23%)
  starting transfers between devices  25.8 us (16%)
  local copies, waits for them, and re-layouts  21.9 us (14%)
  other arithmetic  5.05 us (3%)
    ppermute x13, waiting for transfers between devices, swap(): return lax.ppermute(value, axis, pairs)  37.1 us
    pallas_call x4, Pallas kernels, variation(): pl.pallas_call(functools.partial(variation_kernel, len(outs) + len(after)...  36.1 us
    unnamed x44, local copies, waits for them, and re-layouts  21.1 us
    ppermute x13, starting transfers between devices, swap(): return lax.ppermute(value, axis, pairs)  17.1 us
    pallas_call x1, Pallas kernels, mixing_matrix(): pl.pallas_call(mixing_kernel, out_shape=jax.ShapeDtypeStruct(gram.shape,...  10.6 us
    pallas_call x2, Pallas kernels, residual(): pl.pallas_call(functools.partial(residual_kernel, chans - 1), grid_spec=p...  10.4 us
    ppermute x4, starting transfers between devices, from_behind(): lax.ppermute(value, axis, [(source, source + steps) for source in range(l...  8.64 us
    pallas_call x1, Pallas kernels, spread(): pl.pallas_call(spread_kernel, in_specs=[smem()] + [vmem()] * 4, out_specs...  3.5 us
  transfers between devices with their start and end apart: 17, of which 6 were waited for; matrix products, arithmetic and copies ran while one was open for 3% of the time, Pallas kernels for 29%

profile of v1, /device:TPU:0, one launch (start us, length us, event | category | flops | bytes accessed | tf_op | source)
XLA Modules:
  0.0 156.4 jit_solution(6328126433237232574)
XLA Ops:
  1.2 5.2 %residual.2 = (bf16[1,16,32,512]{3,2,1,0:T(8,128)(2,1)}, bf16[1,16,32,512]{3,2,1,0:T(8,128)(2,1)}) custom-call(s32[2]{0:T(128)} %pad_add_fusion.4.channel_ref, bf16[32,4,16,512]{3,2,1,0:T(8,128)(2,1)} %frames_ref.5, bf16[32,4,16,512]{3,2,1,0:T(8,128)(2,1)} %prev_ref.3, s32[32,16,512]{2,1,0:T(8,128)} %valid_ref.5), custom_call_target="tpu_custom_call" | custom-call | bytes 5400000 | tf_op jit(solution)/shard_map/residual/pallas_call | solution.py:200
  6.4 3.1 %collective-permute-start = (bf16[1,16,32,512]{3,2,1,0:T(8,128)(2,1)}, bf16[1,16,32,512]{3,2,1,0:T(8,128)(2,1)S(1)}, u32[]{:S(2)}, u32[]{:S(2)}) collective-permute-start(bf16[1,16,32,512]{3,2,1,0:T(8,128)(2,1)} %get-tuple-element.26.refs_0_), channel_id=1, source_target_pairs={{0,8},{8,0},{16,24},{24,16},{1,9},{9,1},{17,25},{25,17},{2,10},{10... | collective-permute-start | bytes 1572872 | tf_op jit(solution)/shard_map/ppermute | solution.py:39
  9.5 1.4 collective-permute-start.1
  11.4 5.2 %residual.3 = (bf16[1,16,32,512]{3,2,1,0:T(8,128)(2,1)}, bf16[1,16,32,512]{3,2,1,0:T(8,128)(2,1)}) custom-call(s32[2]{0:T(128)} %pad_add_fusion.5.channel_ref, bf16[32,4,16,512]{3,2,1,0:T(8,128)(2,1)} %frames_ref.5, bf16[32,4,16,512]{3,2,1,0:T(8,128)(2,1)} %prev_ref.3, s32[32,16,512]{2,1,0:T(8,128)} %valid_ref.5), custom_call_target="tpu_custom_call" | custom-call | bytes 5400000 | tf_op jit(solution)/shard_map/residual/pallas_call | solution.py:200
  16.8 1.8 %copy-done.3 = bf16[32,4,16,512]{3,2,1,0:T(8,128)(2,1)S(1)} copy-done((bf16[32,4,16,512]{3,2,1,0:T(8,128)(2,1)S(1)}, bf16[32,4,16,512]{3,2,1,0:T(8,128)(2,1)}, u32[]{:S(2)}) %copy-start.3) | copy-done | bytes 2097176
  18.6 1.2 copy-done.4
  19.8 1.0 copy-done.9
  20.9 1.0 copy-done.16
  21.9 1.0 copy-done.17
  22.9 1.0 copy-done.18
  24.0 2.0 %interleave.1 = (bf16[5,16,32,512]{3,2,1,0:T(8,128)(2,1)S(1)}, bf16[5,5,32,512]{3,2,1,0:T(8,128)(2,1)S(1)}, bf16[5,5,32,512]{3,2,1,0:T(8,128)(2,1)S(1)}) custom-call(bf16[32,4,16,512]{3,2,1,0:T(8,128)(2,1)S(1)} %copy-done.3, s32[32,16,512]{2,1,0:T(8,128)S(1)} %copy-done.4, bf16[512,512]{1,0:T(8,128)(2,1)S(1)} %fusion.order_ref, ...), custom_call_target="tpu_custom_call" | custom-call | bytes 11880000 | tf_op jit(solution)/shard_map/interleave/pallas_call | solution.py:238
  26.0 0.9 copy-done.14
  26.9 0.9 copy-done.15
  27.8 0.8 copy-done.5
  28.5 1.3 collective-permute-start.3
  29.8 4.0 %collective-permute-start.2 = (bf16[5,5,32,512]{3,2,1,0:T(8,128)(2,1)}, bf16[5,5,32,512]{3,2,1,0:T(8,128)(2,1)}, u32[]{:S(2)}, u32[]{:S(2)}) collective-permute-start(bf16[5,5,32,512]{3,2,1,0:T(8,128)(2,1)} %gate.3), channel_id=1, source_target_pairs={{0,1},{1,2},{2,3},{3,4},{4,5},{5,6},{6,7},{8,9},{9,10},{10,11},{11... | collective-permute-start | bytes 2457608 | tf_op jit(solution)/shard_map/ppermute | solution.py:23
  34.1 15.1 %collective-permute-done.4 = bf16[1,16,32,512]{3,2,1,0:T(8,128)(2,1)} collective-permute-done((bf16[1,16,32,512]{3,2,1,0:T(8,128)(2,1)}, bf16[1,16,32,512]{3,2,1,0:T(8,128)(2,1)}, u32[]{:S(2)}, u32[]{:S(2)}) %collective-permute-start.4) | collective-permute-done | bytes 524320 | tf_op jit(solution)/shard_map/ppermute | solution.py:39
  49.2 1.0 copy-done.6
  50.2 1.0 copy-done.10
  51.3 3.0 %gram.1 = (f32[128,128]{1,0:T(8,128)S(1)}, bf16[16,128,512]{2,1,0:T(8,128)(2,1)S(1)}, bf16[1,5,128,512]{3,2,1,0:T(8,128)(2,1)}, bf16[1,5,128,512]{3,2,1,0:T(8,128)(2,1)}) custom-call(s32[8]{0:T(128)S(1)} %stack.91.ids_ref, bf16[16,32,512]{2,1,0:T(8,128)(2,1)S(1)} %bitcast.14, bf16[16,32,512]{2,1,0:T(8,128)(2,1)S(1)} %bitcast.13, ...), custom_call_target="tpu_custom_call" | custom-call | bytes 5040000 | tf_op jit(solution)/shard_map/gram/pallas_call | solution.py:272
  54.3 1.3 copy-done.7
  56.2 1.4 collective-permute-start.6
  57.6 1.5 collective-permute-start.5
  59.1 2.1 %collective-permute-start.12 = (bf16[1,5,128,512]{3,2,1,0:T(8,128)(2,1)}, bf16[1,5,128,512]{3,2,1,0:T(8,128)(2,1)}, u32[]{:S(2)}, u32[]{:S(2)}) collective-permute-start(bf16[1,5,128,512]{3,2,1,0:T(8,128)(2,1)} %get-tuple-element.35), channel_id=1, source_target_pairs={{0,1},{1,2},{2,3},{3,4},{4,5},{5,6},{6,7},{8,9},{9,10},{10,11},{11... | collective-permute-start | bytes 1966088 | tf_op jit(solution)/shard_map/ppermute | solution.py:23
  61.2 1.3 collective-permute-start.13
  62.6 1.7 %collective-permute-start.8 = (f32[128,128]{1,0:T(8,128)S(1)}, f32[128,128]{1,0:T(8,128)S(1)}, u32[]{:S(2)}, u32[]{:S(2)}) collective-permute-start(f32[128,128]{1,0:T(8,128)S(1)} %add_add_fusion.1), channel_id=1, source_target_pairs={{0,1},{1,0},{2,3},{3,2},{4,5},{5,4},{6,7},{7,6},{8,9},{9,8},{10,11... | collective-permute-start | bytes 196616 | tf_op jit(solution)/shard_map/ppermute | solution.py:39
  64.3 1.5 collective-permute-done.8
  65.8 2.1 %collective-permute-start.11 = (f32[128,128]{1,0:T(8,128)S(1)}, f32[128,128]{1,0:T(8,128)S(1)}, u32[]{:S(2)}, u32[]{:S(2)}) collective-permute-start(f32[128,128]{1,0:T(8,128)S(1)} %add.68), channel_id=1, source_target_pairs={{0,6},{1,7},{2,4},{3,5},{4,2},{5,3},{6,0},{7,1},{8,14},{9,15},{10,... | collective-permute-start | bytes 196616 | tf_op jit(solution)/shard_map/ppermute | solution.py:39
  68.0 1.0 collective-permute-start.10
  68.9 1.3 collective-permute-start.9
  70.3 7.9 %collective-permute-done.11 = f32[128,128]{1,0:T(8,128)S(1)} collective-permute-done((f32[128,128]{1,0:T(8,128)S(1)}, f32[128,128]{1,0:T(8,128)S(1)}, u32[]{:S(2)}, u32[]{:S(2)}) %collective-permute-start.11) | collective-permute-done | bytes 65568 | tf_op jit(solution)/shard_map/ppermute | solution.py:39
  78.1 3.0 %collective-permute-done.10 = f32[128,128]{1,0:T(8,128)S(1)} collective-permute-done((f32[128,128]{1,0:T(8,128)S(1)}, f32[128,128]{1,0:T(8,128)S(1)}, u32[]{:S(2)}, u32[]{:S(2)}) %collective-permute-start.10) | collective-permute-done | bytes 65568 | tf_op jit(solution)/shard_map/ppermute | solution.py:39
  81.8 10.6 %mixing.1.mixing_ref = bf16[128,128]{1,0:T(8,128)(2,1)} custom-call(f32[128,128]{1,0:T(8,128)} %add_add_fusion.gram_ref, f32[64,128]{1,0:T(8,128)} %bitcast.15), custom_call_target="tpu_custom_call" | custom-call | bytes 38160000 | tf_op jit(solution)/shard_map/mixing/pallas_call | solution.py:133
  92.4 1.6 %copy-done.8 = bf16[16,128,512]{2,1,0:T(8,128)(2,1)S(1)} copy-done((bf16[16,128,512]{2,1,0:T(8,128)(2,1)S(1)}, bf16[16,128,512]{2,1,0:T(8,128)(2,1)}, u32[]{:S(2)}) %copy-start.8) | copy-done | bytes 2097176
  94.0 0.8 copy-done.19
  94.8 3.5 %spread.1 = (bf16[1,26,32,512]{3,2,1,0:T(8,128)(2,1)S(1)}, bf16[1,26,32,512]{3,2,1,0:T(8,128)(2,1)}, bf16[1,26,32,512]{3,2,1,0:T(8,128)(2,1)}, bf16[1,26,32,512]{3,2,1,0:T(8,128)(2,1)S(1)}) custom-call(s32[8]{0:T(128)S(1)} %stack.91.ids_ref, bf16[128,128]{1,0:T(8,128)(2,1)S(1)} %copy-done.19, bf16[16,128,512]{2,1,0:T(8,128)(2,1)S(1)} %copy-done.8, ...), custom_call_target="tpu_custom_call" | custom-call | bytes 9000000 | tf_op jit(solution)/shard_map/spread/pallas_call | solution.py:314
  98.3 0.9 copy-done.11
  99.2 0.9 copy-done.13
  102.7 1.0 copy-done.1
  103.8 1.2 copy-done.12
  104.9 8.5 %variation.4 = (bf16[32,4,16,512]{3,2,1,0:T(8,128)(2,1)}, bf16[32,4,16,512]{3,2,1,0:T(8,128)(2,1)}, f32[8,128]{1,0:T(8,128)S(1)}) custom-call(f32[3]{0:T(128)S(1)} %maximum_maximum_fusion.1.scale_ref, s32[2]{0:T(128)S(1)} %pad_add_fusion.2.at_ref, bf16[512,512]{1,0:T(8,128)(2,1)S(1)} %copy-done.1, bf16[5,16,32,512]{3,2,1,0:T(8,128)(2,1)S(1)} %get-tuple-element.30.refs_0_, ...), custom_call_target="tpu_custom_call" | custom-call | bytes 30600000 | tf_op jit(solution)/shard_map/variation/pallas_call | solution.py:452
  114.0 4.2 %collective-permute-done.14.refs_2_.refs_3_ = bf16[1,26,32,512]{3,2,1,0:T(8,128)(2,1)} collective-permute-done((bf16[1,26,32,512]{3,2,1,0:T(8,128)(2,1)}, bf16[1,26,32,512]{3,2,1,0:T(8,128)(2,1)}, u32[]{:S(2)}, u32[]{:S(2)}) %collective-permute-start.14) | collective-permute-done | bytes 852000 | tf_op jit(solution)/shard_map/ppermute | solution.py:39
  118.3 5.4 %collective-permute-done.15.refs_3_ = bf16[1,26,32,512]{3,2,1,0:T(8,128)(2,1)} collective-permute-done((bf16[1,26,32,512]{3,2,1,0:T(8,128)(2,1)}, bf16[1,26,32,512]{3,2,1,0:T(8,128)(2,1)}, u32[]{:S(2)}, u32[]{:S(2)}) %collective-permute-start.15) | collective-permute-done | bytes 852000 | tf_op jit(solution)/shard_map/ppermute | solution.py:39
  123.7 1.5 collective-permute-start.16
  127.5 1.0 copy-done.2
  128.6 9.2 %variation.5 = (bf16[32,4,16,512]{3,2,1,0:T(8,128)(2,1)}, bf16[32,4,16,512]{3,2,1,0:T(8,128)(2,1)}, f32[8,128]{1,0:T(8,128)}) custom-call(f32[3]{0:T(128)S(1)} %maximum_maximum_fusion.3.scale_ref, s32[2]{0:T(128)S(1)} %pad_add_fusion.at_ref, bf16[512,512]{1,0:T(8,128)(2,1)S(1)} %copy-done.2, ...), custom_call_target="tpu_custom_call", output_to_operand_aliasing={{0}: (7, {}), {1}: (8, {})} | custom-call | bytes 30600000 | tf_op jit(solution)/shard_map/variation/pallas_call | solution.py:452
  137.7 9.2 %variation.6 = (bf16[32,4,16,512]{3,2,1,0:T(8,128)(2,1)}, bf16[32,4,16,512]{3,2,1,0:T(8,128)(2,1)}, f32[8,128]{1,0:T(8,128)}) custom-call(f32[3]{0:T(128)S(1)} %maximum_maximum_fusion.2.scale_ref, s32[2]{0:T(128)S(1)} %pad_add_fusion.1.at_ref, bf16[512,512]{1,0:T(8,128)(2,1)S(1)} %copy-done.2, ...), custom_call_target="tpu_custom_call", output_to_operand_aliasing={{0}: (7, {}), {1}: (8, {})} | custom-call | bytes 30600000 | tf_op jit(solution)/shard_map/variation/pallas_call | solution.py:452
  146.9 9.3 %variation.7 = (bf16[32,4,16,512]{3,2,1,0:T(8,128)(2,1)}, bf16[32,4,16,512]{3,2,1,0:T(8,128)(2,1)}, f32[8,128]{1,0:T(8,128)}) custom-call(f32[3]{0:T(128)S(1)} %maximum_maximum_fusion.scale_ref, s32[2]{0:T(128)S(1)} %pad_add_fusion.3.at_ref, bf16[512,512]{1,0:T(8,128)(2,1)S(1)} %copy-done.2, ...), custom_call_target="tpu_custom_call", output_to_operand_aliasing={{0}: (7, {}), {1}: (8, {})} | custom-call | bytes 30600000 | tf_op jit(solution)/shard_map/variation/pallas_call | solution.py:452
  (62 shorter events, 8.5 us)
Async XLA Ops:
  6.4 21.4 %collective-permute-start = (bf16[1,16,32,512]{3,2,1,0:T(8,128)(2,1)}, bf16[1,16,32,512]{3,2,1,0:T(8,128)(2,1)S(1)}, u32[]{:S(2)}, u32[]{:S(2)}) collective-permute-start(bf16[1,16,32,512]{3,2,1,0:T(8,128)(2,1)} %get-tuple-element.26.refs_0_), channel_id=1, source_target_pairs={{0,8},{8,0},{16,24},{24,16},{1,9},{9,1},{17,25},{25,17},{2,10},{10... | collective-permute-start | bytes 1572872 | tf_op jit(solution)/shard_map/ppermute | solution.py:39
  9.5 18.3 %collective-permute-start.1 = (bf16[1,16,32,512]{3,2,1,0:T(8,128)(2,1)}, bf16[1,16,32,512]{3,2,1,0:T(8,128)(2,1)}, u32[]{:S(2)}, u32[]{:S(2)}) collective-permute-start(bf16[1,16,32,512]{3,2,1,0:T(8,128)(2,1)} %get-tuple-element.27.refs_1_), channel_id=1, source_target_pairs={{0,16},{8,24},{16,0},{24,8},{1,17},{9,25},{17,1},{25,9},{2,18},{10... | collective-permute-start | bytes 1572872 | tf_op jit(solution)/shard_map/ppermute | solution.py:39
  16.8 9.2 %copy-start = (bf16[512,512]{1,0:T(8,128)(2,1)}, bf16[512,512]{1,0:T(8,128)(2,1)S(1)}, u32[]{:S(2)}) copy-start(bf16[512,512]{1,0:T(8,128)(2,1)S(1)} %fusion.order_ref) | copy-start | bytes 1572868
  16.8 1.8 %copy-start.3 = (bf16[32,4,16,512]{3,2,1,0:T(8,128)(2,1)S(1)}, bf16[32,4,16,512]{3,2,1,0:T(8,128)(2,1)}, u32[]{:S(2)}) copy-start(bf16[32,4,16,512]{3,2,1,0:T(8,128)(2,1)} %frames_ref.5) | copy-start | bytes 6291460
  18.6 1.2 copy-start.4
  19.8 1.0 copy-start.9
  20.9 1.0 copy-start.16
  21.9 1.0 copy-start.17
  22.9 1.0 copy-start.18
  26.0 0.9 copy-start.14
  26.9 0.9 copy-start.15
  27.7 0.8 copy-start.5
  28.5 20.6 %collective-permute-start.3 = (bf16[5,5,32,512]{3,2,1,0:T(8,128)(2,1)}, bf16[5,5,32,512]{3,2,1,0:T(8,128)(2,1)S(1)}, u32[]{:S(2)}, u32[]{:S(2)}) collective-permute-start(bf16[5,5,32,512]{3,2,1,0:T(8,128)(2,1)} %gate.4), channel_id=1, source_target_pairs={{1,0},{2,1},{3,2},{4,3},{5,4},{6,5},{7,6},{9,8},{10,9},{11,10},{12... | collective-permute-start | bytes 2457608 | tf_op jit(solution)/shard_map/ppermute | solution.py:23
  29.8 19.4 %collective-permute-start.2 = (bf16[5,5,32,512]{3,2,1,0:T(8,128)(2,1)}, bf16[5,5,32,512]{3,2,1,0:T(8,128)(2,1)}, u32[]{:S(2)}, u32[]{:S(2)}) collective-permute-start(bf16[5,5,32,512]{3,2,1,0:T(8,128)(2,1)} %gate.3), channel_id=1, source_target_pairs={{0,1},{1,2},{2,3},{3,4},{4,5},{5,6},{6,7},{8,9},{9,10},{10,11},{11... | collective-permute-start | bytes 2457608 | tf_op jit(solution)/shard_map/ppermute | solution.py:23
  33.8 15.4 %collective-permute-start.4 = (bf16[1,16,32,512]{3,2,1,0:T(8,128)(2,1)}, bf16[1,16,32,512]{3,2,1,0:T(8,128)(2,1)}, u32[]{:S(2)}, u32[]{:S(2)}) collective-permute-start(bf16[1,16,32,512]{3,2,1,0:T(8,128)(2,1)} %get-tuple-element.28.refs_2_), channel_id=1, source_target_pairs={{0,24},{8,16},{16,8},{24,0},{1,25},{9,17},{17,9},{25,1},{2,26},{10... | collective-permute-start | bytes 1572872 | tf_op jit(solution)/shard_map/ppermute | solution.py:39
  49.2 1.0 copy-start.6
  50.2 1.0 copy-start.10
  54.3 1.3 copy-start.7
  55.6 6.9 %collective-permute-start.7 = (f32[128,128]{1,0:T(8,128)S(1)}, f32[128,128]{1,0:T(8,128)S(1)}, u32[]{:S(2)}, u32[]{:S(2)}) collective-permute-start(f32[128,128]{1,0:T(8,128)S(1)} %get-tuple-element.33), channel_id=1, source_target_pairs={{0,24},{8,16},{16,8},{24,0},{1,25},{9,17},{17,9},{25,1},{2,26},{10... | collective-permute-start | bytes 196616 | tf_op jit(solution)/shard_map/ppermute | solution.py:39
  56.2 6.3 %collective-permute-start.6 = (f32[128,128]{1,0:T(8,128)S(1)}, f32[128,128]{1,0:T(8,128)S(1)}, u32[]{:S(2)}, u32[]{:S(2)}) collective-permute-start(f32[128,128]{1,0:T(8,128)S(1)} %get-tuple-element.33), channel_id=1, source_target_pairs={{0,16},{8,24},{16,0},{24,8},{1,17},{9,25},{17,1},{25,9},{2,18},{10... | collective-permute-start | bytes 196616 | tf_op jit(solution)/shard_map/ppermute | solution.py:39
  57.6 4.9 %collective-permute-start.5 = (f32[128,128]{1,0:T(8,128)S(1)}, f32[128,128]{1,0:T(8,128)S(1)}, u32[]{:S(2)}, u32[]{:S(2)}) collective-permute-start(f32[128,128]{1,0:T(8,128)S(1)} %get-tuple-element.33), channel_id=1, source_target_pairs={{0,8},{8,0},{16,24},{24,16},{1,9},{9,1},{17,25},{25,17},{2,10},{10... | collective-permute-start | bytes 196616 | tf_op jit(solution)/shard_map/ppermute | solution.py:39
  59.1 33.3 %collective-permute-start.12 = (bf16[1,5,128,512]{3,2,1,0:T(8,128)(2,1)}, bf16[1,5,128,512]{3,2,1,0:T(8,128)(2,1)}, u32[]{:S(2)}, u32[]{:S(2)}) collective-permute-start(bf16[1,5,128,512]{3,2,1,0:T(8,128)(2,1)} %get-tuple-element.35), channel_id=1, source_target_pairs={{0,1},{1,2},{2,3},{3,4},{4,5},{5,6},{6,7},{8,9},{9,10},{10,11},{11... | collective-permute-start | bytes 1966088 | tf_op jit(solution)/shard_map/ppermute | solution.py:23
  61.2 31.2 %collective-permute-start.13 = (bf16[1,5,128,512]{3,2,1,0:T(8,128)(2,1)}, bf16[1,5,128,512]{3,2,1,0:T(8,128)(2,1)}, u32[]{:S(2)}, u32[]{:S(2)}) collective-permute-start(bf16[1,5,128,512]{3,2,1,0:T(8,128)(2,1)} %get-tuple-element.36), channel_id=1, source_target_pairs={{1,0},{2,1},{3,2},{4,3},{5,4},{6,5},{7,6},{9,8},{10,9},{11,10},{12... | collective-permute-start | bytes 1966088 | tf_op jit(solution)/shard_map/ppermute | solution.py:23
  62.6 38.7 %copy-start.21 = (f32[4]{0:T(128)S(1)}, f32[4]{0:T(128)}, u32[]{:S(2)}) copy-start(f32[4]{0:T(128)} %param.9) | copy-start | bytes 52
  62.6 3.2 %collective-permute-start.8 = (f32[128,128]{1,0:T(8,128)S(1)}, f32[128,128]{1,0:T(8,128)S(1)}, u32[]{:S(2)}, u32[]{:S(2)}) collective-permute-start(f32[128,128]{1,0:T(8,128)S(1)} %add_add_fusion.1), channel_id=1, source_target_pairs={{0,1},{1,0},{2,3},{3,2},{4,5},{5,4},{6,7},{7,6},{8,9},{9,8},{10,11... | collective-permute-start | bytes 196616 | tf_op jit(solution)/shard_map/ppermute | solution.py:39
  65.8 12.3 %collective-permute-start.11 = (f32[128,128]{1,0:T(8,128)S(1)}, f32[128,128]{1,0:T(8,128)S(1)}, u32[]{:S(2)}, u32[]{:S(2)}) collective-permute-start(f32[128,128]{1,0:T(8,128)S(1)} %add.68), channel_id=1, source_target_pairs={{0,6},{1,7},{2,4},{3,5},{4,2},{5,3},{6,0},{7,1},{8,14},{9,15},{10,... | collective-permute-start | bytes 196616 | tf_op jit(solution)/shard_map/ppermute | solution.py:39
  68.0 13.2 %collective-permute-start.10 = (f32[128,128]{1,0:T(8,128)S(1)}, f32[128,128]{1,0:T(8,128)S(1)}, u32[]{:S(2)}, u32[]{:S(2)}) collective-permute-start(f32[128,128]{1,0:T(8,128)S(1)} %add.68), channel_id=1, source_target_pairs={{0,4},{1,5},{2,6},{3,7},{4,0},{5,1},{6,2},{7,3},{8,12},{9,13},{10,... | collective-permute-start | bytes 196616 | tf_op jit(solution)/shard_map/ppermute | solution.py:39
  68.9 12.2 %collective-permute-start.9 = (f32[128,128]{1,0:T(8,128)S(1)}, f32[128,128]{1,0:T(8,128)S(1)}, u32[]{:S(2)}, u32[]{:S(2)}) collective-permute-start(f32[128,128]{1,0:T(8,128)S(1)} %add.68), channel_id=1, source_target_pairs={{0,2},{1,3},{2,0},{3,1},{4,6},{5,7},{6,4},{7,5},{8,10},{9,11},{10,... | collective-permute-start | bytes 196616 | tf_op jit(solution)/shard_map/ppermute | solution.py:39
  92.4 1.6 %copy-start.8 = (bf16[16,128,512]{2,1,0:T(8,128)(2,1)S(1)}, bf16[16,128,512]{2,1,0:T(8,128)(2,1)}, u32[]{:S(2)}) copy-start(bf16[16,128,512]{2,1,0:T(8,128)(2,1)} %copy-done.7) | copy-start | bytes 6291460
  94.0 0.8 copy-start.19
  98.3 0.9 copy-start.11
  99.2 0.9 copy-start.13
  100.1 18.2 %collective-permute-start.14 = (bf16[1,26,32,512]{3,2,1,0:T(8,128)(2,1)}, bf16[1,26,32,512]{3,2,1,0:T(8,128)(2,1)}, u32[]{:S(2)}, u32[]{:S(2)}) collective-permute-start(bf16[1,26,32,512]{3,2,1,0:T(8,128)(2,1)} %get-tuple-element.40), channel_id=1, source_target_pairs={{0,8},{8,0},{16,24},{24,16},{1,9},{9,1},{17,25},{25,17},{2,10},{10... | collective-permute-start | bytes 2555912 | tf_op jit(solution)/shard_map/ppermute | solution.py:39
  100.6 23.1 %collective-permute-start.15 = (bf16[1,26,32,512]{3,2,1,0:T(8,128)(2,1)}, bf16[1,26,32,512]{3,2,1,0:T(8,128)(2,1)}, u32[]{:S(2)}, u32[]{:S(2)}) collective-permute-start(bf16[1,26,32,512]{3,2,1,0:T(8,128)(2,1)} %get-tuple-element.41), channel_id=1, source_target_pairs={{0,16},{8,24},{16,0},{24,8},{1,17},{9,25},{17,1},{25,9},{2,18},{10... | collective-permute-start | bytes 2555912 | tf_op jit(solution)/shard_map/ppermute | solution.py:39
  102.7 1.0 copy-start.1
  103.8 1.2 copy-start.12
  113.4 0.6 copy-start.20
  123.7 23.2 %collective-permute-start.16 = (bf16[1,26,32,512]{3,2,1,0:T(8,128)(2,1)}, bf16[1,26,32,512]{3,2,1,0:T(8,128)(2,1)S(1)}, u32[]{:S(2)}, u32[]{:S(2)}) collective-permute-start(bf16[1,26,32,512]{3,2,1,0:T(8,128)(2,1)} %gate.5), channel_id=1, source_target_pairs={{0,24},{8,16},{16,8},{24,0},{1,25},{9,17},{17,9},{25,1},{2,26},{10... | collective-permute-start | bytes 2555912 | tf_op jit(solution)/shard_map/ppermute | solution.py:39
  127.5 1.0 copy-start.2

commit v2 on v1

--- a/solution.py
+++ b/solution.py
@@ -14,7 +14,8 @@
 SUB = 8
 LANE = 128
 PACK = 16
-SPARE_BYTES = 12 * 1024 * 1024
+SPARE_BYTES = 7 * 1024 * 1024
+MOST_BYTES = 58 * 1024 * 1024
 
 
 def from_behind(value, axis, steps):
@@ -133,6 +134,7 @@
     return pl.pallas_call(
         mixing_kernel,
         out_shape=jax.ShapeDtypeStruct(gram.shape, jnp.bfloat16),
+        compiler_params=room(),
         cost_estimate=cost(10.6),
         name="mixing",
     )(gram, sketch.T)
@@ -163,54 +165,61 @@
     return pl.CostEstimate(flops=0, bytes_accessed=int(micros * 3.6e6), transcendentals=0)
 
 
-def residual_kernel(last, channel_ref, frames_ref, prev_ref, valid_ref, *outs):
-    pick, c = pl.program_id(0), pl.program_id(1)
-    cols = frames_ref.shape[-1]
-    keep = jnp.where(channel_ref[pick] + c == last, 0.0, 1.0)
-    for j in range(cols // LANE):
-        valid = jnp.where(valid_ref[:, :, tile(j)] != 0, 1.0, keep)
-        diff = frames_ref[:, 0, :, tile(j)].astype(jnp.float32)
-        diff = diff - prev_ref[:, 0, :, tile(j)].astype(jnp.float32)
-        turned = jnp.swapaxes(diff * valid, 0, 1).astype(jnp.bfloat16)
-        for n, out in enumerate(outs):
-
-            @pl.when(pick == n)
-            def write(out=out, turned=turned, j=j):
-                out[0, :, :, tile(j)] = turned
-
-
-def residual(channels, each, frames, prev_fg, depth_valid):
+def residual_kernel(last, picks, info_ref, frames_ref, prev_ref, valid_ref, *refs):
+    outs, (now, before, ok, sems) = refs[: len(picks)], refs[len(picks) :]
+    _, each, count, rows, cols = now.shape
+    valid_copy = pltpu.make_async_copy(valid_ref, ok, sems.at[0])
+    copies = []
+    for n, pick in enumerate(picks):
+        for c in range(each):
+            chan = info_ref[pick] * each + c
+            at = 1 + 2 * (n * each + c)
+            copies.append(
+                (
+                    pltpu.make_async_copy(frames_ref.at[:, chan], now.at[n, c], sems.at[at]),
+                    pltpu.make_async_copy(prev_ref.at[:, chan], before.at[n, c], sems.at[at + 1]),
+                )
+            )
+    for copy in copies[0]:
+        copy.start()
+    valid_copy.start()
+    for pair in copies[1:]:
+        for copy in pair:
+            copy.start()
+    valid_copy.wait()
+    for n, pick in enumerate(picks):
+        for c in range(each):
+            for copy in copies[n * each + c]:
+                copy.wait()
+            keep = jnp.where(info_ref[pick] * each + c == last, 0.0, 1.0)
+            for g in range(count // PACK):
+                some = pl.ds(g * PACK, PACK)
+                for j in range(cols // LANE):
+                    valid = jnp.where(ok[some, :, tile(j)] != 0, 1.0, keep)
+                    diff = now[n, c, some, :, tile(j)].astype(jnp.float32)
+                    diff = diff - before[n, c, some, :, tile(j)].astype(jnp.float32)
+                    turned = jnp.swapaxes(diff * valid, 0, 1)
+                    outs[n][c, :, some, tile(j)] = turned.astype(jnp.bfloat16)
+
+
+def residual(info, picks, each, frames, prev_fg, depth_valid):
     count, chans, rows, cols = frames.shape
-    picks = channels.shape[0]
-    halves = count // PACK
-
-    def image_at(p, c, g, first):
-        return (g, first[p] + c, 0, 0)
-
-    def valid_at(p, c, g, first):
-        return (jnp.where(first[p] + c == chans - 1, g, 0), 0, 0)
-
-    def out_at(n, p, c, g, first):
-        early, late = p < n, p > n
-        c = jnp.where(early, 0, jnp.where(late, each - 1, c))
-        g = jnp.where(early, 0, jnp.where(late, halves - 1, g))
-        return (c, 0, g, 0)
-
-    image = pl.BlockSpec((PACK, 1, rows, cols), image_at)
-    return pl.pallas_call(
-        functools.partial(residual_kernel, chans - 1),
-        grid_spec=pltpu.PrefetchScalarGridSpec(
-            num_scalar_prefetch=1,
-            grid=(picks, each, halves),
-            in_specs=[image, image, pl.BlockSpec((PACK, rows, cols), valid_at)],
-            out_specs=[
-                pl.BlockSpec((1, rows, PACK, cols), functools.partial(out_at, n)) for n in range(picks)
-            ],
-        ),
-        out_shape=[jax.ShapeDtypeStruct((each, rows, count, cols), jnp.bfloat16)] * picks,
-        cost_estimate=cost(1.5),
+    held = pltpu.VMEM((len(picks), each, count, rows, cols), jnp.bfloat16)
+    return pl.pallas_call(
+        functools.partial(residual_kernel, chans - 1, picks),
+        in_specs=[smem()] + [anywhere()] * 3,
+        out_specs=[vmem()] * len(picks),
+        out_shape=[jax.ShapeDtypeStruct((each, rows, count, cols), jnp.bfloat16)] * len(picks),
+        scratch_shapes=[
+            held,
+            held,
+            pltpu.VMEM((count, rows, cols), jnp.int32),
+            pltpu.SemaphoreType.DMA((1 + 2 * each * len(picks),)),
+        ],
+        compiler_params=pltpu.CompilerParams(vmem_limit_bytes=MOST_BYTES),
+        cost_estimate=cost(3.0),
         name="residual",
-    )(channels, frames, prev_fg, depth_valid)
+    )(info, frames, prev_fg, depth_valid)
 
 
 def interleave_kernel(frames_ref, valid_ref, order_ref, *refs):
@@ -334,23 +343,27 @@
         out_specs=anywhere(),
         out_shape=jax.ShapeDtypeStruct(value.shape, value.dtype),
         input_output_aliases={0: 0},
+        compiler_params=room(),
         name="gate",
     )(value, *after)
 
 
-def variation_kernel(n_after, scale_ref, at_ref, order_ref, *refs):
+def variation_kernel(pick, at, each, n_after, info_ref, weight_ref, order_ref, *refs):
     own, above, below, back_ref = refs[:4]
     fg_out, bg_out, token_ref, source, first, second, flat_fg, flat_bg, fg_held, bg_held, sems = refs[
         4 + n_after :
     ]
-    chan, at = at_ref[0], at_ref[1]
+    groups = (info_ref.shape[0] - 2) // 2
+    chan = info_ref[groups + pick] * each + at
     edge = NSWEEP
     nf = PACK
     chans, rows, count, cols = own.shape
     chans -= 1
     tiles = cols // LANE
     lines = rows + 2 * edge
-    lam, up_flag, down_flag = scale_ref[0], scale_ref[1], scale_ref[2]
+    lam = weight_ref[chan]
+    up_flag = info_ref[2 * groups].astype(jnp.float32)
+    down_flag = info_ref[2 * groups + 1].astype(jnp.float32)
     step = STEP_SIZE / lam
     end = lax.broadcasted_iota(jnp.int32, (nf, LANE), 1) == LANE - 1
     strips = ((0, above), (edge, own), (edge + rows, below))
@@ -443,15 +456,16 @@
             pltpu.make_async_copy(held.at[g], out.at[pl.ds(g * nf, nf), chan], sems.at[n, g]).wait()
 
 
-def variation(scales, at, order, own, above, below, back, outs, after, shape):
+def variation(info, weights, pick, at, order, own, above, below, back, outs, shape):
     count, chans, rows, cols = shape
     lines = rows + 2 * NSWEEP
+    each = back.shape[0]
     flat = pltpu.VMEM((cols // LANE, PACK * rows, LANE), jnp.float32)
     field = pltpu.VMEM((lines, PACK, cols), jnp.float32)
     held = pltpu.VMEM((count // PACK, PACK, rows, cols), jnp.bfloat16)
     return pl.pallas_call(
-        functools.partial(variation_kernel, len(outs) + len(after)),
-        in_specs=[smem(), smem()] + [vmem()] * 5 + [anywhere()] * (len(outs) + len(after)),
+        functools.partial(variation_kernel, pick, at, each, len(outs)),
+        in_specs=[smem(), smem()] + [vmem()] * 5 + [anywhere()] * len(outs),
         out_specs=[anywhere(), anywhere(), vmem()],
         out_shape=[jax.ShapeDtypeStruct(shape, jnp.bfloat16)] * 2
         + [jax.ShapeDtypeStruct((SUB, LANE), jnp.float32)],
@@ -469,7 +483,7 @@
         compiler_params=room(field, field, field, flat, flat, held, held),
         cost_estimate=cost(8.5),
         name="variation",
-    )(scales, at, order, own, above, below, back, *outs, *after)
+    )(info, weights, order, own, above, below, back, *outs)
 
 
 def body(frames, prev_fg, depth_valid, sketch, tv_weight):
@@ -479,17 +493,17 @@
     each = chans // groups
     nval = chans * rows * strips * cols
     tiles = cols // LANE
-    me = lax.axis_index("frame")
+    me, strip = lax.axis_index("frame"), lax.axis_index("pix")
     targets = [partner(me, k, groups) for k in range(groups)]
     sources = [partner(me, k, groups, back=True) for k in range(groups)]
-    ids = jnp.stack(targets + sources).astype(jnp.int32)
+    ends = [strip > 0, strip < strips - 1]
+    info = jnp.stack([jnp.asarray(one, jnp.int32) for one in targets + sources + ends])
     near = [k for k in range(1, groups) if power_of_two(k)]
     far = [k for k in range(1, groups) if not power_of_two(k)]
 
     resid = {}
     for picks in (near, far + [0]):
-        channels = jnp.stack([targets[k] * each for k in picks]).astype(jnp.int32)
-        resid.update(zip(picks, residual(channels, each, frames, prev_fg, depth_valid)))
+        resid.update(zip(picks, residual(info, picks, each, frames, prev_fg, depth_valid)))
     blocks = [resid[0]] + [swap(resid[k], "frame", k) for k in range(1, groups)]
     blocks = [block.reshape(each * rows, count, cols) for block in blocks]
 
@@ -497,38 +511,34 @@
     places = places % LANE * tiles + places // LANE
     order = (places == lax.broadcasted_iota(jnp.int32, (cols, cols), 0)).astype(jnp.bfloat16)
     lined, top, bottom = interleaved(frames, depth_valid, order, tuple(resid.values()))
-    got = tuple(blocks[k] for k in near)
-    lined_above = from_behind(gate(bottom, got), "pix", 1)
-    lined_below = from_behind(gate(top, got), "pix", -1)
-
-    after = (lined_above, lined_below)
-    terms, pixels, top, bottom = gram_terms(ids, blocks, each, nval, after)
-    above = from_behind(bottom, "pix", 1)
-    below = from_behind(top, "pix", -1)
-    gram = all_sum(all_sum(terms, "frame"), "pix")
+    lined_above = from_behind(bottom, "pix", 1)
+    lined_below = from_behind(top, "pix", -1)
+
+    terms, pixels, top, bottom = gram_terms(info, blocks, each, nval, ())
+    gram = gate(all_sum(terms, "frame"), (lined_above, lined_below))
+    gram = all_sum(gram, "pix")
+    above = from_behind(gate(bottom, (gram,)), "pix", 1)
+    below = from_behind(gate(top, (gram,)), "pix", -1)
     mixing = mixing_matrix(gram, sketch)
-    pieces = spread(ids, mixing, pixels, above, below, groups)
+    pieces = spread(info, mixing, pixels, above, below, groups)
     arrived = {0: pieces[0]}
     for k in near:
         arrived[k] = swap(pieces[k], "frame", k)
 
-    strip = lax.axis_index("pix")
-    flags = [(strip > 0).astype(jnp.float32), (strip < strips - 1).astype(jnp.float32)]
     outs = []
     for k in [0] + near + far:
         for c in range(each):
-            chan = sources[k] * each + c
-            lam = lax.dynamic_index_in_dim(tv_weight, chan, keepdims=False)
             *outs, token = variation(
-                jnp.stack([lam] + flags),
-                jnp.stack([chan, c]).astype(jnp.int32),
+                info,
+                tv_weight,
+                k,
+                c,
                 order,
                 lined,
                 lined_above,
                 lined_below,
                 arrived[k],
                 outs,
-                (),
                 frames.shape,
             )
         if k == 0:

time: 158 us -> 119 us (0.75); the launches traced: 156 us -> 119 us
  local copies, waits for them, and re-layouts: 21.9 us -> 2.74 us
  Pallas kernels: 65.6 us -> 55.8 us
  other arithmetic: 5.05 us -> 0.19 us
  starting transfers between devices: 25.8 us -> 23.2 us
    unnamed x44 -> x18, local copies, waits for them, and re-layouts: 21.1 us -> 2.11 us
    pallas_call x6, Pallas kernels: 46.5 us -> 41.4 us  [the longest x4 33.6 us: variation(): pl.pallas_call(functools.partial(variation_kernel, pick, at, each, len(ou...]
    another operation x10 -> x0, other arithmetic: 4.24 us -> none  [the longest x4 2.77 us: body(): jnp.stack([lam] + flags)]
    ppermute x4, starting transfers between devices: 8.64 us -> 5.75 us  [from_behind(): lax.ppermute(value, axis, [(source, source + steps) for source in range(l...]
    pallas_call x1, Pallas kernels: 3.5 us -> 1.58 us  [spread(): pl.pallas_call(spread_kernel, in_specs=[smem()] + [vmem()] * 4, out_specs...]
  transfers between devices with their start and end apart: 17 -> 17, of which waited for: 6 -> 11; matrix products, arithmetic and copies ran while one was open for 3% -> 0% of each run, Pallas kernels for 29% -> 35%
where the time goes in v2:
time: 119 us
  Pallas kernels  55.8 us (47%)
  waiting for transfers between devices  35.8 us (30%)
  starting transfers between devices  23.2 us (19%)
  local copies, waits for them, and re-layouts  2.74 us (2%)
    ppermute x13, waiting for transfers between devices, swap(): return lax.ppermute(value, axis, pairs)  35.8 us
    pallas_call x4, Pallas kernels, variation(): pl.pallas_call(functools.partial(variation_kernel, pick, at, each, len(ou...  33.6 us
    ppermute x13, starting transfers between devices, swap(): return lax.ppermute(value, axis, pairs)  17.5 us
    pallas_call x1, Pallas kernels, mixing_matrix(): pl.pallas_call(mixing_kernel, out_shape=jax.ShapeDtypeStruct(gram.shape,...  9.18 us
    pallas_call x2, Pallas kernels, residual(): pl.pallas_call(functools.partial(residual_kernel, chans - 1, picks), in_s...  7.87 us
    ppermute x4, starting transfers between devices, from_behind(): lax.ppermute(value, axis, [(source, source + steps) for source in range(l...  5.75 us
  transfers between devices with their start and end apart: 17, of which 11 were waited for; matrix products, arithmetic and copies ran while one was open for 0% of the time, Pallas kernels for 35%

profile of v2, /device:TPU:0, one launch (start us, length us, event | category | flops | bytes accessed | tf_op | source)
XLA Modules:
  0.0 119.0 jit_solution(3916320402753138294)
XLA Ops:
  0.6 0.6 stack.39.info_ref.ids_ref
  1.3 3.9 %residual.3 = (bf16[1,16,32,512]{3,2,1,0:T(8,128)(2,1)}, bf16[1,16,32,512]{3,2,1,0:T(8,128)(2,1)}) custom-call(s32[10]{0:T(128)} %stack.39.info_ref.ids_ref, bf16[32,4,16,512]{3,2,1,0:T(8,128)(2,1)} %frames_ref.5, bf16[32,4,16,512]{3,2,1,0:T(8,128)(2,1)} %prev_ref.3, s32[32,16,512]{2,1,0:T(8,128)} %valid_ref.5), custom_call_target="tpu_custom_call" | custom-call | bytes 10800000 | tf_op jit(solution)/shard_map/residual/pallas_call | solution.py:208
  5.2 0.0 copy-start
  5.2 0.0 copy-start.1
  5.3 4.0 %collective-permute-start.4 = (bf16[1,16,32,512]{3,2,1,0:T(8,128)(2,1)}, bf16[1,16,32,512]{3,2,1,0:T(8,128)(2,1)S(1)}, u32[]{:S(2)}, u32[]{:S(2)}) collective-permute-start(bf16[1,16,32,512]{3,2,1,0:T(8,128)(2,1)} %get-tuple-element.28.refs_2_), channel_id=1, source_target_pairs={{0,24},{8,16},{16,8},{24,0},{1,25},{9,17},{17,9},{25,1},{2,26},{10... | collective-permute-start | bytes 1572872 | tf_op jit(solution)/shard_map/ppermute | solution.py:40
  9.2 3.9 %residual.2 = (bf16[1,16,32,512]{3,2,1,0:T(8,128)(2,1)}, bf16[1,16,32,512]{3,2,1,0:T(8,128)(2,1)}) custom-call(s32[10]{0:T(128)} %stack.39.info_ref.ids_ref, bf16[32,4,16,512]{3,2,1,0:T(8,128)(2,1)} %frames_ref.5, bf16[32,4,16,512]{3,2,1,0:T(8,128)(2,1)} %prev_ref.3, s32[32,16,512]{2,1,0:T(8,128)} %valid_ref.5), custom_call_target="tpu_custom_call" | custom-call | bytes 10800000 | tf_op jit(solution)/shard_map/residual/pallas_call | solution.py:208
  13.2 0.6 collective-permute-start.2
  13.8 0.5 collective-permute-start.3
  14.3 0.1 fusion.order_ref
  14.5 0.0 copy-start.4
  14.5 1.0 copy-done.4
  15.5 1.0 copy-done.5
  16.6 2.2 %interleave.1 = (bf16[5,16,32,512]{3,2,1,0:T(8,128)(2,1)S(1)}, bf16[5,5,32,512]{3,2,1,0:T(8,128)(2,1)S(1)}, bf16[5,5,32,512]{3,2,1,0:T(8,128)(2,1)S(1)}) custom-call(bf16[32,4,16,512]{3,2,1,0:T(8,128)(2,1)S(1)} %copy-done, s32[32,16,512]{2,1,0:T(8,128)S(1)} %copy-done.1, bf16[512,512]{1,0:T(8,128)(2,1)S(1)} %fusion.order_ref, ...), custom_call_target="tpu_custom_call" | custom-call | bytes 11880000 | tf_op jit(solution)/shard_map/interleave/pallas_call | solution.py:247
  18.7 1.3 %collective-permute-start = (bf16[5,5,32,512]{3,2,1,0:T(8,128)(2,1)S(1)}, bf16[5,5,32,512]{3,2,1,0:T(8,128)(2,1)S(1)}, u32[]{:S(2)}, u32[]{:S(2)}) collective-permute-start(bf16[5,5,32,512]{3,2,1,0:T(8,128)(2,1)S(1)} %get-tuple-element.31), channel_id=1, source_target_pairs={{0,1},{1,2},{2,3},{3,4},{4,5},{5,6},{6,7},{8,9},{9,10},{10,11},{11... | collective-permute-start | bytes 2457608 | tf_op jit(solution)/shard_map/ppermute | solution.py:24
  20.1 1.3 %collective-permute-start.1 = (bf16[5,5,32,512]{3,2,1,0:T(8,128)(2,1)S(1)}, bf16[5,5,32,512]{3,2,1,0:T(8,128)(2,1)S(1)}, u32[]{:S(2)}, u32[]{:S(2)}) collective-permute-start(bf16[5,5,32,512]{3,2,1,0:T(8,128)(2,1)S(1)} %get-tuple-element.32), channel_id=1, source_target_pairs={{1,0},{2,1},{3,2},{4,3},{5,4},{6,5},{7,6},{9,8},{10,9},{11,10},{12... | collective-permute-start | bytes 2457608 | tf_op jit(solution)/shard_map/ppermute | solution.py:24
  21.4 0.8 collective-permute-done.4
  22.2 10.7 %collective-permute-done.2 = bf16[1,16,32,512]{3,2,1,0:T(8,128)(2,1)S(1)} collective-permute-done((bf16[1,16,32,512]{3,2,1,0:T(8,128)(2,1)}, bf16[1,16,32,512]{3,2,1,0:T(8,128)(2,1)S(1)}, u32[]{:S(2)}, u32[]{:S(2)}) %collective-permute-start.2) | collective-permute-done | bytes 524320 | tf_op jit(solution)/shard_map/ppermute | solution.py:40
  32.9 1.5 %gram.1 = (f32[128,128]{1,0:T(8,128)S(1)}, bf16[16,128,512]{2,1,0:T(8,128)(2,1)S(1)}, bf16[1,5,128,512]{3,2,1,0:T(8,128)(2,1)S(1)}, bf16[1,5,128,512]{3,2,1,0:T(8,128)(2,1)S(1)}) custom-call(s32[10]{0:T(128)S(1)} %copy-done.6, bf16[16,32,512]{2,1,0:T(8,128)(2,1)S(1)} %bitcast.11, bf16[16,32,512]{2,1,0:T(8,128)(2,1)S(1)} %bitcast.13, ...), custom_call_target="tpu_custom_call" | custom-call | bytes 5040000 | tf_op jit(solution)/shard_map/gram/pallas_call | solution.py:281
  34.4 2.4 %collective-permute-start.7 = (f32[128,128]{1,0:T(8,128)S(1)}, f32[128,128]{1,0:T(8,128)S(1)}, u32[]{:S(2)}, u32[]{:S(2)}) collective-permute-start(f32[128,128]{1,0:T(8,128)S(1)} %get-tuple-element.33), channel_id=1, source_target_pairs={{0,24},{8,16},{16,8},{24,0},{1,25},{9,17},{17,9},{25,1},{2,26},{10... | collective-permute-start | bytes 196616 | tf_op jit(solution)/shard_map/ppermute | solution.py:40
  36.8 0.6 collective-permute-start.6
  37.4 0.5 collective-permute-start.5
  37.9 1.7 %collective-permute-done.7 = f32[128,128]{1,0:T(8,128)S(1)} collective-permute-done((f32[128,128]{1,0:T(8,128)S(1)}, f32[128,128]{1,0:T(8,128)S(1)}, u32[]{:S(2)}, u32[]{:S(2)}) %collective-permute-start.7) | collective-permute-done | bytes 65568 | tf_op jit(solution)/shard_map/ppermute | solution.py:40
  39.6 1.4 %collective-permute-done.6 = f32[128,128]{1,0:T(8,128)S(1)} collective-permute-done((f32[128,128]{1,0:T(8,128)S(1)}, f32[128,128]{1,0:T(8,128)S(1)}, u32[]{:S(2)}, u32[]{:S(2)}) %collective-permute-start.6) | collective-permute-done | bytes 65568 | tf_op jit(solution)/shard_map/ppermute | solution.py:40
  41.0 0.6 collective-permute-done.5
  41.7 0.0 copy-start.7
  41.7 0.0 collective-permute-done.1.refs_2_
  41.7 0.1 collective-permute-start.8
  41.8 1.2 %collective-permute-done.8 = f32[128,128]{1,0:T(8,128)S(1)} collective-permute-done((f32[128,128]{1,0:T(8,128)S(1)}, f32[128,128]{1,0:T(8,128)S(1)}, u32[]{:S(2)}, u32[]{:S(2)}) %collective-permute-start.8) | collective-permute-done | bytes 65568 | tf_op jit(solution)/shard_map/ppermute | solution.py:40
  43.0 3.7 %collective-permute-start.11 = (f32[128,128]{1,0:T(8,128)S(1)}, f32[128,128]{1,0:T(8,128)S(1)}, u32[]{:S(2)}, u32[]{:S(2)}) collective-permute-start(f32[128,128]{1,0:T(8,128)S(1)} %add.54), channel_id=1, source_target_pairs={{0,6},{1,7},{2,4},{3,5},{4,2},{5,3},{6,0},{7,1},{8,14},{9,15},{10,... | collective-permute-start | bytes 196616 | tf_op jit(solution)/shard_map/ppermute | solution.py:40
  46.7 0.0 collective-permute-start.10
  46.7 0.8 collective-permute-start.9
  47.5 1.9 %collective-permute-done.11 = f32[128,128]{1,0:T(8,128)S(1)} collective-permute-done((f32[128,128]{1,0:T(8,128)S(1)}, f32[128,128]{1,0:T(8,128)S(1)}, u32[]{:S(2)}, u32[]{:S(2)}) %collective-permute-start.11) | collective-permute-done | bytes 65568 | tf_op jit(solution)/shard_map/ppermute | solution.py:40
  49.4 3.2 %collective-permute-done.10 = f32[128,128]{1,0:T(8,128)S(1)} collective-permute-done((f32[128,128]{1,0:T(8,128)S(1)}, f32[128,128]{1,0:T(8,128)S(1)}, u32[]{:S(2)}, u32[]{:S(2)}) %collective-permute-start.10) | collective-permute-done | bytes 65568 | tf_op jit(solution)/shard_map/ppermute | solution.py:40
  52.6 0.0 copy-start.8
  52.7 1.6 %collective-permute-start.12 = (bf16[1,5,128,512]{3,2,1,0:T(8,128)(2,1)S(1)}, bf16[1,5,128,512]{3,2,1,0:T(8,128)(2,1)S(1)}, u32[]{:S(2)}, u32[]{:S(2)}) collective-permute-start(bf16[1,5,128,512]{3,2,1,0:T(8,128)(2,1)S(1)} %gate.5), channel_id=1, source_target_pairs={{0,1},{1,2},{2,3},{3,4},{4,5},{5,6},{6,7},{8,9},{9,10},{10,11},{11... | collective-permute-start | bytes 1966088 | tf_op jit(solution)/shard_map/ppermute | solution.py:24
  54.3 1.5 %collective-permute-start.13 = (bf16[1,5,128,512]{3,2,1,0:T(8,128)(2,1)S(1)}, bf16[1,5,128,512]{3,2,1,0:T(8,128)(2,1)S(1)}, u32[]{:S(2)}, u32[]{:S(2)}) collective-permute-start(bf16[1,5,128,512]{3,2,1,0:T(8,128)(2,1)S(1)} %gate.6), channel_id=1, source_target_pairs={{1,0},{2,1},{3,2},{4,3},{5,4},{6,5},{7,6},{9,8},{10,9},{11,10},{12... | collective-permute-start | bytes 1966088 | tf_op jit(solution)/shard_map/ppermute | solution.py:24
  55.8 9.2 %mixing.1.mixing_ref = bf16[128,128]{1,0:T(8,128)(2,1)S(1)} custom-call(f32[128,128]{1,0:T(8,128)S(1)} %add_add_fusion.gram_ref.refs_1_, f32[64,128]{1,0:T(8,128)S(1)} %bitcast.15), custom_call_target="tpu_custom_call" | custom-call | bytes 38160000 | tf_op jit(solution)/shard_map/mixing/pallas_call | solution.py:134
  65.0 1.6 %spread.1 = (bf16[1,26,32,512]{3,2,1,0:T(8,128)(2,1)S(1)}, bf16[1,26,32,512]{3,2,1,0:T(8,128)(2,1)S(1)}, bf16[1,26,32,512]{3,2,1,0:T(8,128)(2,1)S(1)}, bf16[1,26,32,512]{3,2,1,0:T(8,128)(2,1)S(1)}) custom-call(s32[10]{0:T(128)S(1)} %copy-done.6, bf16[128,128]{1,0:T(8,128)(2,1)S(1)} %mixing.1.mixing_ref, bf16[16,128,512]{2,1,0:T(8,128)(2,1)S(1)} %get-tuple-element.34.all_ref, ...), custom_call_target="tpu_custom_call" | custom-call | bytes 9000000 | tf_op jit(solution)/shard_map/spread/pallas_call | solution.py:323
  66.6 0.6 collective-permute-start.14
  67.2 1.4 %collective-permute-start.15 = (bf16[1,26,32,512]{3,2,1,0:T(8,128)(2,1)S(1)}, bf16[1,26,32,512]{3,2,1,0:T(8,128)(2,1)S(1)}, u32[]{:S(2)}, u32[]{:S(2)}) collective-permute-start(bf16[1,26,32,512]{3,2,1,0:T(8,128)(2,1)S(1)} %get-tuple-element.41), channel_id=1, source_target_pairs={{0,16},{8,24},{16,0},{24,8},{1,17},{9,25},{17,1},{25,9},{2,18},{10... | collective-permute-start | bytes 2555912 | tf_op jit(solution)/shard_map/ppermute | solution.py:40
  68.6 8.0 %variation.4 = (bf16[32,4,16,512]{3,2,1,0:T(8,128)(2,1)}, bf16[32,4,16,512]{3,2,1,0:T(8,128)(2,1)}, f32[8,128]{1,0:T(8,128)S(1)}) custom-call(s32[10]{0:T(128)S(1)} %copy-done.6, f32[4]{0:T(128)S(1)} %copy-done.8, bf16[512,512]{1,0:T(8,128)(2,1)S(1)} %fusion.order_ref, bf16[5,16,32,512]{3,2,1,0:T(8,128)(2,1)S(1)} %get-tuple-element.30.refs_0_, ...), custom_call_target="tpu_custom_call" | custom-call | bytes 30600000 | tf_op jit(solution)/shard_map/variation/pallas_call | solution.py:466
  76.6 10.0 %collective-permute-done.14.refs_2_.refs_3_ = bf16[1,26,32,512]{3,2,1,0:T(8,128)(2,1)S(1)} collective-permute-done((bf16[1,26,32,512]{3,2,1,0:T(8,128)(2,1)S(1)}, bf16[1,26,32,512]{3,2,1,0:T(8,128)(2,1)S(1)}, u32[]{:S(2)}, u32[]{:S(2)}) %collective-permute-start.14) | collective-permute-done | bytes 852000 | tf_op jit(solution)/shard_map/ppermute | solution.py:40
  86.7 0.8 collective-permute-done.15.refs_3_
  87.5 2.3 %collective-permute-start.16 = (bf16[1,26,32,512]{3,2,1,0:T(8,128)(2,1)S(1)}, bf16[1,26,32,512]{3,2,1,0:T(8,128)(2,1)S(1)}, u32[]{:S(2)}, u32[]{:S(2)}) collective-permute-start(bf16[1,26,32,512]{3,2,1,0:T(8,128)(2,1)S(1)} %gate.7), channel_id=1, source_target_pairs={{0,24},{8,16},{16,8},{24,0},{1,25},{9,17},{17,9},{25,1},{2,26},{10... | collective-permute-start | bytes 2555912 | tf_op jit(solution)/shard_map/ppermute | solution.py:40
  89.8 8.4 %variation.5 = (bf16[32,4,16,512]{3,2,1,0:T(8,128)(2,1)}, bf16[32,4,16,512]{3,2,1,0:T(8,128)(2,1)}, f32[8,128]{1,0:T(8,128)}) custom-call(s32[10]{0:T(128)S(1)} %copy-done.6, f32[4]{0:T(128)S(1)} %copy-done.8, bf16[512,512]{1,0:T(8,128)(2,1)S(1)} %fusion.order_ref, ...), custom_call_target="tpu_custom_call", output_to_operand_aliasing={{0}: (7, {}), {1}: (8, {})} | custom-call | bytes 30600000 | tf_op jit(solution)/shard_map/variation/pallas_call | solution.py:466
  98.2 8.4 %variation.6 = (bf16[32,4,16,512]{3,2,1,0:T(8,128)(2,1)}, bf16[32,4,16,512]{3,2,1,0:T(8,128)(2,1)}, f32[8,128]{1,0:T(8,128)}) custom-call(s32[10]{0:T(128)S(1)} %copy-done.6, f32[4]{0:T(128)S(1)} %copy-done.8, bf16[512,512]{1,0:T(8,128)(2,1)S(1)} %fusion.order_ref, ...), custom_call_target="tpu_custom_call", output_to_operand_aliasing={{0}: (7, {}), {1}: (8, {})} | custom-call | bytes 30600000 | tf_op jit(solution)/shard_map/variation/pallas_call | solution.py:466
  106.6 3.4 %collective-permute-done.16.refs_3_ = bf16[1,26,32,512]{3,2,1,0:T(8,128)(2,1)S(1)} collective-permute-done((bf16[1,26,32,512]{3,2,1,0:T(8,128)(2,1)S(1)}, bf16[1,26,32,512]{3,2,1,0:T(8,128)(2,1)S(1)}, u32[]{:S(2)}, u32[]{:S(2)}) %collective-permute-start.16) | collective-permute-done | bytes 852000 | tf_op jit(solution)/shard_map/ppermute | solution.py:40
  110.0 8.8 %variation.7 = (bf16[32,4,16,512]{3,2,1,0:T(8,128)(2,1)}, bf16[32,4,16,512]{3,2,1,0:T(8,128)(2,1)}, f32[8,128]{1,0:T(8,128)}) custom-call(s32[10]{0:T(128)S(1)} %copy-done.6, f32[4]{0:T(128)S(1)} %copy-done.8, bf16[512,512]{1,0:T(8,128)(2,1)S(1)} %fusion.order_ref, ...), custom_call_target="tpu_custom_call", output_to_operand_aliasing={{0}: (7, {}), {1}: (8, {})} | custom-call | bytes 30600000 | tf_op jit(solution)/shard_map/variation/pallas_call | solution.py:466
  (26 shorter events, 0.1 us)
Async XLA Ops:
  5.2 9.2 %copy-start = (bf16[32,4,16,512]{3,2,1,0:T(8,128)(2,1)S(1)}, bf16[32,4,16,512]{3,2,1,0:T(8,128)(2,1)}, u32[]{:S(2)}) copy-start(bf16[32,4,16,512]{3,2,1,0:T(8,128)(2,1)} %frames_ref.5) | copy-start | bytes 6291460
  5.2 9.2 %copy-start.1 = (s32[32,16,512]{2,1,0:T(8,128)S(1)}, s32[32,16,512]{2,1,0:T(8,128)}, u32[]{:S(2)}) copy-start(s32[32,16,512]{2,1,0:T(8,128)} %valid_ref.5) | copy-start | bytes 3145732
  5.2 9.2 %copy-start.2 = (bf16[1,16,32,512]{3,2,1,0:T(8,128)(2,1)S(1)}, bf16[1,16,32,512]{3,2,1,0:T(8,128)(2,1)}, u32[]{:S(2)}) copy-start(bf16[1,16,32,512]{3,2,1,0:T(8,128)(2,1)} %get-tuple-element.29.refs_3_) | copy-start | bytes 1572868
  5.2 9.2 %copy-start.3 = (bf16[1,16,32,512]{3,2,1,0:T(8,128)(2,1)S(1)}, bf16[1,16,32,512]{3,2,1,0:T(8,128)(2,1)}, u32[]{:S(2)}) copy-start(bf16[1,16,32,512]{3,2,1,0:T(8,128)(2,1)} %get-tuple-element.28.refs_2_) | copy-start | bytes 1572868
  5.3 17.0 %collective-permute-start.4 = (bf16[1,16,32,512]{3,2,1,0:T(8,128)(2,1)}, bf16[1,16,32,512]{3,2,1,0:T(8,128)(2,1)S(1)}, u32[]{:S(2)}, u32[]{:S(2)}) collective-permute-start(bf16[1,16,32,512]{3,2,1,0:T(8,128)(2,1)} %get-tuple-element.28.refs_2_), channel_id=1, source_target_pairs={{0,24},{8,16},{16,8},{24,0},{1,25},{9,17},{17,9},{25,1},{2,26},{10... | collective-permute-start | bytes 1572872 | tf_op jit(solution)/shard_map/ppermute | solution.py:40
  13.2 19.7 %collective-permute-start.2 = (bf16[1,16,32,512]{3,2,1,0:T(8,128)(2,1)}, bf16[1,16,32,512]{3,2,1,0:T(8,128)(2,1)S(1)}, u32[]{:S(2)}, u32[]{:S(2)}) collective-permute-start(bf16[1,16,32,512]{3,2,1,0:T(8,128)(2,1)} %get-tuple-element.26.refs_0_), channel_id=1, source_target_pairs={{0,8},{8,0},{16,24},{24,16},{1,9},{9,1},{17,25},{25,17},{2,10},{10... | collective-permute-start | bytes 1572872 | tf_op jit(solution)/shard_map/ppermute | solution.py:40
  13.8 19.1 %collective-permute-start.3 = (bf16[1,16,32,512]{3,2,1,0:T(8,128)(2,1)}, bf16[1,16,32,512]{3,2,1,0:T(8,128)(2,1)S(1)}, u32[]{:S(2)}, u32[]{:S(2)}) collective-permute-start(bf16[1,16,32,512]{3,2,1,0:T(8,128)(2,1)} %get-tuple-element.27.refs_1_), channel_id=1, source_target_pairs={{0,16},{8,24},{16,0},{24,8},{1,17},{9,25},{17,1},{25,9},{2,18},{10... | collective-permute-start | bytes 1572872 | tf_op jit(solution)/shard_map/ppermute | solution.py:40
  14.5 1.0 copy-start.4
  15.5 1.0 copy-start.5
  16.6 16.3 %copy-start.6 = (s32[10]{0:T(128)S(1)}, s32[10]{0:T(128)}, u32[]{:S(2)}) copy-start(s32[10]{0:T(128)} %stack.39.info_ref.ids_ref) | copy-start | bytes 124
  18.7 22.9 %collective-permute-start = (bf16[5,5,32,512]{3,2,1,0:T(8,128)(2,1)S(1)}, bf16[5,5,32,512]{3,2,1,0:T(8,128)(2,1)S(1)}, u32[]{:S(2)}, u32[]{:S(2)}) collective-permute-start(bf16[5,5,32,512]{3,2,1,0:T(8,128)(2,1)S(1)} %get-tuple-element.31), channel_id=1, source_target_pairs={{0,1},{1,2},{2,3},{3,4},{4,5},{5,6},{6,7},{8,9},{9,10},{10,11},{11... | collective-permute-start | bytes 2457608 | tf_op jit(solution)/shard_map/ppermute | solution.py:24
  20.1 21.6 %collective-permute-start.1 = (bf16[5,5,32,512]{3,2,1,0:T(8,128)(2,1)S(1)}, bf16[5,5,32,512]{3,2,1,0:T(8,128)(2,1)S(1)}, u32[]{:S(2)}, u32[]{:S(2)}) collective-permute-start(bf16[5,5,32,512]{3,2,1,0:T(8,128)(2,1)S(1)} %get-tuple-element.32), channel_id=1, source_target_pairs={{1,0},{2,1},{3,2},{4,3},{5,4},{6,5},{7,6},{9,8},{10,9},{11,10},{12... | collective-permute-start | bytes 2457608 | tf_op jit(solution)/shard_map/ppermute | solution.py:24
  34.4 5.3 %collective-permute-start.7 = (f32[128,128]{1,0:T(8,128)S(1)}, f32[128,128]{1,0:T(8,128)S(1)}, u32[]{:S(2)}, u32[]{:S(2)}) collective-permute-start(f32[128,128]{1,0:T(8,128)S(1)} %get-tuple-element.33), channel_id=1, source_target_pairs={{0,24},{8,16},{16,8},{24,0},{1,25},{9,17},{17,9},{25,1},{2,26},{10... | collective-permute-start | bytes 196616 | tf_op jit(solution)/shard_map/ppermute | solution.py:40
  36.8 4.3 %collective-permute-start.6 = (f32[128,128]{1,0:T(8,128)S(1)}, f32[128,128]{1,0:T(8,128)S(1)}, u32[]{:S(2)}, u32[]{:S(2)}) collective-permute-start(f32[128,128]{1,0:T(8,128)S(1)} %get-tuple-element.33), channel_id=1, source_target_pairs={{0,16},{8,24},{16,0},{24,8},{1,17},{9,25},{17,1},{25,9},{2,18},{10... | collective-permute-start | bytes 196616 | tf_op jit(solution)/shard_map/ppermute | solution.py:40
  37.4 4.3 %collective-permute-start.5 = (f32[128,128]{1,0:T(8,128)S(1)}, f32[128,128]{1,0:T(8,128)S(1)}, u32[]{:S(2)}, u32[]{:S(2)}) collective-permute-start(f32[128,128]{1,0:T(8,128)S(1)} %get-tuple-element.33), channel_id=1, source_target_pairs={{0,8},{8,0},{16,24},{24,16},{1,9},{9,1},{17,25},{25,17},{2,10},{10... | collective-permute-start | bytes 196616 | tf_op jit(solution)/shard_map/ppermute | solution.py:40
  41.7 14.1 %copy-start.7 = (f32[128,64]{0,1:T(8,128)S(1)}, f32[128,64]{0,1:T(8,128)}, u32[]{:S(2)}) copy-start(f32[128,64]{0,1:T(8,128)} %param.8) | copy-start | bytes 98308
  41.7 1.3 %collective-permute-start.8 = (f32[128,128]{1,0:T(8,128)S(1)}, f32[128,128]{1,0:T(8,128)S(1)}, u32[]{:S(2)}, u32[]{:S(2)}) collective-permute-start(f32[128,128]{1,0:T(8,128)S(1)} %gate.4), channel_id=1, source_target_pairs={{0,1},{1,0},{2,3},{3,2},{4,5},{5,4},{6,7},{7,6},{8,9},{9,8},{10,11... | collective-permute-start | bytes 196616 | tf_op jit(solution)/shard_map/ppermute | solution.py:40
  43.0 6.3 %collective-permute-start.11 = (f32[128,128]{1,0:T(8,128)S(1)}, f32[128,128]{1,0:T(8,128)S(1)}, u32[]{:S(2)}, u32[]{:S(2)}) collective-permute-start(f32[128,128]{1,0:T(8,128)S(1)} %add.54), channel_id=1, source_target_pairs={{0,6},{1,7},{2,4},{3,5},{4,2},{5,3},{6,0},{7,1},{8,14},{9,15},{10,... | collective-permute-start | bytes 196616 | tf_op jit(solution)/shard_map/ppermute | solution.py:40
  46.7 5.9 %collective-permute-start.10 = (f32[128,128]{1,0:T(8,128)S(1)}, f32[128,128]{1,0:T(8,128)S(1)}, u32[]{:S(2)}, u32[]{:S(2)}) collective-permute-start(f32[128,128]{1,0:T(8,128)S(1)} %add.54), channel_id=1, source_target_pairs={{0,4},{1,5},{2,6},{3,7},{4,0},{5,1},{6,2},{7,3},{8,12},{9,13},{10,... | collective-permute-start | bytes 196616 | tf_op jit(solution)/shard_map/ppermute | solution.py:40
  46.7 5.9 %collective-permute-start.9 = (f32[128,128]{1,0:T(8,128)S(1)}, f32[128,128]{1,0:T(8,128)S(1)}, u32[]{:S(2)}, u32[]{:S(2)}) collective-permute-start(f32[128,128]{1,0:T(8,128)S(1)} %add.54), channel_id=1, source_target_pairs={{0,2},{1,3},{2,0},{3,1},{4,6},{5,7},{6,4},{7,5},{8,10},{9,11},{10,... | collective-permute-start | bytes 196616 | tf_op jit(solution)/shard_map/ppermute | solution.py:40
  52.6 16.0 %copy-start.8 = (f32[4]{0:T(128)S(1)}, f32[4]{0:T(128)}, u32[]{:S(2)}) copy-start(f32[4]{0:T(128)} %weight_ref.7) | copy-start | bytes 52
  52.7 12.3 %collective-permute-start.12 = (bf16[1,5,128,512]{3,2,1,0:T(8,128)(2,1)S(1)}, bf16[1,5,128,512]{3,2,1,0:T(8,128)(2,1)S(1)}, u32[]{:S(2)}, u32[]{:S(2)}) collective-permute-start(bf16[1,5,128,512]{3,2,1,0:T(8,128)(2,1)S(1)} %gate.5), channel_id=1, source_target_pairs={{0,1},{1,2},{2,3},{3,4},{4,5},{5,6},{6,7},{8,9},{9,10},{10,11},{11... | collective-permute-start | bytes 1966088 | tf_op jit(solution)/shard_map/ppermute | solution.py:24
  54.3 10.7 %collective-permute-start.13 = (bf16[1,5,128,512]{3,2,1,0:T(8,128)(2,1)S(1)}, bf16[1,5,128,512]{3,2,1,0:T(8,128)(2,1)S(1)}, u32[]{:S(2)}, u32[]{:S(2)}) collective-permute-start(bf16[1,5,128,512]{3,2,1,0:T(8,128)(2,1)S(1)} %gate.6), channel_id=1, source_target_pairs={{1,0},{2,1},{3,2},{4,3},{5,4},{6,5},{7,6},{9,8},{10,9},{11,10},{12... | collective-permute-start | bytes 1966088 | tf_op jit(solution)/shard_map/ppermute | solution.py:24
  66.6 20.1 %collective-permute-start.14 = (bf16[1,26,32,512]{3,2,1,0:T(8,128)(2,1)S(1)}, bf16[1,26,32,512]{3,2,1,0:T(8,128)(2,1)S(1)}, u32[]{:S(2)}, u32[]{:S(2)}) collective-permute-start(bf16[1,26,32,512]{3,2,1,0:T(8,128)(2,1)S(1)} %get-tuple-element.40), channel_id=1, source_target_pairs={{0,8},{8,0},{16,24},{24,16},{1,9},{9,1},{17,25},{25,17},{2,10},{10... | collective-permute-start | bytes 2555912 | tf_op jit(solution)/shard_map/ppermute | solution.py:40
  67.2 20.3 %collective-permute-start.15 = (bf16[1,26,32,512]{3,2,1,0:T(8,128)(2,1)S(1)}, bf16[1,26,32,512]{3,2,1,0:T(8,128)(2,1)S(1)}, u32[]{:S(2)}, u32[]{:S(2)}) collective-permute-start(bf16[1,26,32,512]{3,2,1,0:T(8,128)(2,1)S(1)} %get-tuple-element.41), channel_id=1, source_target_pairs={{0,16},{8,24},{16,0},{24,8},{1,17},{9,25},{17,1},{25,9},{2,18},{10... | collective-permute-start | bytes 2555912 | tf_op jit(solution)/shard_map/ppermute | solution.py:40
  87.5 22.5 %collective-permute-start.16 = (bf16[1,26,32,512]{3,2,1,0:T(8,128)(2,1)S(1)}, bf16[1,26,32,512]{3,2,1,0:T(8,128)(2,1)S(1)}, u32[]{:S(2)}, u32[]{:S(2)}) collective-permute-start(bf16[1,26,32,512]{3,2,1,0:T(8,128)(2,1)S(1)} %gate.7), channel_id=1, source_target_pairs={{0,24},{8,16},{16,8},{24,0},{1,25},{9,17},{17,9},{25,1},{2,26},{10... | collective-permute-start | bytes 2555912 | tf_op jit(solution)/shard_map/ppermute | solution.py:40

commit v3 on v2

--- a/solution.py
+++ b/solution.py
@@ -18,12 +18,6 @@
 MOST_BYTES = 58 * 1024 * 1024
 
 
-def from_behind(value, axis, steps):
-    count = lax.axis_size(axis)
-    leading, last = (max(0, -steps), min(count, count - steps))
-    return lax.ppermute(value, axis, [(source, source + steps) for source in range(leading, last)])
-
-
 def power_of_two(count):
     return count & (count - 1) == 0
 
@@ -32,6 +26,18 @@
     if power_of_two(count):
         return index ^ offset
     return (index + (count - offset if back else offset)) % count
+
+
+def pair_swap(value, axis, start):
+    count = lax.axis_size(axis)
+    pairs = []
+    for lower in range(start, count - 1, 2):
+        pairs += [(lower, lower + 1), (lower + 1, lower)]
+    return lax.ppermute(value, axis, pairs)
+
+
+def rims_swapped(rims):
+    return [pair_swap(rim, "pix", start) for start, rim in enumerate(rims)]
 
 
 def swap(value, axis, offset):
@@ -222,10 +228,10 @@
     )(info, frames, prev_fg, depth_valid)
 
 
-def interleave_kernel(frames_ref, valid_ref, order_ref, *refs):
-    out_ref, top_ref, bottom_ref = refs[-3:]
+def interleave_kernel(info_ref, frames_ref, valid_ref, order_ref, *refs):
+    out_ref, rims = refs[-3], refs[-2:]
+    odd = info_ref[info_ref.shape[0] - 1]
     count, chans, rows, cols = frames_ref.shape
-    edge = NSWEEP
     for c in range(chans + 1):
         for g in range(count // PACK):
             some = pl.ds(g * PACK, PACK)
@@ -238,15 +244,21 @@
                 turned = lines[:, LANE * j : LANE * (j + 1)].reshape(PACK, rows, LANE)
                 turned = jnp.swapaxes(turned, 0, 1).astype(jnp.bfloat16)
                 out_ref[c, :, some, tile(j)] = turned
-                top_ref[c, :, some, tile(j)] = turned[:edge]
-                bottom_ref[c, :, some, tile(j)] = turned[rows - edge :]
-
-
-def interleaved(frames, depth_valid, order, after):
+    write_rims(rims, odd, lambda h: out_ref[:, h], rows)
+
+
+def write_rims(rims, odd, read, rows, axis_rows=NSWEEP):
+    first = jnp.where(odd != 0, 0, rows - axis_rows)
+    for h in range(axis_rows):
+        rims[0][:, h] = read(first + h)
+        rims[1][:, h] = read(rows - axis_rows - first + h)
+
+
+def interleaved(info, frames, depth_valid, order, after):
     count, chans, rows, cols = frames.shape
     return pl.pallas_call(
         interleave_kernel,
-        in_specs=[vmem()] * 3 + [anywhere()] * len(after),
+        in_specs=[smem()] + [vmem()] * 3 + [anywhere()] * len(after),
         out_specs=[vmem()] * 3,
         out_shape=[
             jax.ShapeDtypeStruct((chans + 1, height, count, cols), jnp.bfloat16)
@@ -255,19 +267,20 @@
         compiler_params=room(),
         cost_estimate=cost(3.3),
         name="interleave",
-    )(frames, depth_valid, order, *after)
+    )(info, frames, depth_valid, order, *after)
 
 
 def gram_kernel(groups, each, nval, ids_ref, *refs):
-    blocks, (gram_ref, all_ref, top_ref, bottom_ref) = refs[:groups], refs[-4:]
+    blocks, (gram_ref, all_ref), rims = refs[:groups], refs[-4:-2], refs[-2:]
     lines, count, cols = blocks[0].shape
     for k, block in enumerate(blocks):
         start = pl.multiple_of(ids_ref[groups + k] * count, count)
         all_ref[:, pl.ds(start, count), :] = block[...]
     rows = lines // each
+    odd = ids_ref[ids_ref.shape[0] - 1]
     for c in range(each):
-        top_ref[c] = all_ref[c * rows : c * rows + NSWEEP]
-        bottom_ref[c] = all_ref[(c + 1) * rows - NSWEEP : (c + 1) * rows]
+        some = [rim.at[pl.ds(c, 1)] for rim in rims]
+        write_rims(some, odd, lambda h, c=c: all_ref[pl.ds(c * rows + h, 1)], rows)
     total = jnp.zeros(gram_ref.shape, jnp.float32)
     for r in range(lines):
         total = total + short_dot(all_ref[r], all_ref[r], 1, 1)
@@ -294,80 +307,92 @@
     )(ids, *blocks, *after)
 
 
-def spread_kernel(ids_ref, mixing_ref, all_ref, above_ref, below_ref, *refs):
-    pieces, weights = refs[:-1], refs[-1]
-    each, lines, count, cols = pieces[0].shape
+def spread_kernel(picks, ids_ref, mixing_ref, all_ref, *refs):
+    rims, pieces, weights = refs[:2], refs[2:-1], refs[-1]
+    odd = ids_ref[ids_ref.shape[0] - 1] != 0
+    each, lines, _, cols = pieces[0].shape
+    halves = len(pieces) // len(picks)
+    count = halves * PACK
     rows = lines - 2 * NSWEEP
-    for k in range(len(pieces)):
-        start = pl.multiple_of(ids_ref[k] * count, count)
+    for k, pick in enumerate(picks):
+        start = pl.multiple_of(ids_ref[pick] * count, count)
         weights[pl.ds(k * count, count), :] = mixing_ref[pl.ds(start, count), :]
     chosen = weights[...]
     for c in range(each):
         for at in range(lines):
-            if at < NSWEEP:
-                pixels = above_ref[c, at]
-            elif at < NSWEEP + rows:
-                pixels = all_ref[c * rows + at - NSWEEP]
+            h = at - NSWEEP
+            if h < 0:
+                pixels = jnp.where(odd, rims[0][c, at], rims[1][c, at])
+            elif h < rows:
+                pixels = all_ref[c * rows + h]
             else:
-                pixels = below_ref[c, at - NSWEEP - rows]
+                pixels = jnp.where(odd, rims[1][c, h - rows], rims[0][c, h - rows])
             back = short_dot(chosen, pixels, 1, 0).astype(jnp.bfloat16)
             for k, piece in enumerate(pieces):
-                piece[c, at] = back[k * count : (k + 1) * count]
-
-
-def spread(ids, mixing, pixels, above, below, groups):
+                piece[c, at] = back[k * PACK : (k + 1) * PACK]
+
+
+def spread(ids, mixing, pixels, rims, groups, picks):
     lines, every, cols = pixels.shape
-    each = above.shape[0]
+    each = rims[0].shape[0]
     count = every // groups
-    piece = jax.ShapeDtypeStruct((each, lines // each + 2 * NSWEEP, count, cols), jnp.bfloat16)
-    return pl.pallas_call(
-        spread_kernel,
+    halves = count // PACK
+    piece = jax.ShapeDtypeStruct((each, lines // each + 2 * NSWEEP, PACK, cols), jnp.bfloat16)
+    pieces = pl.pallas_call(
+        functools.partial(spread_kernel, picks),
         in_specs=[smem()] + [vmem()] * 4,
-        out_specs=[vmem()] * groups,
-        out_shape=[piece] * groups,
-        scratch_shapes=[pltpu.VMEM((every, every), jnp.bfloat16)],
+        out_specs=[vmem()] * len(picks) * halves,
+        out_shape=[piece] * len(picks) * halves,
+        scratch_shapes=[pltpu.VMEM((len(picks) * count, every), jnp.bfloat16)],
         compiler_params=room(),
-        cost_estimate=cost(2.5),
+        cost_estimate=cost(1.6),
         name="spread",
-    )(ids, mixing, pixels, above, below)
+    )(ids, mixing, pixels, *rims)
+    return [pieces[n * halves : (n + 1) * halves] for n in range(len(picks))]
 
 
 def gate_kernel(*refs):
     pass
 
 
-def gate(value, after):
+def gate(values, after):
+    count = len(values)
     return pl.pallas_call(
         gate_kernel,
-        in_specs=[anywhere()] * (1 + len(after)),
-        out_specs=anywhere(),
-        out_shape=jax.ShapeDtypeStruct(value.shape, value.dtype),
-        input_output_aliases={0: 0},
+        in_specs=[anywhere()] * (count + len(after)),
+        out_specs=[anywhere()] * count,
+        out_shape=[jax.ShapeDtypeStruct(value.shape, value.dtype) for value in values],
+        input_output_aliases={n: n for n in range(count)},
         compiler_params=room(),
         name="gate",
-    )(value, *after)
-
-
-def variation_kernel(pick, at, each, n_after, info_ref, weight_ref, order_ref, *refs):
-    own, above, below, back_ref = refs[:4]
-    fg_out, bg_out, token_ref, source, first, second, flat_fg, flat_bg, fg_held, bg_held, sems = refs[
-        4 + n_after :
+    )(*values, *after)
+
+
+def variation_kernel(units, at, n_outs, info_ref, weight_ref, order_ref, *refs):
+    n_back = len(units)
+    own, rims, backs = refs[0], refs[1:3], refs[3 : 3 + n_back]
+    fg_out, bg_out, token_ref, source, first, second, flat_fg, flat_bg, image_held, fg_held, bg_held, sems = refs[
+        3 + n_back + n_outs :
     ]
-    groups = (info_ref.shape[0] - 2) // 2
-    chan = info_ref[groups + pick] * each + at
+    groups = (info_ref.shape[0] - 3) // 2
+    odd = info_ref[2 * groups + 2] != 0
+    channels = [info_ref[groups + pick] * backs[0].shape[0] + at for pick, _ in units]
     edge = NSWEEP
     nf = PACK
     chans, rows, count, cols = own.shape
     chans -= 1
     tiles = cols // LANE
     lines = rows + 2 * edge
-    lam = weight_ref[chan]
     up_flag = info_ref[2 * groups].astype(jnp.float32)
     down_flag = info_ref[2 * groups + 1].astype(jnp.float32)
-    step = STEP_SIZE / lam
     end = lax.broadcasted_iota(jnp.int32, (nf, LANE), 1) == LANE - 1
-    strips = ((0, above), (edge, own), (edge + rows, below))
-    token_ref[...] = jnp.zeros_like(token_ref)
+
+    def frames_at(chan, h, some):
+        if h < 0:
+            return jnp.where(odd, rims[0][chan, h + edge, some, :], rims[1][chan, h + edge, some, :])
+        if h < rows:
+            return own[chan, h, some, :]
+        return jnp.where(odd, rims[1][chan, h - rows, some, :], rims[0][chan, h - rows, some, :])
 
     def load(ref, i):
         return [ref[i, :, tile(j)] for j in range(tiles)]
@@ -381,34 +406,39 @@
         image = load(source, i)
         return [image[j] - STEP_SIZE * div[j] for j in range(tiles)]
 
-    @pl.loop(0, count // nf)
-    def some_frames(g):
-        some = pl.ds(pl.multiple_of(g * nf, nf), nf)
-        copies = [
-            pltpu.make_async_copy(held.at[g], out.at[some, chan], sems.at[n, g])
-            for n, (held, out) in enumerate(((fg_held, fg_out), (bg_held, bg_out)))
-        ]
+    def copy_of(held, out, n, g, chan, start):
+        place = pl.ds(pl.multiple_of(start * nf, nf), nf)
+        return pltpu.make_async_copy(held.at[g], out.at[place, chan], sems.at[n, g])
+
+    for g, back in enumerate(backs):
         for h in range(rows):
             for j in range(tiles):
-                back = back_ref[at, edge + h, some, tile(j)].astype(jnp.float32)
-                flat_bg[j, pl.ds(h, nf, stride=rows), :] = back
+                line = back[at, edge + h, :, tile(j)].astype(jnp.float32)
+                flat_bg[j, pl.ds(h, nf, stride=rows), :] = line
         for j in range(tiles):
             bg_held[g, :, :, tile(j)] = flat_bg[j].astype(jnp.bfloat16).reshape(nf, rows, LANE)
-        copies[1].start()
-
-        moved = back_ref[at, :, some, :].reshape(lines * nf, cols)
-        moved = short_dot(moved, order_ref[...], 1, 0)
-        for start, frames in strips:
-            for h in range(frames.shape[1]):
-                image = frames[chan, h, some, :].astype(jnp.float32)
-                source[start + h] = (image - moved[(start + h) * nf : (start + h + 1) * nf]) * step
+        moved = short_dot(back[at].reshape(lines * nf, cols), order_ref[...], 1, 0)
+        for i in range(lines):
+            image_held[g, i] = moved[i * nf : (i + 1) * nf]
+        copy_of(bg_held, bg_out, 1, g, channels[g], units[g][1]).start()
+
+    @pl.loop(0, n_back)
+    def some_frames(g):
+        chan, start = channels[0], units[0][1]
+        for n in range(1, n_back):
+            chan = jnp.where(g == n, channels[n], chan)
+            start = jnp.where(g == n, units[n][1], start)
+        some = pl.ds(pl.multiple_of(start * nf, nf), nf)
+        lam = weight_ref[chan]
+        step = STEP_SIZE / lam
+        for i in range(lines):
+            image = frames_at(chan, i - edge, some).astype(jnp.float32)
+            source[i] = (image - image_held[g, i]) * step
 
         @pl.when(chan == chans - 1)
         def mask():
-            for start, frames in strips:
-                for h in range(frames.shape[1]):
-                    valid = frames[chans, h, some, :].astype(jnp.float32)
-                    source[start + h] = source[start + h] * valid
+            for i in range(lines):
+                source[i] = source[i] * frames_at(chans, i - edge, some).astype(jnp.float32)
 
         for sweep in range(NSWEEP):
             here = beside = None
@@ -449,23 +479,23 @@
         fg = jnp.concatenate([flat_fg[j].astype(jnp.bfloat16) for j in range(tiles)], axis=1)
         fg = short_dot(fg, order_ref[...], 1, 1).astype(jnp.bfloat16)
         fg_held[g] = fg.reshape(nf, rows, cols)
-        copies[0].start()
-
-    for g in range(count // nf):
-        for n, (held, out) in enumerate(((fg_held, fg_out), (bg_held, bg_out))):
-            pltpu.make_async_copy(held.at[g], out.at[pl.ds(g * nf, nf), chan], sems.at[n, g]).wait()
-
-
-def variation(info, weights, pick, at, order, own, above, below, back, outs, shape):
+        copy_of(fg_held, fg_out, 0, g, chan, start).start()
+
+    for g in range(n_back):
+        copy_of(fg_held, fg_out, 0, g, channels[g], units[g][1]).wait()
+        copy_of(bg_held, bg_out, 1, g, channels[g], units[g][1]).wait()
+
+
+def variation(info, weights, units, at, order, own, rims, backs, outs, shape):
     count, chans, rows, cols = shape
     lines = rows + 2 * NSWEEP
-    each = back.shape[0]
     flat = pltpu.VMEM((cols // LANE, PACK * rows, LANE), jnp.float32)
     field = pltpu.VMEM((lines, PACK, cols), jnp.float32)
-    held = pltpu.VMEM((count // PACK, PACK, rows, cols), jnp.bfloat16)
+    held = pltpu.VMEM((len(backs), PACK, rows, cols), jnp.bfloat16)
+    images = pltpu.VMEM((len(backs), lines, PACK, cols), jnp.float32)
     return pl.pallas_call(
-        functools.partial(variation_kernel, pick, at, each, len(outs)),
-        in_specs=[smem(), smem()] + [vmem()] * 5 + [anywhere()] * len(outs),
+        functools.partial(variation_kernel, units, at, len(outs)),
+        in_specs=[smem(), smem()] + [vmem()] * (4 + len(backs)) + [anywhere()] * len(outs),
         out_specs=[anywhere(), anywhere(), vmem()],
         out_shape=[jax.ShapeDtypeStruct(shape, jnp.bfloat16)] * 2
         + [jax.ShapeDtypeStruct((SUB, LANE), jnp.float32)],
@@ -475,15 +505,16 @@
             field,
             flat,
             flat,
+            images,
             held,
             held,
-            pltpu.SemaphoreType.DMA((2, count // PACK)),
+            pltpu.SemaphoreType.DMA((2, len(backs))),
         ],
-        input_output_aliases={7 + n: n for n in range(len(outs))},
-        compiler_params=room(field, field, field, flat, flat, held, held),
-        cost_estimate=cost(8.5),
+        input_output_aliases={6 + len(backs) + n: n for n in range(len(outs))},
+        compiler_params=room(field, field, field, flat, flat, images, held, held),
+        cost_estimate=cost(4.3 * len(backs)),
         name="variation",
-    )(info, weights, order, own, above, below, back, *outs)
+    )(info, weights, order, own, *rims, *backs, *outs)
 
 
 def body(frames, prev_fg, depth_valid, sketch, tv_weight):
@@ -496,7 +527,7 @@
     me, strip = lax.axis_index("frame"), lax.axis_index("pix")
     targets = [partner(me, k, groups) for k in range(groups)]
     sources = [partner(me, k, groups, back=True) for k in range(groups)]
-    ends = [strip > 0, strip < strips - 1]
+    ends = [strip > 0, strip < strips - 1, strip % 2]
     info = jnp.stack([jnp.asarray(one, jnp.int32) for one in targets + sources + ends])
     near = [k for k in range(1, groups) if power_of_two(k)]
     far = [k for k in range(1, groups) if not power_of_two(k)]
@@ -510,41 +541,42 @@
     places = lax.broadcasted_iota(jnp.int32, (cols, cols), 1)
     places = places % LANE * tiles + places // LANE
     order = (places == lax.broadcasted_iota(jnp.int32, (cols, cols), 0)).astype(jnp.bfloat16)
-    lined, top, bottom = interleaved(frames, depth_valid, order, tuple(resid.values()))
-    lined_above = from_behind(bottom, "pix", 1)
-    lined_below = from_behind(top, "pix", -1)
-
-    terms, pixels, top, bottom = gram_terms(info, blocks, each, nval, ())
-    gram = gate(all_sum(terms, "frame"), (lined_above, lined_below))
+    lined, *rims = interleaved(info, frames, depth_valid, order, tuple(resid.values()))
+    lined_rims = rims_swapped(rims)
+
+    terms, pixels, *rims = gram_terms(info, blocks, each, nval, ())
+    (gram,) = gate([all_sum(terms, "frame")], lined_rims)
     gram = all_sum(gram, "pix")
-    above = from_behind(gate(bottom, (gram,)), "pix", 1)
-    below = from_behind(gate(top, (gram,)), "pix", -1)
+    around = rims_swapped(gate(rims, [gram]))
     mixing = mixing_matrix(gram, sketch)
-    pieces = spread(info, mixing, pixels, above, below, groups)
-    arrived = {0: pieces[0]}
+    picks = [0] + near + far
+    pieces = dict(zip(picks, spread(info, mixing, pixels, around, groups, picks)))
+    halves = range(count // PACK)
+    arrived = {(0, g): pieces[0][g] for g in halves}
     for k in near:
-        arrived[k] = swap(pieces[k], "frame", k)
+        arrived[k, 0] = swap(pieces[k][0], "frame", k)
 
     outs = []
-    for k in [0] + near + far:
+
+    def work_on(units, outs):
+        parts = [arrived[unit] for unit in units]
         for c in range(each):
             *outs, token = variation(
-                info,
-                tv_weight,
-                k,
-                c,
-                order,
-                lined,
-                lined_above,
-                lined_below,
-                arrived[k],
-                outs,
-                frames.shape,
+                info, tv_weight, units, c, order, lined, lined_rims, parts, outs, frames.shape
             )
-        if k == 0:
-            for other in far:
-                held = gate(pieces[other], (token,) + tuple(arrived[one] for one in near))
-                arrived[other] = swap(held, "frame", other)
+        return outs, token
+
+    token = None
+    stages = [[(0, g) for g in halves]] + [[(k, g) for k in near] for g in halves]
+    stages += [[(k, g)] for k in far for g in halves]
+    sends = [[(k, g) for k in near] for g in halves[1:]] + [[(k, g) for k in far for g in halves]]
+    for n, stage in enumerate(stages):
+        outs, token = work_on(stage, outs)
+        following = sends[n] if n < len(sends) else []
+        there = list(arrived.values()) if n else []
+        for k, g in following:
+            (held,) = gate([pieces[k][g]], [token] + there)
+            arrived[k, g] = swap(held, "frame", k)
     foreground, background = outs
     return (background, foreground)
 

time: 119 us -> 116 us (0.975)
  waiting for transfers between devices: 35.8 us -> 31.9 us
  Pallas kernels: 55.8 us -> 57.6 us
    ppermute x4, starting transfers between devices: 5.75 us -> 1.74 us  [pair_swap(): return lax.ppermute(value, axis, pairs)]
    ppermute x13 -> x16, waiting for transfers between devices: 35.8 us -> 31.9 us  [swap(): return lax.ppermute(value, axis, pairs)]
    ppermute x13 -> x16, starting transfers between devices: 17.5 us -> 20.4 us  [swap(): return lax.ppermute(value, axis, pairs)]
    pallas_call x10 -> x13, Pallas kernels: 37.3 us -> 39.1 us  [the longest x5 34.9 us: variation(): pl.pallas_call(functools.partial(variation_kernel, units, at, len(outs)),...]
  transfers between devices with their start and end apart: 17 -> 20, of which waited for: 11 -> 12; matrix products, arithmetic and copies ran while one was open for 0% -> 0% of each run, Pallas kernels for 35% -> 40%
where the time goes in v3:
time: 116 us
  Pallas kernels  57.6 us (50%)
  waiting for transfers between devices  31.9 us (28%)
  starting transfers between devices  22.2 us (19%)
  local copies, waits for them, and re-layouts  2.7 us (2%)
  between operations  1.18 us (1%)
    pallas_call x5, Pallas kernels, variation(): pl.pallas_call(functools.partial(variation_kernel, units, at, len(outs)),...  34.9 us
    ppermute x16, waiting for transfers between devices, swap(): return lax.ppermute(value, axis, pairs)  31.9 us
    ppermute x16, starting transfers between devices, swap(): return lax.ppermute(value, axis, pairs)  20.4 us
    pallas_call x1, Pallas kernels, mixing_matrix(): pl.pallas_call(mixing_kernel, out_shape=jax.ShapeDtypeStruct(gram.shape,...  9.18 us
    pallas_call x2, Pallas kernels, residual(): pl.pallas_call(functools.partial(residual_kernel, chans - 1, picks), in_s...  7.91 us
    pallas_call x1, Pallas kernels, interleaved(): pl.pallas_call(interleave_kernel, in_specs=[smem()] + [vmem()] * 3 + [any...  2.56 us
  transfers between devices with their start and end apart: 20, of which 12 were waited for; matrix products, arithmetic and copies ran while one was open for 0% of the time, Pallas kernels for 40%

profile of v3, /device:TPU:0, one launch (start us, length us, event | category | flops | bytes accessed | tf_op | source)
XLA Modules:
  0.0 115.8 jit_solution(10167224294637208283)
XLA Ops:
  0.6 0.6 stack.43.info_ref.ids_ref
  1.2 4.0 %residual.3 = (bf16[1,16,32,512]{3,2,1,0:T(8,128)(2,1)}, bf16[1,16,32,512]{3,2,1,0:T(8,128)(2,1)}) custom-call(s32[11]{0:T(128)} %stack.43.info_ref.ids_ref, bf16[32,4,16,512]{3,2,1,0:T(8,128)(2,1)} %frames_ref.5, bf16[32,4,16,512]{3,2,1,0:T(8,128)(2,1)} %prev_ref.3, s32[32,16,512]{2,1,0:T(8,128)} %valid_ref.5), custom_call_target="tpu_custom_call" | custom-call | bytes 10800000 | tf_op jit(solution)/shard_map/residual/pallas_call | solution.py:214
  5.2 0.0 copy-start
  5.2 0.0 copy-start.1
  5.3 4.0 %collective-permute-start.4 = (bf16[1,16,32,512]{3,2,1,0:T(8,128)(2,1)}, bf16[1,16,32,512]{3,2,1,0:T(8,128)(2,1)S(1)}, u32[]{:S(2)}, u32[]{:S(2)}) collective-permute-start(bf16[1,16,32,512]{3,2,1,0:T(8,128)(2,1)} %get-tuple-element.37.refs_2_), channel_id=1, source_target_pairs={{0,24},{8,16},{16,8},{24,0},{1,25},{9,17},{17,9},{25,1},{2,26},{10... | collective-permute-start | bytes 1572872 | tf_op jit(solution)/shard_map/ppermute | solution.py:46
  9.2 3.9 %residual.2 = (bf16[1,16,32,512]{3,2,1,0:T(8,128)(2,1)}, bf16[1,16,32,512]{3,2,1,0:T(8,128)(2,1)}) custom-call(s32[11]{0:T(128)} %stack.43.info_ref.ids_ref, bf16[32,4,16,512]{3,2,1,0:T(8,128)(2,1)} %frames_ref.5, bf16[32,4,16,512]{3,2,1,0:T(8,128)(2,1)} %prev_ref.3, s32[32,16,512]{2,1,0:T(8,128)} %valid_ref.5), custom_call_target="tpu_custom_call" | custom-call | bytes 10800000 | tf_op jit(solution)/shard_map/residual/pallas_call | solution.py:214
  13.2 0.6 collective-permute-start.2
  13.8 0.5 collective-permute-start.3
  14.3 0.1 fusion.order_ref
  14.5 1.0 copy-done.4
  15.5 1.0 copy-done.5
  16.6 2.6 %interleave.1 = (bf16[5,16,32,512]{3,2,1,0:T(8,128)(2,1)S(1)}, bf16[5,5,32,512]{3,2,1,0:T(8,128)(2,1)S(1)}, bf16[5,5,32,512]{3,2,1,0:T(8,128)(2,1)S(1)}) custom-call(s32[11]{0:T(128)S(1)} %copy-done.6, bf16[32,4,16,512]{3,2,1,0:T(8,128)(2,1)S(1)} %copy-done, s32[32,16,512]{2,1,0:T(8,128)S(1)} %copy-done.1, bf16[512,512]{1,0:T(8,128)(2,1)S(1)} %fusion.order_ref, ...), custom_call_target="tpu_custom_call" | custom-call | bytes 11880000 | tf_op jit(solution)/shard_map/interleave/pallas_call | solution.py:259
  19.1 0.1 collective-permute-start
  19.2 0.7 collective-permute-start.1
  19.9 2.3 %collective-permute-done.4 = bf16[1,16,32,512]{3,2,1,0:T(8,128)(2,1)S(1)} collective-permute-done((bf16[1,16,32,512]{3,2,1,0:T(8,128)(2,1)}, bf16[1,16,32,512]{3,2,1,0:T(8,128)(2,1)S(1)}, u32[]{:S(2)}, u32[]{:S(2)}) %collective-permute-start.4) | collective-permute-done | bytes 524320 | tf_op jit(solution)/shard_map/ppermute | solution.py:46
  22.2 10.7 %collective-permute-done.2 = bf16[1,16,32,512]{3,2,1,0:T(8,128)(2,1)S(1)} collective-permute-done((bf16[1,16,32,512]{3,2,1,0:T(8,128)(2,1)}, bf16[1,16,32,512]{3,2,1,0:T(8,128)(2,1)S(1)}, u32[]{:S(2)}, u32[]{:S(2)}) %collective-permute-start.2) | collective-permute-done | bytes 524320 | tf_op jit(solution)/shard_map/ppermute | solution.py:46
  32.9 1.5 %gram.1 = (f32[128,128]{1,0:T(8,128)S(1)}, bf16[16,128,512]{2,1,0:T(8,128)(2,1)S(1)}, bf16[1,5,128,512]{3,2,1,0:T(8,128)(2,1)S(1)}, bf16[1,5,128,512]{3,2,1,0:T(8,128)(2,1)S(1)}) custom-call(s32[11]{0:T(128)S(1)} %copy-done.6, bf16[16,32,512]{2,1,0:T(8,128)(2,1)S(1)} %bitcast.12, bf16[16,32,512]{2,1,0:T(8,128)(2,1)S(1)} %bitcast.14, ...), custom_call_target="tpu_custom_call" | custom-call | bytes 5040000 | tf_op jit(solution)/shard_map/gram/pallas_call | solution.py:294
  34.4 2.4 %collective-permute-start.7 = (f32[128,128]{1,0:T(8,128)S(1)}, f32[128,128]{1,0:T(8,128)S(1)}, u32[]{:S(2)}, u32[]{:S(2)}) collective-permute-start(f32[128,128]{1,0:T(8,128)S(1)} %get-tuple-element.42), channel_id=1, source_target_pairs={{0,24},{8,16},{16,8},{24,0},{1,25},{9,17},{17,9},{25,1},{2,26},{10... | collective-permute-start | bytes 196616 | tf_op jit(solution)/shard_map/ppermute | solution.py:46
  36.8 0.6 collective-permute-start.6
  37.4 0.5 collective-permute-start.5
  37.9 1.7 %collective-permute-done.7 = f32[128,128]{1,0:T(8,128)S(1)} collective-permute-done((f32[128,128]{1,0:T(8,128)S(1)}, f32[128,128]{1,0:T(8,128)S(1)}, u32[]{:S(2)}, u32[]{:S(2)}) %collective-permute-start.7) | collective-permute-done | bytes 65568 | tf_op jit(solution)/shard_map/ppermute | solution.py:46
  39.7 1.4 %collective-permute-done.6 = f32[128,128]{1,0:T(8,128)S(1)} collective-permute-done((f32[128,128]{1,0:T(8,128)S(1)}, f32[128,128]{1,0:T(8,128)S(1)}, u32[]{:S(2)}, u32[]{:S(2)}) %collective-permute-start.6) | collective-permute-done | bytes 65568 | tf_op jit(solution)/shard_map/ppermute | solution.py:46
  41.0 0.6 collective-permute-done.5
  41.7 0.1 collective-permute-start.8
  41.8 1.2 %collective-permute-done.8 = f32[128,128]{1,0:T(8,128)S(1)} collective-permute-done((f32[128,128]{1,0:T(8,128)S(1)}, f32[128,128]{1,0:T(8,128)S(1)}, u32[]{:S(2)}, u32[]{:S(2)}) %collective-permute-start.8) | collective-permute-done | bytes 65568 | tf_op jit(solution)/shard_map/ppermute | solution.py:46
  43.0 3.7 %collective-permute-start.11 = (f32[128,128]{1,0:T(8,128)S(1)}, f32[128,128]{1,0:T(8,128)S(1)}, u32[]{:S(2)}, u32[]{:S(2)}) collective-permute-start(f32[128,128]{1,0:T(8,128)S(1)} %add.63), channel_id=1, source_target_pairs={{0,6},{1,7},{2,4},{3,5},{4,2},{5,3},{6,0},{7,1},{8,14},{9,15},{10,... | collective-permute-start | bytes 196616 | tf_op jit(solution)/shard_map/ppermute | solution.py:46
  46.7 0.8 collective-permute-start.9
  47.5 1.9 %collective-permute-done.11 = f32[128,128]{1,0:T(8,128)S(1)} collective-permute-done((f32[128,128]{1,0:T(8,128)S(1)}, f32[128,128]{1,0:T(8,128)S(1)}, u32[]{:S(2)}, u32[]{:S(2)}) %collective-permute-start.11) | collective-permute-done | bytes 65568 | tf_op jit(solution)/shard_map/ppermute | solution.py:46
  49.4 3.2 %collective-permute-done.10 = f32[128,128]{1,0:T(8,128)S(1)} collective-permute-done((f32[128,128]{1,0:T(8,128)S(1)}, f32[128,128]{1,0:T(8,128)S(1)}, u32[]{:S(2)}, u32[]{:S(2)}) %collective-permute-start.10) | collective-permute-done | bytes 65568 | tf_op jit(solution)/shard_map/ppermute | solution.py:46
  52.6 0.1 collective-permute-start.12
  52.7 0.9 collective-permute-start.13
  53.6 9.2 %mixing.1.mixing_ref = bf16[128,128]{1,0:T(8,128)(2,1)S(1)} custom-call(f32[128,128]{1,0:T(8,128)S(1)} %add_add_fusion.gram_ref.refs_2_, f32[64,128]{1,0:T(8,128)S(1)} %bitcast.16), custom_call_target="tpu_custom_call" | custom-call | bytes 38160000 | tf_op jit(solution)/shard_map/mixing/pallas_call | solution.py:140
  62.8 1.6 %spread.1 = (bf16[1,26,16,512]{3,2,1,0:T(8,128)(2,1)S(1)}, bf16[1,26,16,512]{3,2,1,0:T(8,128)(2,1)S(1)}, bf16[1,26,16,512]{3,2,1,0:T(8,128)(2,1)S(1)}, bf16[1,26...) custom-call(s32[11]{0:T(128)S(1)} %copy-done.6, ...), custom_call_target="tpu_custom_call" | custom-call | bytes 5760000 | tf_op jit(solution)/shard_map/spread/pallas_call | solution.py:341
  64.4 0.6 collective-permute-start.14
  65.0 1.4 %collective-permute-start.15 = (bf16[1,26,16,512]{3,2,1,0:T(8,128)(2,1)S(1)}, bf16[1,26,16,512]{3,2,1,0:T(8,128)(2,1)S(1)}, u32[]{:S(2)}, u32[]{:S(2)}) collective-permute-start(bf16[1,26,16,512]{3,2,1,0:T(8,128)(2,1)S(1)} %get-tuple-element.50), channel_id=1, source_target_pairs={{0,16},{8,24},{16,0},{24,8},{1,17},{9,25},{17,1},{25,9},{2,18},{10... | collective-permute-start | bytes 1277960 | tf_op jit(solution)/shard_map/ppermute | solution.py:46
  66.5 8.0 %variation.5 = (bf16[32,4,16,512]{3,2,1,0:T(8,128)(2,1)}, bf16[32,4,16,512]{3,2,1,0:T(8,128)(2,1)}, f32[8,128]{1,0:T(8,128)S(1)}) custom-call(s32[11]{0:T(128)S(1)} %copy-done.6, f32[4]{0:T(128)S(1)} %copy-done.8, bf16[512,512]{1,0:T(8,128)(2,1)S(1)} %fusion.order_ref, bf16[5,16,32,512]{3,2,1,0:T(8,128)(2,1)S(1)} %get-tuple-element.39.refs_0_, ...), custom_call_target="tpu_custom_call" | custom-call | bytes 30960000 | tf_op jit(solution)/shard_map/variation/pallas_call | solution.py:496
  74.5 1.6 %collective-permute-start.16 = (bf16[1,26,16,512]{3,2,1,0:T(8,128)(2,1)S(1)}, bf16[1,26,16,512]{3,2,1,0:T(8,128)(2,1)S(1)}, u32[]{:S(2)}, u32[]{:S(2)}) collective-permute-start(bf16[1,26,16,512]{3,2,1,0:T(8,128)(2,1)S(1)} %gate.8), channel_id=1, source_target_pairs={{0,8},{8,0},{16,24},{24,16},{1,9},{9,1},{17,25},{25,17},{2,10},{10... | collective-permute-start | bytes 1277960 | tf_op jit(solution)/shard_map/ppermute | solution.py:46
  76.1 0.8 collective-permute-start.17
  76.9 7.8 %variation.6 = (bf16[32,4,16,512]{3,2,1,0:T(8,128)(2,1)}, bf16[32,4,16,512]{3,2,1,0:T(8,128)(2,1)}, f32[8,128]{1,0:T(8,128)S(1)}) custom-call(s32[11]{0:T(128)S(1)} %copy-done.6, f32[4]{0:T(128)S(1)} %copy-done.8, bf16[512,512]{1,0:T(8,128)(2,1)S(1)} %fusion.order_ref, ...), custom_call_target="tpu_custom_call", output_to_operand_aliasing={{0}: (8, {}), {1}: (9, {})} | custom-call | bytes 30960000 | tf_op jit(solution)/shard_map/variation/pallas_call | solution.py:496
  84.7 1.7 %collective-permute-done.16.refs_6_.refs_3_ = bf16[1,26,16,512]{3,2,1,0:T(8,128)(2,1)S(1)} collective-permute-done((bf16[1,26,16,512]{3,2,1,0:T(8,128)(2,1)S(1)}, bf16[1,26,16,512]{3,2,1,0:T(8,128)(2,1)S(1)}, u32[]{:S(2)}, u32[]{:S(2)}) %collective-permute-start.16) | collective-permute-done | bytes 426016 | tf_op jit(solution)/shard_map/ppermute | solution.py:46
  86.4 1.8 %collective-permute-done.17.refs_7_.refs_4_ = bf16[1,26,16,512]{3,2,1,0:T(8,128)(2,1)S(1)} collective-permute-done((bf16[1,26,16,512]{3,2,1,0:T(8,128)(2,1)S(1)}, bf16[1,26,16,512]{3,2,1,0:T(8,128)(2,1)S(1)}, u32[]{:S(2)}, u32[]{:S(2)}) %collective-permute-start.17) | collective-permute-done | bytes 426016 | tf_op jit(solution)/shard_map/ppermute | solution.py:46
  88.2 0.6 collective-permute-start.19
  88.8 2.3 %collective-permute-start.18 = (bf16[1,26,16,512]{3,2,1,0:T(8,128)(2,1)S(1)}, bf16[1,26,16,512]{3,2,1,0:T(8,128)(2,1)S(1)}, u32[]{:S(2)}, u32[]{:S(2)}) collective-permute-start(bf16[1,26,16,512]{3,2,1,0:T(8,128)(2,1)S(1)} %gate.10), channel_id=1, source_target_pairs={{0,24},{8,16},{16,8},{24,0},{1,25},{9,17},{17,9},{25,1},{2,26},{10... | collective-permute-start | bytes 1277960 | tf_op jit(solution)/shard_map/ppermute | solution.py:46
  91.1 8.4 %variation.7 = (bf16[32,4,16,512]{3,2,1,0:T(8,128)(2,1)}, bf16[32,4,16,512]{3,2,1,0:T(8,128)(2,1)}, f32[8,128]{1,0:T(8,128)}) custom-call(s32[11]{0:T(128)S(1)} %copy-done.6, f32[4]{0:T(128)S(1)} %copy-done.8, bf16[512,512]{1,0:T(8,128)(2,1)S(1)} %fusion.order_ref, ...), custom_call_target="tpu_custom_call", output_to_operand_aliasing={{0}: (8, {}), {1}: (9, {})} | custom-call | bytes 30960000 | tf_op jit(solution)/shard_map/variation/pallas_call | solution.py:496
  99.5 2.2 %collective-permute-done.19.refs_3_ = bf16[1,26,16,512]{3,2,1,0:T(8,128)(2,1)S(1)} collective-permute-done((bf16[1,26,16,512]{3,2,1,0:T(8,128)(2,1)S(1)}, bf16[1,26,16,512]{3,2,1,0:T(8,128)(2,1)S(1)}, u32[]{:S(2)}, u32[]{:S(2)}) %collective-permute-start.19) | collective-permute-done | bytes 426016 | tf_op jit(solution)/shard_map/ppermute | solution.py:46
  101.7 5.5 %variation.8 = (bf16[32,4,16,512]{3,2,1,0:T(8,128)(2,1)}, bf16[32,4,16,512]{3,2,1,0:T(8,128)(2,1)}, f32[8,128]{1,0:T(8,128)}) custom-call(s32[11]{0:T(128)S(1)} %copy-done.6, f32[4]{0:T(128)S(1)} %copy-done.8, bf16[512,512]{1,0:T(8,128)(2,1)S(1)} %fusion.order_ref, ...), custom_call_target="tpu_custom_call", output_to_operand_aliasing={{0}: (7, {}), {1}: (8, {})} | custom-call | bytes 15480000 | tf_op jit(solution)/shard_map/variation/pallas_call | solution.py:496
  107.2 3.2 %collective-permute-done.18.refs_3_ = bf16[1,26,16,512]{3,2,1,0:T(8,128)(2,1)S(1)} collective-permute-done((bf16[1,26,16,512]{3,2,1,0:T(8,128)(2,1)S(1)}, bf16[1,26,16,512]{3,2,1,0:T(8,128)(2,1)S(1)}, u32[]{:S(2)}, u32[]{:S(2)}) %collective-permute-start.18) | collective-permute-done | bytes 426016 | tf_op jit(solution)/shard_map/ppermute | solution.py:46
  110.4 5.2 %variation.9 = (bf16[32,4,16,512]{3,2,1,0:T(8,128)(2,1)}, bf16[32,4,16,512]{3,2,1,0:T(8,128)(2,1)}, f32[8,128]{1,0:T(8,128)}) custom-call(s32[11]{0:T(128)S(1)} %copy-done.6, f32[4]{0:T(128)S(1)} %copy-done.8, bf16[512,512]{1,0:T(8,128)(2,1)S(1)} %fusion.order_ref, ...), custom_call_target="tpu_custom_call", output_to_operand_aliasing={{0}: (7, {}), {1}: (8, {})} | custom-call | bytes 15480000 | tf_op jit(solution)/shard_map/variation/pallas_call | solution.py:496
  (35 shorter events, 0.1 us)
Async XLA Ops:
  5.2 9.2 %copy-start = (bf16[32,4,16,512]{3,2,1,0:T(8,128)(2,1)S(1)}, bf16[32,4,16,512]{3,2,1,0:T(8,128)(2,1)}, u32[]{:S(2)}) copy-start(bf16[32,4,16,512]{3,2,1,0:T(8,128)(2,1)} %frames_ref.5) | copy-start | bytes 6291460
  5.2 9.2 %copy-start.1 = (s32[32,16,512]{2,1,0:T(8,128)S(1)}, s32[32,16,512]{2,1,0:T(8,128)}, u32[]{:S(2)}) copy-start(s32[32,16,512]{2,1,0:T(8,128)} %valid_ref.5) | copy-start | bytes 3145732
  5.2 9.2 %copy-start.2 = (bf16[1,16,32,512]{3,2,1,0:T(8,128)(2,1)S(1)}, bf16[1,16,32,512]{3,2,1,0:T(8,128)(2,1)}, u32[]{:S(2)}) copy-start(bf16[1,16,32,512]{3,2,1,0:T(8,128)(2,1)} %get-tuple-element.38.refs_3_) | copy-start | bytes 1572868
  5.2 9.2 %copy-start.3 = (bf16[1,16,32,512]{3,2,1,0:T(8,128)(2,1)S(1)}, bf16[1,16,32,512]{3,2,1,0:T(8,128)(2,1)}, u32[]{:S(2)}) copy-start(bf16[1,16,32,512]{3,2,1,0:T(8,128)(2,1)} %get-tuple-element.37.refs_2_) | copy-start | bytes 1572868
  5.3 9.2 %copy-start.6 = (s32[11]{0:T(128)S(1)}, s32[11]{0:T(128)}, u32[]{:S(2)}) copy-start(s32[11]{0:T(128)} %stack.43.info_ref.ids_ref) | copy-start | bytes 136
  5.3 17.0 %collective-permute-start.4 = (bf16[1,16,32,512]{3,2,1,0:T(8,128)(2,1)}, bf16[1,16,32,512]{3,2,1,0:T(8,128)(2,1)S(1)}, u32[]{:S(2)}, u32[]{:S(2)}) collective-permute-start(bf16[1,16,32,512]{3,2,1,0:T(8,128)(2,1)} %get-tuple-element.37.refs_2_), channel_id=1, source_target_pairs={{0,24},{8,16},{16,8},{24,0},{1,25},{9,17},{17,9},{25,1},{2,26},{10... | collective-permute-start | bytes 1572872 | tf_op jit(solution)/shard_map/ppermute | solution.py:46
  13.2 19.7 %collective-permute-start.2 = (bf16[1,16,32,512]{3,2,1,0:T(8,128)(2,1)}, bf16[1,16,32,512]{3,2,1,0:T(8,128)(2,1)S(1)}, u32[]{:S(2)}, u32[]{:S(2)}) collective-permute-start(bf16[1,16,32,512]{3,2,1,0:T(8,128)(2,1)} %get-tuple-element.35.refs_0_), channel_id=1, source_target_pairs={{0,8},{8,0},{16,24},{24,16},{1,9},{9,1},{17,25},{25,17},{2,10},{10... | collective-permute-start | bytes 1572872 | tf_op jit(solution)/shard_map/ppermute | solution.py:46
  13.8 19.1 %collective-permute-start.3 = (bf16[1,16,32,512]{3,2,1,0:T(8,128)(2,1)}, bf16[1,16,32,512]{3,2,1,0:T(8,128)(2,1)S(1)}, u32[]{:S(2)}, u32[]{:S(2)}) collective-permute-start(bf16[1,16,32,512]{3,2,1,0:T(8,128)(2,1)} %get-tuple-element.36.refs_1_), channel_id=1, source_target_pairs={{0,16},{8,24},{16,0},{24,8},{1,17},{9,25},{17,1},{25,9},{2,18},{10... | collective-permute-start | bytes 1572872 | tf_op jit(solution)/shard_map/ppermute | solution.py:46
  14.5 1.0 copy-start.4
  15.5 1.0 copy-start.5
  19.1 22.5 %collective-permute-start = (bf16[5,5,32,512]{3,2,1,0:T(8,128)(2,1)S(1)}, bf16[5,5,32,512]{3,2,1,0:T(8,128)(2,1)S(1)}, u32[]{:S(2)}, u32[]{:S(2)}) collective-permute-start(bf16[5,5,32,512]{3,2,1,0:T(8,128)(2,1)S(1)} %get-tuple-element.40), channel_id=1, source_target_pairs={{0,1},{1,0},{2,3},{3,2},{4,5},{5,4},{6,7},{7,6},{8,9},{9,8},{10,11... | collective-permute-start | bytes 2457608 | tf_op jit(solution)/shard_map/ppermute | solution.py:36
  19.2 22.5 %collective-permute-start.1 = (bf16[5,5,32,512]{3,2,1,0:T(8,128)(2,1)S(1)}, bf16[5,5,32,512]{3,2,1,0:T(8,128)(2,1)S(1)}, u32[]{:S(2)}, u32[]{:S(2)}) collective-permute-start(bf16[5,5,32,512]{3,2,1,0:T(8,128)(2,1)S(1)} %get-tuple-element.41), channel_id=1, source_target_pairs={{1,2},{2,1},{3,4},{4,3},{5,6},{6,5},{9,10},{10,9},{11,12},{12,11},... | collective-permute-start | bytes 2457608 | tf_op jit(solution)/shard_map/ppermute | solution.py:36
  34.4 19.3 %copy-start.7 = (f32[128,64]{0,1:T(8,128)S(1)}, f32[128,64]{0,1:T(8,128)}, u32[]{:S(2)}) copy-start(f32[128,64]{0,1:T(8,128)} %param.8) | copy-start | bytes 98308
  34.4 5.3 %collective-permute-start.7 = (f32[128,128]{1,0:T(8,128)S(1)}, f32[128,128]{1,0:T(8,128)S(1)}, u32[]{:S(2)}, u32[]{:S(2)}) collective-permute-start(f32[128,128]{1,0:T(8,128)S(1)} %get-tuple-element.42), channel_id=1, source_target_pairs={{0,24},{8,16},{16,8},{24,0},{1,25},{9,17},{17,9},{25,1},{2,26},{10... | collective-permute-start | bytes 196616 | tf_op jit(solution)/shard_map/ppermute | solution.py:46
  36.8 4.3 %collective-permute-start.6 = (f32[128,128]{1,0:T(8,128)S(1)}, f32[128,128]{1,0:T(8,128)S(1)}, u32[]{:S(2)}, u32[]{:S(2)}) collective-permute-start(f32[128,128]{1,0:T(8,128)S(1)} %get-tuple-element.42), channel_id=1, source_target_pairs={{0,16},{8,24},{16,0},{24,8},{1,17},{9,25},{17,1},{25,9},{2,18},{10... | collective-permute-start | bytes 196616 | tf_op jit(solution)/shard_map/ppermute | solution.py:46
  37.4 4.3 %collective-permute-start.5 = (f32[128,128]{1,0:T(8,128)S(1)}, f32[128,128]{1,0:T(8,128)S(1)}, u32[]{:S(2)}, u32[]{:S(2)}) collective-permute-start(f32[128,128]{1,0:T(8,128)S(1)} %get-tuple-element.42), channel_id=1, source_target_pairs={{0,8},{8,0},{16,24},{24,16},{1,9},{9,1},{17,25},{25,17},{2,10},{10... | collective-permute-start | bytes 196616 | tf_op jit(solution)/shard_map/ppermute | solution.py:46
  41.7 1.3 %collective-permute-start.8 = (f32[128,128]{1,0:T(8,128)S(1)}, f32[128,128]{1,0:T(8,128)S(1)}, u32[]{:S(2)}, u32[]{:S(2)}) collective-permute-start(f32[128,128]{1,0:T(8,128)S(1)} %gate.6), channel_id=1, source_target_pairs={{0,1},{1,0},{2,3},{3,2},{4,5},{5,4},{6,7},{7,6},{8,9},{9,8},{10,11... | collective-permute-start | bytes 196616 | tf_op jit(solution)/shard_map/ppermute | solution.py:46
  43.0 6.3 %collective-permute-start.11 = (f32[128,128]{1,0:T(8,128)S(1)}, f32[128,128]{1,0:T(8,128)S(1)}, u32[]{:S(2)}, u32[]{:S(2)}) collective-permute-start(f32[128,128]{1,0:T(8,128)S(1)} %add.63), channel_id=1, source_target_pairs={{0,6},{1,7},{2,4},{3,5},{4,2},{5,3},{6,0},{7,1},{8,14},{9,15},{10,... | collective-permute-start | bytes 196616 | tf_op jit(solution)/shard_map/ppermute | solution.py:46
  46.7 5.9 %collective-permute-start.10 = (f32[128,128]{1,0:T(8,128)S(1)}, f32[128,128]{1,0:T(8,128)S(1)}, u32[]{:S(2)}, u32[]{:S(2)}) collective-permute-start(f32[128,128]{1,0:T(8,128)S(1)} %add.63), channel_id=1, source_target_pairs={{0,4},{1,5},{2,6},{3,7},{4,0},{5,1},{6,2},{7,3},{8,12},{9,13},{10,... | collective-permute-start | bytes 196616 | tf_op jit(solution)/shard_map/ppermute | solution.py:46
  46.7 5.9 %collective-permute-start.9 = (f32[128,128]{1,0:T(8,128)S(1)}, f32[128,128]{1,0:T(8,128)S(1)}, u32[]{:S(2)}, u32[]{:S(2)}) collective-permute-start(f32[128,128]{1,0:T(8,128)S(1)} %add.63), channel_id=1, source_target_pairs={{0,2},{1,3},{2,0},{3,1},{4,6},{5,7},{6,4},{7,5},{8,10},{9,11},{10,... | collective-permute-start | bytes 196616 | tf_op jit(solution)/shard_map/ppermute | solution.py:46
  52.6 13.8 %copy-start.8 = (f32[4]{0:T(128)S(1)}, f32[4]{0:T(128)}, u32[]{:S(2)}) copy-start(f32[4]{0:T(128)} %weight_ref.9) | copy-start | bytes 52
  52.6 10.2 %collective-permute-start.12 = (bf16[1,5,128,512]{3,2,1,0:T(8,128)(2,1)S(1)}, bf16[1,5,128,512]{3,2,1,0:T(8,128)(2,1)S(1)}, u32[]{:S(2)}, u32[]{:S(2)}) collective-permute-start(bf16[1,5,128,512]{3,2,1,0:T(8,128)(2,1)S(1)} %get-tuple-element.46), channel_id=1, source_target_pairs={{0,1},{1,0},{2,3},{3,2},{4,5},{5,4},{6,7},{7,6},{8,9},{9,8},{10,11... | collective-permute-start | bytes 1966088 | tf_op jit(solution)/shard_map/ppermute | solution.py:36
  52.7 10.1 %collective-permute-start.13 = (bf16[1,5,128,512]{3,2,1,0:T(8,128)(2,1)S(1)}, bf16[1,5,128,512]{3,2,1,0:T(8,128)(2,1)S(1)}, u32[]{:S(2)}, u32[]{:S(2)}) collective-permute-start(bf16[1,5,128,512]{3,2,1,0:T(8,128)(2,1)S(1)} %get-tuple-element.47), channel_id=1, source_target_pairs={{1,2},{2,1},{3,4},{4,3},{5,6},{6,5},{9,10},{10,9},{11,12},{12,11},... | collective-permute-start | bytes 1966088 | tf_op jit(solution)/shard_map/ppermute | solution.py:36
  64.4 12.4 %collective-permute-start.14 = (bf16[1,26,16,512]{3,2,1,0:T(8,128)(2,1)S(1)}, bf16[1,26,16,512]{3,2,1,0:T(8,128)(2,1)S(1)}, u32[]{:S(2)}, u32[]{:S(2)}) collective-permute-start(bf16[1,26,16,512]{3,2,1,0:T(8,128)(2,1)S(1)} %get-tuple-element.49), channel_id=1, source_target_pairs={{0,8},{8,0},{16,24},{24,16},{1,9},{9,1},{17,25},{25,17},{2,10},{10... | collective-permute-start | bytes 1277960 | tf_op jit(solution)/shard_map/ppermute | solution.py:46
  65.0 11.8 %collective-permute-start.15 = (bf16[1,26,16,512]{3,2,1,0:T(8,128)(2,1)S(1)}, bf16[1,26,16,512]{3,2,1,0:T(8,128)(2,1)S(1)}, u32[]{:S(2)}, u32[]{:S(2)}) collective-permute-start(bf16[1,26,16,512]{3,2,1,0:T(8,128)(2,1)S(1)} %get-tuple-element.50), channel_id=1, source_target_pairs={{0,16},{8,24},{16,0},{24,8},{1,17},{9,25},{17,1},{25,9},{2,18},{10... | collective-permute-start | bytes 1277960 | tf_op jit(solution)/shard_map/ppermute | solution.py:46
  74.5 11.9 %collective-permute-start.16 = (bf16[1,26,16,512]{3,2,1,0:T(8,128)(2,1)S(1)}, bf16[1,26,16,512]{3,2,1,0:T(8,128)(2,1)S(1)}, u32[]{:S(2)}, u32[]{:S(2)}) collective-permute-start(bf16[1,26,16,512]{3,2,1,0:T(8,128)(2,1)S(1)} %gate.8), channel_id=1, source_target_pairs={{0,8},{8,0},{16,24},{24,16},{1,9},{9,1},{17,25},{25,17},{2,10},{10... | collective-permute-start | bytes 1277960 | tf_op jit(solution)/shard_map/ppermute | solution.py:46
  76.1 12.1 %collective-permute-start.17 = (bf16[1,26,16,512]{3,2,1,0:T(8,128)(2,1)S(1)}, bf16[1,26,16,512]{3,2,1,0:T(8,128)(2,1)S(1)}, u32[]{:S(2)}, u32[]{:S(2)}) collective-permute-start(bf16[1,26,16,512]{3,2,1,0:T(8,128)(2,1)S(1)} %gate.9), channel_id=1, source_target_pairs={{0,16},{8,24},{16,0},{24,8},{1,17},{9,25},{17,1},{25,9},{2,18},{10... | collective-permute-start | bytes 1277960 | tf_op jit(solution)/shard_map/ppermute | solution.py:46
  88.2 13.5 %collective-permute-start.19 = (bf16[1,26,16,512]{3,2,1,0:T(8,128)(2,1)S(1)}, bf16[1,26,16,512]{3,2,1,0:T(8,128)(2,1)S(1)}, u32[]{:S(2)}, u32[]{:S(2)}) collective-permute-start(bf16[1,26,16,512]{3,2,1,0:T(8,128)(2,1)S(1)} %gate.11), channel_id=1, source_target_pairs={{0,24},{8,16},{16,8},{24,0},{1,25},{9,17},{17,9},{25,1},{2,26},{10... | collective-permute-start | bytes 1277960 | tf_op jit(solution)/shard_map/ppermute | solution.py:46
  88.8 21.6 %collective-permute-start.18 = (bf16[1,26,16,512]{3,2,1,0:T(8,128)(2,1)S(1)}, bf16[1,26,16,512]{3,2,1,0:T(8,128)(2,1)S(1)}, u32[]{:S(2)}, u32[]{:S(2)}) collective-permute-start(bf16[1,26,16,512]{3,2,1,0:T(8,128)(2,1)S(1)} %gate.10), channel_id=1, source_target_pairs={{0,24},{8,16},{16,8},{24,0},{1,25},{9,17},{17,9},{25,1},{2,26},{10... | collective-permute-start | bytes 1277960 | tf_op jit(solution)/shard_map/ppermute | solution.py:46

commit v4 on v3

--- a/solution.py
+++ b/solution.py
@@ -103,30 +103,77 @@
         below = range(k, blocks)
         cols = {b: [col_of(square[b], SUB * k + j) for j in range(SUB)] for b in below}
         pivots = jnp.ones((SUB, width), jnp.float32)
-        for j in range(SUB):
-            pivot = row_of(cols[k][j], j)
-            inverse = 1.0 / pivot
-            pivots = jnp.where(sub_ids == j, pivot, pivots)
-            col_rows = {i: row_of(cols[k][i], j) for i in range(j + 1, SUB)}
-            square_row = row_of(square[k], j)
-            side_rows = [row_of(side[k], j) for side in sides]
+        for j in range(0, SUB, 2):
+            col, after = cols[k][j], cols[k][j + 1]
+            corner, side_value, last = row_of(col, j), row_of(col, j + 1), row_of(after, j + 1)
+            inverse = 1.0 / corner
+            next_inverse = corner * (1.0 / (corner * last - side_value * side_value))
+            link = side_value * inverse
+            pivots = jnp.where(sub_ids == j, corner, pivots)
+            pivots = jnp.where(sub_ids == j + 1, last - side_value * link, pivots)
+
+            def two_rows(rows):
+                upper = row_of(rows, j)
+                return upper, row_of(rows, j + 1) - link * upper
+
+            top = row_of(after, j)
+            col_rows = {i: two_rows(cols[k][i]) for i in range(j + 2, SUB)}
+            square_rows = two_rows(square[k])
+            side_rows = [two_rows(side[k]) for side in sides]
             for b in below:
                 ratio = cols[b][j] * inverse
                 if b == k:
                     ratio = jnp.where(sub_ids > j, ratio, 0.0)
-                for i in range(j + 1, SUB):
-                    cols[b][i] = cols[b][i] - ratio * col_rows[i]
-                square[b] = square[b] - ratio * square_row
-                for side, side_row in zip(sides, side_rows):
-                    side[b] = side[b] - ratio * side_row
+                next_ratio = (cols[b][j + 1] - ratio * top) * next_inverse
+                if b == k:
+                    next_ratio = jnp.where(sub_ids > j + 1, next_ratio, 0.0)
+
+                def reduced(rows, pair):
+                    return rows - ratio * pair[0] - next_ratio * pair[1]
+
+                for i in range(j + 2, SUB):
+                    cols[b][i] = reduced(cols[b][i], col_rows[i])
+                square[b] = reduced(square[b], square_rows)
+                for side, pair in zip(sides, side_rows):
+                    side[b] = reduced(side[b], pair)
         scale = lax.rsqrt(pivots)
         for rows, side in zip(solved, sides):
             rows.append(side[k] * scale)
     return [jnp.concatenate(rows, axis=0) for rows in solved]
 
 
+def corner_masks(size):
+    shape = (size // 2, size)
+    rows = lax.broadcasted_iota(jnp.int32, shape, 0)
+    lanes = lax.broadcasted_iota(jnp.int32, shape, 1)
+    return lanes < size // 2, rows >= lanes, rows == lanes
+
+
+def packed(square):
+    size = square.shape[0]
+    left, lower, diagonal = corner_masks(size)
+    upper_half = square[: size // 2]
+    turned = pltpu.roll(square[size // 2 :], size // 2, 1)
+    rows = jnp.where(left & ~lower, turned, upper_half)
+    line = jnp.sum(jnp.where(left & diagonal, turned, 0.0), axis=0, keepdims=True)
+    return jnp.concatenate([rows, jnp.broadcast_to(line, (SUB, size))], axis=0)
+
+
+def unpacked(rows):
+    size = rows.shape[1]
+    half = size // 2
+    left, lower, diagonal = corner_masks(size)
+    line = rows[half : half + 1]
+    rows = rows[:half]
+    turned = jnp.concatenate([rows, jnp.zeros((half, size), jnp.float32)], axis=0).T
+    upper_half = jnp.where(left & ~lower, turned[:half], rows)
+    corner = jnp.where(diagonal, line, jnp.where(lower, turned[:half], rows))
+    lower_half = jnp.where(left, turned[half:], pltpu.roll(corner, half, 1))
+    return jnp.concatenate([upper_half, lower_half], axis=0)
+
+
 def mixing_kernel(gram_ref, sketch_ref, mixing_ref):
-    gram = gram_ref[...]
+    gram = unpacked(gram_ref[...])
     basis = sketch_ref[...]
     for turn in range(POWER):
         image = exact_dot(basis, gram, 1, 1)
@@ -139,7 +186,7 @@
 def mixing_matrix(gram, sketch):
     return pl.pallas_call(
         mixing_kernel,
-        out_shape=jax.ShapeDtypeStruct(gram.shape, jnp.bfloat16),
+        out_shape=jax.ShapeDtypeStruct(gram.shape[1:] * 2, jnp.bfloat16),
         compiler_params=room(),
         cost_estimate=cost(10.6),
         name="mixing",
@@ -281,10 +328,11 @@
     for c in range(each):
         some = [rim.at[pl.ds(c, 1)] for rim in rims]
         write_rims(some, odd, lambda h, c=c: all_ref[pl.ds(c * rows + h, 1)], rows)
-    total = jnp.zeros(gram_ref.shape, jnp.float32)
+    every = all_ref.shape[1]
+    total = jnp.zeros((every, every), jnp.float32)
     for r in range(lines):
         total = total + short_dot(all_ref[r], all_ref[r], 1, 1)
-    gram_ref[...] = total / nval
+    gram_ref[...] = packed(total / nval)
 
 
 def gram_terms(ids, blocks, each, nval, after):
@@ -296,7 +344,7 @@
         in_specs=[smem()] + [vmem()] * groups + [anywhere()] * len(after),
         out_specs=[vmem()] * 4,
         out_shape=[
-            jax.ShapeDtypeStruct((every, every), jnp.float32),
+            jax.ShapeDtypeStruct((every // 2 + SUB, every), jnp.float32),
             jax.ShapeDtypeStruct((lines, every, cols), jnp.bfloat16),
             jax.ShapeDtypeStruct((each, NSWEEP, every, cols), jnp.bfloat16),
             jax.ShapeDtypeStruct((each, NSWEEP, every, cols), jnp.bfloat16),
@@ -545,9 +593,9 @@
     lined_rims = rims_swapped(rims)
 
     terms, pixels, *rims = gram_terms(info, blocks, each, nval, ())
-    (gram,) = gate([all_sum(terms, "frame")], lined_rims)
-    gram = all_sum(gram, "pix")
-    around = rims_swapped(gate(rims, [gram]))
+    gram = all_sum(all_sum(terms, "frame"), "pix")
+    gram, *rims = gate([gram] + rims, lined_rims)
+    around = rims_swapped(rims)
     mixing = mixing_matrix(gram, sketch)
     picks = [0] + near + far
     pieces = dict(zip(picks, spread(info, mixing, pixels, around, groups, picks)))

time: 116 us -> 114 us (0.983)
  waiting for transfers between devices: 31.9 us -> 30.5 us
    ppermute x16, waiting for transfers between devices: 31.9 us -> 30.5 us  [swap(): return lax.ppermute(value, axis, pairs)]
  transfers between devices with their start and end apart: 20 -> 20, of which waited for: 12 -> 12; matrix products, arithmetic and copies ran while one was open for 0% -> 0% of each run, Pallas kernels for 40% -> 41%
where the time goes in v4:
time: 114 us
  Pallas kernels  57.5 us (50%)
  waiting for transfers between devices  30.5 us (27%)
  starting transfers between devices  22.1 us (19%)
  local copies, waits for them, and re-layouts  2.7 us (2%)
  between operations  1.15 us (1%)
    pallas_call x5, Pallas kernels, variation(): pl.pallas_call(functools.partial(variation_kernel, units, at, len(outs)),...  34.9 us
    ppermute x16, waiting for transfers between devices, swap(): return lax.ppermute(value, axis, pairs)  30.5 us
    ppermute x16, starting transfers between devices, swap(): return lax.ppermute(value, axis, pairs)  20.4 us
    pallas_call x1, Pallas kernels, mixing_matrix(): pl.pallas_call(mixing_kernel, out_shape=jax.ShapeDtypeStruct(gram.shape[1...  8.99 us
    pallas_call x2, Pallas kernels, residual(): pl.pallas_call(functools.partial(residual_kernel, chans - 1, picks), in_s...  7.91 us
    pallas_call x1, Pallas kernels, interleaved(): pl.pallas_call(interleave_kernel, in_specs=[smem()] + [vmem()] * 3 + [any...  2.56 us
  transfers between devices with their start and end apart: 20, of which 12 were waited for; matrix products, arithmetic and copies ran while one was open for 0% of the time, Pallas kernels for 41%

profile of v4, /device:TPU:0, one launch (start us, length us, event | category | flops | bytes accessed | tf_op | source)
XLA Modules:
  0.0 114.2 jit_solution(5237119597015158722)
XLA Ops:
  0.6 0.6 stack.43.info_ref.ids_ref
  1.2 4.0 %residual.3 = (bf16[1,16,32,512]{3,2,1,0:T(8,128)(2,1)}, bf16[1,16,32,512]{3,2,1,0:T(8,128)(2,1)}) custom-call(s32[11]{0:T(128)} %stack.43.info_ref.ids_ref, bf16[32,4,16,512]{3,2,1,0:T(8,128)(2,1)} %frames_ref.5, bf16[32,4,16,512]{3,2,1,0:T(8,128)(2,1)} %prev_ref.3, s32[32,16,512]{2,1,0:T(8,128)} %valid_ref.5), custom_call_target="tpu_custom_call" | custom-call | bytes 10800000 | tf_op jit(solution)/shard_map/residual/pallas_call | solution.py:261
  5.2 0.0 copy-start.1
  5.3 4.0 %collective-permute-start.4 = (bf16[1,16,32,512]{3,2,1,0:T(8,128)(2,1)}, bf16[1,16,32,512]{3,2,1,0:T(8,128)(2,1)S(1)}, u32[]{:S(2)}, u32[]{:S(2)}) collective-permute-start(bf16[1,16,32,512]{3,2,1,0:T(8,128)(2,1)} %get-tuple-element.38.refs_2_), channel_id=1, source_target_pairs={{0,24},{8,16},{16,8},{24,0},{1,25},{9,17},{17,9},{25,1},{2,26},{10... | collective-permute-start | bytes 1572872 | tf_op jit(solution)/shard_map/ppermute | solution.py:46
  9.2 3.9 %residual.2 = (bf16[1,16,32,512]{3,2,1,0:T(8,128)(2,1)}, bf16[1,16,32,512]{3,2,1,0:T(8,128)(2,1)}) custom-call(s32[11]{0:T(128)} %stack.43.info_ref.ids_ref, bf16[32,4,16,512]{3,2,1,0:T(8,128)(2,1)} %frames_ref.5, bf16[32,4,16,512]{3,2,1,0:T(8,128)(2,1)} %prev_ref.3, s32[32,16,512]{2,1,0:T(8,128)} %valid_ref.5), custom_call_target="tpu_custom_call" | custom-call | bytes 10800000 | tf_op jit(solution)/shard_map/residual/pallas_call | solution.py:261
  13.2 0.6 collective-permute-start.2
  13.8 0.5 collective-permute-start.3
  14.3 0.1 fusion.order_ref
  14.5 0.0 copy-start.4
  14.5 1.0 copy-done.4
  15.5 1.0 copy-done.5
  16.6 2.6 %interleave.1 = (bf16[5,16,32,512]{3,2,1,0:T(8,128)(2,1)S(1)}, bf16[5,5,32,512]{3,2,1,0:T(8,128)(2,1)S(1)}, bf16[5,5,32,512]{3,2,1,0:T(8,128)(2,1)S(1)}) custom-call(s32[11]{0:T(128)S(1)} %copy-done.6, bf16[32,4,16,512]{3,2,1,0:T(8,128)(2,1)S(1)} %copy-done, s32[32,16,512]{2,1,0:T(8,128)S(1)} %copy-done.1, bf16[512,512]{1,0:T(8,128)(2,1)S(1)} %fusion.order_ref, ...), custom_call_target="tpu_custom_call" | custom-call | bytes 11880000 | tf_op jit(solution)/shard_map/interleave/pallas_call | solution.py:306
  19.1 0.1 collective-permute-start
  19.2 0.7 collective-permute-start.1
  19.9 2.3 %collective-permute-done.4 = bf16[1,16,32,512]{3,2,1,0:T(8,128)(2,1)S(1)} collective-permute-done((bf16[1,16,32,512]{3,2,1,0:T(8,128)(2,1)}, bf16[1,16,32,512]{3,2,1,0:T(8,128)(2,1)S(1)}, u32[]{:S(2)}, u32[]{:S(2)}) %collective-permute-start.4) | collective-permute-done | bytes 524320 | tf_op jit(solution)/shard_map/ppermute | solution.py:46
  22.2 10.7 %collective-permute-done.2 = bf16[1,16,32,512]{3,2,1,0:T(8,128)(2,1)S(1)} collective-permute-done((bf16[1,16,32,512]{3,2,1,0:T(8,128)(2,1)}, bf16[1,16,32,512]{3,2,1,0:T(8,128)(2,1)S(1)}, u32[]{:S(2)}, u32[]{:S(2)}) %collective-permute-start.2) | collective-permute-done | bytes 524320 | tf_op jit(solution)/shard_map/ppermute | solution.py:46
  32.9 1.5 %gram.1 = (f32[72,128]{1,0:T(8,128)S(1)}, bf16[16,128,512]{2,1,0:T(8,128)(2,1)S(1)}, bf16[1,5,128,512]{3,2,1,0:T(8,128)(2,1)S(1)}, bf16[1,5,128,512]{3,2,1,0:T(8,128)(2,1)S(1)}) custom-call(s32[11]{0:T(128)S(1)} %copy-done.6, bf16[16,32,512]{2,1,0:T(8,128)(2,1)S(1)} %bitcast.12, bf16[16,32,512]{2,1,0:T(8,128)(2,1)S(1)} %bitcast.14, ...), custom_call_target="tpu_custom_call" | custom-call | bytes 5040000 | tf_op jit(solution)/shard_map/gram/pallas_call | solution.py:342
  34.4 2.4 %collective-permute-start.7 = (f32[72,128]{1,0:T(8,128)S(1)}, f32[72,128]{1,0:T(8,128)S(1)}, u32[]{:S(2)}, u32[]{:S(2)}) collective-permute-start(f32[72,128]{1,0:T(8,128)S(1)} %get-tuple-element.43), channel_id=1, source_target_pairs={{0,24},{8,16},{16,8},{24,0},{1,25},{9,17},{17,9},{25,1},{2,26},{10... | collective-permute-start | bytes 110600 | tf_op jit(solution)/shard_map/ppermute | solution.py:46
  36.9 0.6 collective-permute-start.6
  37.5 0.5 collective-permute-start.5
  38.0 1.4 %collective-permute-done.7 = f32[72,128]{1,0:T(8,128)S(1)} collective-permute-done((f32[72,128]{1,0:T(8,128)S(1)}, f32[72,128]{1,0:T(8,128)S(1)}, u32[]{:S(2)}, u32[]{:S(2)}) %collective-permute-start.7) | collective-permute-done | bytes 36896 | tf_op jit(solution)/shard_map/ppermute | solution.py:46
  39.4 1.4 %collective-permute-done.6 = f32[72,128]{1,0:T(8,128)S(1)} collective-permute-done((f32[72,128]{1,0:T(8,128)S(1)}, f32[72,128]{1,0:T(8,128)S(1)}, u32[]{:S(2)}, u32[]{:S(2)}) %collective-permute-start.6) | collective-permute-done | bytes 36896 | tf_op jit(solution)/shard_map/ppermute | solution.py:46
  40.8 0.6 collective-permute-done.5
  41.4 0.1 collective-permute-start.8
  41.5 1.2 %collective-permute-done.8 = f32[72,128]{1,0:T(8,128)S(1)} collective-permute-done((f32[72,128]{1,0:T(8,128)S(1)}, f32[72,128]{1,0:T(8,128)S(1)}, u32[]{:S(2)}, u32[]{:S(2)}) %collective-permute-start.8) | collective-permute-done | bytes 36896 | tf_op jit(solution)/shard_map/ppermute | solution.py:46
  42.7 3.6 %collective-permute-start.11 = (f32[72,128]{1,0:T(8,128)S(1)}, f32[72,128]{1,0:T(8,128)S(1)}, u32[]{:S(2)}, u32[]{:S(2)}) collective-permute-start(f32[72,128]{1,0:T(8,128)S(1)} %add.63), channel_id=1, source_target_pairs={{0,6},{1,7},{2,4},{3,5},{4,2},{5,3},{6,0},{7,1},{8,14},{9,15},{10,... | collective-permute-start | bytes 110600 | tf_op jit(solution)/shard_map/ppermute | solution.py:46
  46.3 0.8 collective-permute-start.9
  47.1 1.4 %collective-permute-done.11 = f32[72,128]{1,0:T(8,128)S(1)} collective-permute-done((f32[72,128]{1,0:T(8,128)S(1)}, f32[72,128]{1,0:T(8,128)S(1)}, u32[]{:S(2)}, u32[]{:S(2)}) %collective-permute-start.11) | collective-permute-done | bytes 36896 | tf_op jit(solution)/shard_map/ppermute | solution.py:46
  48.5 2.7 %collective-permute-done.10 = f32[72,128]{1,0:T(8,128)S(1)} collective-permute-done((f32[72,128]{1,0:T(8,128)S(1)}, f32[72,128]{1,0:T(8,128)S(1)}, u32[]{:S(2)}, u32[]{:S(2)}) %collective-permute-start.10) | collective-permute-done | bytes 36896 | tf_op jit(solution)/shard_map/ppermute | solution.py:46
  51.2 0.1 collective-permute-start.12
  51.3 0.9 collective-permute-start.13
  52.2 9.0 %mixing.1.mixing_ref = bf16[128,128]{1,0:T(8,128)(2,1)S(1)} custom-call(f32[72,128]{1,0:T(8,128)S(1)} %get-tuple-element.46.gram_ref, f32[64,128]{1,0:T(8,128)S(1)} %bitcast.16), custom_call_target="tpu_custom_call" | custom-call | bytes 38160000 | tf_op jit(solution)/shard_map/mixing/pallas_call | solution.py:187
  61.2 1.6 %spread.1 = (bf16[1,26,16,512]{3,2,1,0:T(8,128)(2,1)S(1)}, bf16[1,26,16,512]{3,2,1,0:T(8,128)(2,1)S(1)}, bf16[1,26,16,512]{3,2,1,0:T(8,128)(2,1)S(1)}, bf16[1,26...) custom-call(s32[11]{0:T(128)S(1)} %copy-done.6, ...), custom_call_target="tpu_custom_call" | custom-call | bytes 5760000 | tf_op jit(solution)/shard_map/spread/pallas_call | solution.py:389
  62.8 0.6 collective-permute-start.14
  63.4 1.4 %collective-permute-start.15 = (bf16[1,26,16,512]{3,2,1,0:T(8,128)(2,1)S(1)}, bf16[1,26,16,512]{3,2,1,0:T(8,128)(2,1)S(1)}, u32[]{:S(2)}, u32[]{:S(2)}) collective-permute-start(bf16[1,26,16,512]{3,2,1,0:T(8,128)(2,1)S(1)} %get-tuple-element.52), channel_id=1, source_target_pairs={{0,16},{8,24},{16,0},{24,8},{1,17},{9,25},{17,1},{25,9},{2,18},{10... | collective-permute-start | bytes 1277960 | tf_op jit(solution)/shard_map/ppermute | solution.py:46
  64.9 8.0 %variation.5 = (bf16[32,4,16,512]{3,2,1,0:T(8,128)(2,1)}, bf16[32,4,16,512]{3,2,1,0:T(8,128)(2,1)}, f32[8,128]{1,0:T(8,128)S(1)}) custom-call(s32[11]{0:T(128)S(1)} %copy-done.6, f32[4]{0:T(128)S(1)} %copy-done.8, bf16[512,512]{1,0:T(8,128)(2,1)S(1)} %fusion.order_ref, bf16[5,16,32,512]{3,2,1,0:T(8,128)(2,1)S(1)} %get-tuple-element.40.refs_0_, ...), custom_call_target="tpu_custom_call" | custom-call | bytes 30960000 | tf_op jit(solution)/shard_map/variation/pallas_call | solution.py:544
  72.9 1.6 %collective-permute-start.16 = (bf16[1,26,16,512]{3,2,1,0:T(8,128)(2,1)S(1)}, bf16[1,26,16,512]{3,2,1,0:T(8,128)(2,1)S(1)}, u32[]{:S(2)}, u32[]{:S(2)}) collective-permute-start(bf16[1,26,16,512]{3,2,1,0:T(8,128)(2,1)S(1)} %gate.6), channel_id=1, source_target_pairs={{0,8},{8,0},{16,24},{24,16},{1,9},{9,1},{17,25},{25,17},{2,10},{10... | collective-permute-start | bytes 1277960 | tf_op jit(solution)/shard_map/ppermute | solution.py:46
  74.5 0.8 collective-permute-start.17
  75.3 7.8 %variation.6 = (bf16[32,4,16,512]{3,2,1,0:T(8,128)(2,1)}, bf16[32,4,16,512]{3,2,1,0:T(8,128)(2,1)}, f32[8,128]{1,0:T(8,128)S(1)}) custom-call(s32[11]{0:T(128)S(1)} %copy-done.6, f32[4]{0:T(128)S(1)} %copy-done.8, bf16[512,512]{1,0:T(8,128)(2,1)S(1)} %fusion.order_ref, ...), custom_call_target="tpu_custom_call", output_to_operand_aliasing={{0}: (8, {}), {1}: (9, {})} | custom-call | bytes 30960000 | tf_op jit(solution)/shard_map/variation/pallas_call | solution.py:544
  83.1 1.6 %collective-permute-done.16.refs_6_.refs_3_ = bf16[1,26,16,512]{3,2,1,0:T(8,128)(2,1)S(1)} collective-permute-done((bf16[1,26,16,512]{3,2,1,0:T(8,128)(2,1)S(1)}, bf16[1,26,16,512]{3,2,1,0:T(8,128)(2,1)S(1)}, u32[]{:S(2)}, u32[]{:S(2)}) %collective-permute-start.16) | collective-permute-done | bytes 426016 | tf_op jit(solution)/shard_map/ppermute | solution.py:46
  84.8 1.8 %collective-permute-done.17.refs_7_.refs_4_ = bf16[1,26,16,512]{3,2,1,0:T(8,128)(2,1)S(1)} collective-permute-done((bf16[1,26,16,512]{3,2,1,0:T(8,128)(2,1)S(1)}, bf16[1,26,16,512]{3,2,1,0:T(8,128)(2,1)S(1)}, u32[]{:S(2)}, u32[]{:S(2)}) %collective-permute-start.17) | collective-permute-done | bytes 426016 | tf_op jit(solution)/shard_map/ppermute | solution.py:46
  86.6 0.6 collective-permute-start.19
  87.2 2.3 %collective-permute-start.18 = (bf16[1,26,16,512]{3,2,1,0:T(8,128)(2,1)S(1)}, bf16[1,26,16,512]{3,2,1,0:T(8,128)(2,1)S(1)}, u32[]{:S(2)}, u32[]{:S(2)}) collective-permute-start(bf16[1,26,16,512]{3,2,1,0:T(8,128)(2,1)S(1)} %gate.8), channel_id=1, source_target_pairs={{0,24},{8,16},{16,8},{24,0},{1,25},{9,17},{17,9},{25,1},{2,26},{10... | collective-permute-start | bytes 1277960 | tf_op jit(solution)/shard_map/ppermute | solution.py:46
  89.5 8.4 %variation.7 = (bf16[32,4,16,512]{3,2,1,0:T(8,128)(2,1)}, bf16[32,4,16,512]{3,2,1,0:T(8,128)(2,1)}, f32[8,128]{1,0:T(8,128)}) custom-call(s32[11]{0:T(128)S(1)} %copy-done.6, f32[4]{0:T(128)S(1)} %copy-done.8, bf16[512,512]{1,0:T(8,128)(2,1)S(1)} %fusion.order_ref, ...), custom_call_target="tpu_custom_call", output_to_operand_aliasing={{0}: (8, {}), {1}: (9, {})} | custom-call | bytes 30960000 | tf_op jit(solution)/shard_map/variation/pallas_call | solution.py:544
  97.9 2.2 %collective-permute-done.19.refs_3_ = bf16[1,26,16,512]{3,2,1,0:T(8,128)(2,1)S(1)} collective-permute-done((bf16[1,26,16,512]{3,2,1,0:T(8,128)(2,1)S(1)}, bf16[1,26,16,512]{3,2,1,0:T(8,128)(2,1)S(1)}, u32[]{:S(2)}, u32[]{:S(2)}) %collective-permute-start.19) | collective-permute-done | bytes 426016 | tf_op jit(solution)/shard_map/ppermute | solution.py:46
  100.1 5.5 %variation.8 = (bf16[32,4,16,512]{3,2,1,0:T(8,128)(2,1)}, bf16[32,4,16,512]{3,2,1,0:T(8,128)(2,1)}, f32[8,128]{1,0:T(8,128)}) custom-call(s32[11]{0:T(128)S(1)} %copy-done.6, f32[4]{0:T(128)S(1)} %copy-done.8, bf16[512,512]{1,0:T(8,128)(2,1)S(1)} %fusion.order_ref, ...), custom_call_target="tpu_custom_call", output_to_operand_aliasing={{0}: (7, {}), {1}: (8, {})} | custom-call | bytes 15480000 | tf_op jit(solution)/shard_map/variation/pallas_call | solution.py:544
  105.6 3.2 %collective-permute-done.18.refs_3_ = bf16[1,26,16,512]{3,2,1,0:T(8,128)(2,1)S(1)} collective-permute-done((bf16[1,26,16,512]{3,2,1,0:T(8,128)(2,1)S(1)}, bf16[1,26,16,512]{3,2,1,0:T(8,128)(2,1)S(1)}, u32[]{:S(2)}, u32[]{:S(2)}) %collective-permute-start.18) | collective-permute-done | bytes 426016 | tf_op jit(solution)/shard_map/ppermute | solution.py:46
  108.8 5.2 %variation.9 = (bf16[32,4,16,512]{3,2,1,0:T(8,128)(2,1)}, bf16[32,4,16,512]{3,2,1,0:T(8,128)(2,1)}, f32[8,128]{1,0:T(8,128)}) custom-call(s32[11]{0:T(128)S(1)} %copy-done.6, f32[4]{0:T(128)S(1)} %copy-done.8, bf16[512,512]{1,0:T(8,128)(2,1)S(1)} %fusion.order_ref, ...), custom_call_target="tpu_custom_call", output_to_operand_aliasing={{0}: (7, {}), {1}: (8, {})} | custom-call | bytes 15480000 | tf_op jit(solution)/shard_map/variation/pallas_call | solution.py:544
  (34 shorter events, 0.1 us)
Async XLA Ops:
  5.2 9.2 %copy-start = (bf16[32,4,16,512]{3,2,1,0:T(8,128)(2,1)S(1)}, bf16[32,4,16,512]{3,2,1,0:T(8,128)(2,1)}, u32[]{:S(2)}) copy-start(bf16[32,4,16,512]{3,2,1,0:T(8,128)(2,1)} %frames_ref.5) | copy-start | bytes 6291460
  5.2 9.2 %copy-start.1 = (s32[32,16,512]{2,1,0:T(8,128)S(1)}, s32[32,16,512]{2,1,0:T(8,128)}, u32[]{:S(2)}) copy-start(s32[32,16,512]{2,1,0:T(8,128)} %valid_ref.5) | copy-start | bytes 3145732
  5.2 9.2 %copy-start.2 = (bf16[1,16,32,512]{3,2,1,0:T(8,128)(2,1)S(1)}, bf16[1,16,32,512]{3,2,1,0:T(8,128)(2,1)}, u32[]{:S(2)}) copy-start(bf16[1,16,32,512]{3,2,1,0:T(8,128)(2,1)} %get-tuple-element.39.refs_3_) | copy-start | bytes 1572868
  5.2 9.2 %copy-start.3 = (bf16[1,16,32,512]{3,2,1,0:T(8,128)(2,1)S(1)}, bf16[1,16,32,512]{3,2,1,0:T(8,128)(2,1)}, u32[]{:S(2)}) copy-start(bf16[1,16,32,512]{3,2,1,0:T(8,128)(2,1)} %get-tuple-element.38.refs_2_) | copy-start | bytes 1572868
  5.3 9.2 %copy-start.6 = (s32[11]{0:T(128)S(1)}, s32[11]{0:T(128)}, u32[]{:S(2)}) copy-start(s32[11]{0:T(128)} %stack.43.info_ref.ids_ref) | copy-start | bytes 136
  5.3 17.0 %collective-permute-start.4 = (bf16[1,16,32,512]{3,2,1,0:T(8,128)(2,1)}, bf16[1,16,32,512]{3,2,1,0:T(8,128)(2,1)S(1)}, u32[]{:S(2)}, u32[]{:S(2)}) collective-permute-start(bf16[1,16,32,512]{3,2,1,0:T(8,128)(2,1)} %get-tuple-element.38.refs_2_), channel_id=1, source_target_pairs={{0,24},{8,16},{16,8},{24,0},{1,25},{9,17},{17,9},{25,1},{2,26},{10... | collective-permute-start | bytes 1572872 | tf_op jit(solution)/shard_map/ppermute | solution.py:46
  13.2 19.7 %collective-permute-start.2 = (bf16[1,16,32,512]{3,2,1,0:T(8,128)(2,1)}, bf16[1,16,32,512]{3,2,1,0:T(8,128)(2,1)S(1)}, u32[]{:S(2)}, u32[]{:S(2)}) collective-permute-start(bf16[1,16,32,512]{3,2,1,0:T(8,128)(2,1)} %get-tuple-element.36.refs_0_), channel_id=1, source_target_pairs={{0,8},{8,0},{16,24},{24,16},{1,9},{9,1},{17,25},{25,17},{2,10},{10... | collective-permute-start | bytes 1572872 | tf_op jit(solution)/shard_map/ppermute | solution.py:46
  13.8 19.1 %collective-permute-start.3 = (bf16[1,16,32,512]{3,2,1,0:T(8,128)(2,1)}, bf16[1,16,32,512]{3,2,1,0:T(8,128)(2,1)S(1)}, u32[]{:S(2)}, u32[]{:S(2)}) collective-permute-start(bf16[1,16,32,512]{3,2,1,0:T(8,128)(2,1)} %get-tuple-element.37.refs_1_), channel_id=1, source_target_pairs={{0,16},{8,24},{16,0},{24,8},{1,17},{9,25},{17,1},{25,9},{2,18},{10... | collective-permute-start | bytes 1572872 | tf_op jit(solution)/shard_map/ppermute | solution.py:46
  14.5 1.0 copy-start.4
  15.5 1.0 copy-start.5
  19.1 32.1 %collective-permute-start = (bf16[5,5,32,512]{3,2,1,0:T(8,128)(2,1)S(1)}, bf16[5,5,32,512]{3,2,1,0:T(8,128)(2,1)S(1)}, u32[]{:S(2)}, u32[]{:S(2)}) collective-permute-start(bf16[5,5,32,512]{3,2,1,0:T(8,128)(2,1)S(1)} %get-tuple-element.41), channel_id=1, source_target_pairs={{0,1},{1,0},{2,3},{3,2},{4,5},{5,4},{6,7},{7,6},{8,9},{9,8},{10,11... | collective-permute-start | bytes 2457608 | tf_op jit(solution)/shard_map/ppermute | solution.py:36
  19.2 32.0 %collective-permute-start.1 = (bf16[5,5,32,512]{3,2,1,0:T(8,128)(2,1)S(1)}, bf16[5,5,32,512]{3,2,1,0:T(8,128)(2,1)S(1)}, u32[]{:S(2)}, u32[]{:S(2)}) collective-permute-start(bf16[5,5,32,512]{3,2,1,0:T(8,128)(2,1)S(1)} %get-tuple-element.42), channel_id=1, source_target_pairs={{1,2},{2,1},{3,4},{4,3},{5,6},{6,5},{9,10},{10,9},{11,12},{12,11},... | collective-permute-start | bytes 2457608 | tf_op jit(solution)/shard_map/ppermute | solution.py:36
  34.4 17.8 %copy-start.7 = (f32[128,64]{0,1:T(8,128)S(1)}, f32[128,64]{0,1:T(8,128)}, u32[]{:S(2)}) copy-start(f32[128,64]{0,1:T(8,128)} %param.8) | copy-start | bytes 98308
  34.4 4.9 %collective-permute-start.7 = (f32[72,128]{1,0:T(8,128)S(1)}, f32[72,128]{1,0:T(8,128)S(1)}, u32[]{:S(2)}, u32[]{:S(2)}) collective-permute-start(f32[72,128]{1,0:T(8,128)S(1)} %get-tuple-element.43), channel_id=1, source_target_pairs={{0,24},{8,16},{16,8},{24,0},{1,25},{9,17},{17,9},{25,1},{2,26},{10... | collective-permute-start | bytes 110600 | tf_op jit(solution)/shard_map/ppermute | solution.py:46
  36.9 4.0 %collective-permute-start.6 = (f32[72,128]{1,0:T(8,128)S(1)}, f32[72,128]{1,0:T(8,128)S(1)}, u32[]{:S(2)}, u32[]{:S(2)}) collective-permute-start(f32[72,128]{1,0:T(8,128)S(1)} %get-tuple-element.43), channel_id=1, source_target_pairs={{0,16},{8,24},{16,0},{24,8},{1,17},{9,25},{17,1},{25,9},{2,18},{10... | collective-permute-start | bytes 110600 | tf_op jit(solution)/shard_map/ppermute | solution.py:46
  37.5 4.0 %collective-permute-start.5 = (f32[72,128]{1,0:T(8,128)S(1)}, f32[72,128]{1,0:T(8,128)S(1)}, u32[]{:S(2)}, u32[]{:S(2)}) collective-permute-start(f32[72,128]{1,0:T(8,128)S(1)} %get-tuple-element.43), channel_id=1, source_target_pairs={{0,8},{8,0},{16,24},{24,16},{1,9},{9,1},{17,25},{25,17},{2,10},{10... | collective-permute-start | bytes 110600 | tf_op jit(solution)/shard_map/ppermute | solution.py:46
  41.4 1.3 %collective-permute-start.8 = (f32[72,128]{1,0:T(8,128)S(1)}, f32[72,128]{1,0:T(8,128)S(1)}, u32[]{:S(2)}, u32[]{:S(2)}) collective-permute-start(f32[72,128]{1,0:T(8,128)S(1)} %add_add_fusion.1), channel_id=1, source_target_pairs={{0,1},{1,0},{2,3},{3,2},{4,5},{5,4},{6,7},{7,6},{8,9},{9,8},{10,11... | collective-permute-start | bytes 110600 | tf_op jit(solution)/shard_map/ppermute | solution.py:46
  42.7 5.8 %collective-permute-start.11 = (f32[72,128]{1,0:T(8,128)S(1)}, f32[72,128]{1,0:T(8,128)S(1)}, u32[]{:S(2)}, u32[]{:S(2)}) collective-permute-start(f32[72,128]{1,0:T(8,128)S(1)} %add.63), channel_id=1, source_target_pairs={{0,6},{1,7},{2,4},{3,5},{4,2},{5,3},{6,0},{7,1},{8,14},{9,15},{10,... | collective-permute-start | bytes 110600 | tf_op jit(solution)/shard_map/ppermute | solution.py:46
  46.3 4.9 %collective-permute-start.10 = (f32[72,128]{1,0:T(8,128)S(1)}, f32[72,128]{1,0:T(8,128)S(1)}, u32[]{:S(2)}, u32[]{:S(2)}) collective-permute-start(f32[72,128]{1,0:T(8,128)S(1)} %add.63), channel_id=1, source_target_pairs={{0,4},{1,5},{2,6},{3,7},{4,0},{5,1},{6,2},{7,3},{8,12},{9,13},{10,... | collective-permute-start | bytes 110600 | tf_op jit(solution)/shard_map/ppermute | solution.py:46
  46.3 4.9 %collective-permute-start.9 = (f32[72,128]{1,0:T(8,128)S(1)}, f32[72,128]{1,0:T(8,128)S(1)}, u32[]{:S(2)}, u32[]{:S(2)}) collective-permute-start(f32[72,128]{1,0:T(8,128)S(1)} %add.63), channel_id=1, source_target_pairs={{0,2},{1,3},{2,0},{3,1},{4,6},{5,7},{6,4},{7,5},{8,10},{9,11},{10,... | collective-permute-start | bytes 110600 | tf_op jit(solution)/shard_map/ppermute | solution.py:46
  51.2 13.6 %copy-start.8 = (f32[4]{0:T(128)S(1)}, f32[4]{0:T(128)}, u32[]{:S(2)}) copy-start(f32[4]{0:T(128)} %weight_ref.9) | copy-start | bytes 52
  51.2 10.0 %collective-permute-start.12 = (bf16[1,5,128,512]{3,2,1,0:T(8,128)(2,1)S(1)}, bf16[1,5,128,512]{3,2,1,0:T(8,128)(2,1)S(1)}, u32[]{:S(2)}, u32[]{:S(2)}) collective-permute-start(bf16[1,5,128,512]{3,2,1,0:T(8,128)(2,1)S(1)} %get-tuple-element.48), channel_id=1, source_target_pairs={{0,1},{1,0},{2,3},{3,2},{4,5},{5,4},{6,7},{7,6},{8,9},{9,8},{10,11... | collective-permute-start | bytes 1966088 | tf_op jit(solution)/shard_map/ppermute | solution.py:36
  51.3 9.9 %collective-permute-start.13 = (bf16[1,5,128,512]{3,2,1,0:T(8,128)(2,1)S(1)}, bf16[1,5,128,512]{3,2,1,0:T(8,128)(2,1)S(1)}, u32[]{:S(2)}, u32[]{:S(2)}) collective-permute-start(bf16[1,5,128,512]{3,2,1,0:T(8,128)(2,1)S(1)} %get-tuple-element.49), channel_id=1, source_target_pairs={{1,2},{2,1},{3,4},{4,3},{5,6},{6,5},{9,10},{10,9},{11,12},{12,11},... | collective-permute-start | bytes 1966088 | tf_op jit(solution)/shard_map/ppermute | solution.py:36
  62.8 12.4 %collective-permute-start.14 = (bf16[1,26,16,512]{3,2,1,0:T(8,128)(2,1)S(1)}, bf16[1,26,16,512]{3,2,1,0:T(8,128)(2,1)S(1)}, u32[]{:S(2)}, u32[]{:S(2)}) collective-permute-start(bf16[1,26,16,512]{3,2,1,0:T(8,128)(2,1)S(1)} %get-tuple-element.51), channel_id=1, source_target_pairs={{0,8},{8,0},{16,24},{24,16},{1,9},{9,1},{17,25},{25,17},{2,10},{10... | collective-permute-start | bytes 1277960 | tf_op jit(solution)/shard_map/ppermute | solution.py:46
  63.4 11.8 %collective-permute-start.15 = (bf16[1,26,16,512]{3,2,1,0:T(8,128)(2,1)S(1)}, bf16[1,26,16,512]{3,2,1,0:T(8,128)(2,1)S(1)}, u32[]{:S(2)}, u32[]{:S(2)}) collective-permute-start(bf16[1,26,16,512]{3,2,1,0:T(8,128)(2,1)S(1)} %get-tuple-element.52), channel_id=1, source_target_pairs={{0,16},{8,24},{16,0},{24,8},{1,17},{9,25},{17,1},{25,9},{2,18},{10... | collective-permute-start | bytes 1277960 | tf_op jit(solution)/shard_map/ppermute | solution.py:46
  72.9 11.8 %collective-permute-start.16 = (bf16[1,26,16,512]{3,2,1,0:T(8,128)(2,1)S(1)}, bf16[1,26,16,512]{3,2,1,0:T(8,128)(2,1)S(1)}, u32[]{:S(2)}, u32[]{:S(2)}) collective-permute-start(bf16[1,26,16,512]{3,2,1,0:T(8,128)(2,1)S(1)} %gate.6), channel_id=1, source_target_pairs={{0,8},{8,0},{16,24},{24,16},{1,9},{9,1},{17,25},{25,17},{2,10},{10... | collective-permute-start | bytes 1277960 | tf_op jit(solution)/shard_map/ppermute | solution.py:46
  74.5 12.1 %collective-permute-start.17 = (bf16[1,26,16,512]{3,2,1,0:T(8,128)(2,1)S(1)}, bf16[1,26,16,512]{3,2,1,0:T(8,128)(2,1)S(1)}, u32[]{:S(2)}, u32[]{:S(2)}) collective-permute-start(bf16[1,26,16,512]{3,2,1,0:T(8,128)(2,1)S(1)} %gate.7), channel_id=1, source_target_pairs={{0,16},{8,24},{16,0},{24,8},{1,17},{9,25},{17,1},{25,9},{2,18},{10... | collective-permute-start | bytes 1277960 | tf_op jit(solution)/shard_map/ppermute | solution.py:46
  86.6 13.5 %collective-permute-start.19 = (bf16[1,26,16,512]{3,2,1,0:T(8,128)(2,1)S(1)}, bf16[1,26,16,512]{3,2,1,0:T(8,128)(2,1)S(1)}, u32[]{:S(2)}, u32[]{:S(2)}) collective-permute-start(bf16[1,26,16,512]{3,2,1,0:T(8,128)(2,1)S(1)} %gate.9), channel_id=1, source_target_pairs={{0,24},{8,16},{16,8},{24,0},{1,25},{9,17},{17,9},{25,1},{2,26},{10... | collective-permute-start | bytes 1277960 | tf_op jit(solution)/shard_map/ppermute | solution.py:46
  87.2 21.6 %collective-permute-start.18 = (bf16[1,26,16,512]{3,2,1,0:T(8,128)(2,1)S(1)}, bf16[1,26,16,512]{3,2,1,0:T(8,128)(2,1)S(1)}, u32[]{:S(2)}, u32[]{:S(2)}) collective-permute-start(bf16[1,26,16,512]{3,2,1,0:T(8,128)(2,1)S(1)} %gate.8), channel_id=1, source_target_pairs={{0,24},{8,16},{16,8},{24,0},{1,25},{9,17},{17,9},{25,1},{2,26},{10... | collective-permute-start | bytes 1277960 | tf_op jit(solution)/shard_map/ppermute | solution.py:46

commit v5 on v4

--- a/solution.py
+++ b/solution.py
@@ -615,14 +615,14 @@
         return outs, token
 
     token = None
-    stages = [[(0, g) for g in halves]] + [[(k, g) for k in near] for g in halves]
+    stages = [[(0, g)] for g in halves] + [[(k, g) for k in near] for g in halves]
     stages += [[(k, g)] for k in far for g in halves]
-    sends = [[(k, g) for k in near] for g in halves[1:]] + [[(k, g) for k in far for g in halves]]
+    sends = {g - 1: [(k, g) for k in near] for g in halves[1:]}
+    sends[len(halves)] = [(k, g) for k in far for g in halves]
     for n, stage in enumerate(stages):
         outs, token = work_on(stage, outs)
-        following = sends[n] if n < len(sends) else []
-        there = list(arrived.values()) if n else []
-        for k, g in following:
+        there = list(arrived.values()) if n >= len(halves) else []
+        for k, g in sends.get(n, []):
             (held,) = gate([pieces[k][g]], [token] + there)
             arrived[k, g] = swap(held, "frame", k)
     foreground, background = outs

time: 114 us -> 113 us (level)
  waiting for transfers between devices: 30.5 us -> 27.3 us
  Pallas kernels: 57.5 us -> 59.3 us
    ppermute x16, waiting for transfers between devices: 30.5 us -> 27.3 us  [swap(): return lax.ppermute(value, axis, pairs)]
    pallas_call x5 -> x6, Pallas kernels: 34.9 us -> 36.7 us  [variation(): pl.pallas_call(functools.partial(variation_kernel, units, at, len(outs)),...]
  transfers between devices with their start and end apart: 20 -> 20, of which waited for: 12 -> 10; matrix products, arithmetic and copies ran while one was open for 0% -> 0% of each run, Pallas kernels for 41% -> 43%
where the time goes in v5:
time: 113 us
  Pallas kernels  59.3 us (52%)
  waiting for transfers between devices  27.3 us (24%)
  starting transfers between devices  22.1 us (20%)
  local copies, waits for them, and re-layouts  2.75 us (2%)
  between operations  1.2 us (1%)
    pallas_call x6, Pallas kernels, variation(): pl.pallas_call(functools.partial(variation_kernel, units, at, len(outs)),...  36.7 us
    ppermute x16, waiting for transfers between devices, swap(): return lax.ppermute(value, axis, pairs)  27.3 us
    ppermute x16, starting transfers between devices, swap(): return lax.ppermute(value, axis, pairs)  20.4 us
    pallas_call x1, Pallas kernels, mixing_matrix(): pl.pallas_call(mixing_kernel, out_shape=jax.ShapeDtypeStruct(gram.shape[1...  9 us
    pallas_call x2, Pallas kernels, residual(): pl.pallas_call(functools.partial(residual_kernel, chans - 1, picks), in_s...  7.89 us
    pallas_call x1, Pallas kernels, interleaved(): pl.pallas_call(interleave_kernel, in_specs=[smem()] + [vmem()] * 3 + [any...  2.57 us
  transfers between devices with their start and end apart: 20, of which 10 were waited for; matrix products, arithmetic and copies ran while one was open for 0% of the time, Pallas kernels for 43%

profile of v5, /device:TPU:0, one launch (start us, length us, event | category | flops | bytes accessed | tf_op | source)
XLA Modules:
  0.0 112.8 jit_solution(10053730205917113869)
XLA Ops:
  0.6 0.6 stack.43.info_ref.ids_ref
  1.3 4.0 %residual.3 = (bf16[1,16,32,512]{3,2,1,0:T(8,128)(2,1)}, bf16[1,16,32,512]{3,2,1,0:T(8,128)(2,1)}) custom-call(s32[11]{0:T(128)} %stack.43.info_ref.ids_ref, bf16[32,4,16,512]{3,2,1,0:T(8,128)(2,1)} %frames_ref.5, bf16[32,4,16,512]{3,2,1,0:T(8,128)(2,1)} %prev_ref.3, s32[32,16,512]{2,1,0:T(8,128)} %valid_ref.5), custom_call_target="tpu_custom_call" | custom-call | bytes 10800000 | tf_op jit(solution)/shard_map/residual/pallas_call | solution.py:261
  5.2 0.0 copy-start
  5.3 0.0 copy-start.1
  5.3 4.0 %collective-permute-start.4 = (bf16[1,16,32,512]{3,2,1,0:T(8,128)(2,1)}, bf16[1,16,32,512]{3,2,1,0:T(8,128)(2,1)S(1)}, u32[]{:S(2)}, u32[]{:S(2)}) collective-permute-start(bf16[1,16,32,512]{3,2,1,0:T(8,128)(2,1)} %get-tuple-element.40.refs_2_), channel_id=1, source_target_pairs={{0,24},{8,16},{16,8},{24,0},{1,25},{9,17},{17,9},{25,1},{2,26},{10... | collective-permute-start | bytes 1572872 | tf_op jit(solution)/shard_map/ppermute | solution.py:46
  9.3 3.9 %residual.2 = (bf16[1,16,32,512]{3,2,1,0:T(8,128)(2,1)}, bf16[1,16,32,512]{3,2,1,0:T(8,128)(2,1)}) custom-call(s32[11]{0:T(128)} %stack.43.info_ref.ids_ref, bf16[32,4,16,512]{3,2,1,0:T(8,128)(2,1)} %frames_ref.5, bf16[32,4,16,512]{3,2,1,0:T(8,128)(2,1)} %prev_ref.3, s32[32,16,512]{2,1,0:T(8,128)} %valid_ref.5), custom_call_target="tpu_custom_call" | custom-call | bytes 10800000 | tf_op jit(solution)/shard_map/residual/pallas_call | solution.py:261
  13.2 0.6 collective-permute-start.2
  13.8 0.5 collective-permute-start.3
  14.3 0.1 fusion.order_ref
  14.5 0.0 copy-start.4
  14.5 1.0 copy-done.4
  15.6 1.0 copy-done.5
  16.6 2.6 %interleave.1 = (bf16[5,16,32,512]{3,2,1,0:T(8,128)(2,1)S(1)}, bf16[5,5,32,512]{3,2,1,0:T(8,128)(2,1)S(1)}, bf16[5,5,32,512]{3,2,1,0:T(8,128)(2,1)S(1)}) custom-call(s32[11]{0:T(128)S(1)} %copy-done.6, bf16[32,4,16,512]{3,2,1,0:T(8,128)(2,1)S(1)} %copy-done, s32[32,16,512]{2,1,0:T(8,128)S(1)} %copy-done.1, bf16[512,512]{1,0:T(8,128)(2,1)S(1)} %fusion.order_ref, ...), custom_call_target="tpu_custom_call" | custom-call | bytes 11880000 | tf_op jit(solution)/shard_map/interleave/pallas_call | solution.py:306
  19.2 0.1 collective-permute-start
  19.2 0.7 collective-permute-start.1
  20.0 2.3 %collective-permute-done.4 = bf16[1,16,32,512]{3,2,1,0:T(8,128)(2,1)S(1)} collective-permute-done((bf16[1,16,32,512]{3,2,1,0:T(8,128)(2,1)}, bf16[1,16,32,512]{3,2,1,0:T(8,128)(2,1)S(1)}, u32[]{:S(2)}, u32[]{:S(2)}) %collective-permute-start.4) | collective-permute-done | bytes 524320 | tf_op jit(solution)/shard_map/ppermute | solution.py:46
  22.3 10.7 %collective-permute-done.2 = bf16[1,16,32,512]{3,2,1,0:T(8,128)(2,1)S(1)} collective-permute-done((bf16[1,16,32,512]{3,2,1,0:T(8,128)(2,1)}, bf16[1,16,32,512]{3,2,1,0:T(8,128)(2,1)S(1)}, u32[]{:S(2)}, u32[]{:S(2)}) %collective-permute-start.2) | collective-permute-done | bytes 524320 | tf_op jit(solution)/shard_map/ppermute | solution.py:46
  32.9 1.5 %gram.1 = (f32[72,128]{1,0:T(8,128)S(1)}, bf16[16,128,512]{2,1,0:T(8,128)(2,1)S(1)}, bf16[1,5,128,512]{3,2,1,0:T(8,128)(2,1)S(1)}, bf16[1,5,128,512]{3,2,1,0:T(8,128)(2,1)S(1)}) custom-call(s32[11]{0:T(128)S(1)} %copy-done.6, bf16[16,32,512]{2,1,0:T(8,128)(2,1)S(1)} %bitcast.12, bf16[16,32,512]{2,1,0:T(8,128)(2,1)S(1)} %bitcast.14, ...), custom_call_target="tpu_custom_call" | custom-call | bytes 5040000 | tf_op jit(solution)/shard_map/gram/pallas_call | solution.py:342
  34.5 2.4 %collective-permute-start.7 = (f32[72,128]{1,0:T(8,128)S(1)}, f32[72,128]{1,0:T(8,128)S(1)}, u32[]{:S(2)}, u32[]{:S(2)}) collective-permute-start(f32[72,128]{1,0:T(8,128)S(1)} %get-tuple-element.45), channel_id=1, source_target_pairs={{0,24},{8,16},{16,8},{24,0},{1,25},{9,17},{17,9},{25,1},{2,26},{10... | collective-permute-start | bytes 110600 | tf_op jit(solution)/shard_map/ppermute | solution.py:46
  36.9 0.6 collective-permute-start.6
  37.5 0.5 collective-permute-start.5
  38.0 1.4 %collective-permute-done.7 = f32[72,128]{1,0:T(8,128)S(1)} collective-permute-done((f32[72,128]{1,0:T(8,128)S(1)}, f32[72,128]{1,0:T(8,128)S(1)}, u32[]{:S(2)}, u32[]{:S(2)}) %collective-permute-start.7) | collective-permute-done | bytes 36896 | tf_op jit(solution)/shard_map/ppermute | solution.py:46
  39.4 1.4 %collective-permute-done.6 = f32[72,128]{1,0:T(8,128)S(1)} collective-permute-done((f32[72,128]{1,0:T(8,128)S(1)}, f32[72,128]{1,0:T(8,128)S(1)}, u32[]{:S(2)}, u32[]{:S(2)}) %collective-permute-start.6) | collective-permute-done | bytes 36896 | tf_op jit(solution)/shard_map/ppermute | solution.py:46
  40.8 0.6 collective-permute-done.5
  41.5 0.1 collective-permute-start.8
  41.6 1.2 %collective-permute-done.8 = f32[72,128]{1,0:T(8,128)S(1)} collective-permute-done((f32[72,128]{1,0:T(8,128)S(1)}, f32[72,128]{1,0:T(8,128)S(1)}, u32[]{:S(2)}, u32[]{:S(2)}) %collective-permute-start.8) | collective-permute-done | bytes 36896 | tf_op jit(solution)/shard_map/ppermute | solution.py:46
  42.8 3.6 %collective-permute-start.11 = (f32[72,128]{1,0:T(8,128)S(1)}, f32[72,128]{1,0:T(8,128)S(1)}, u32[]{:S(2)}, u32[]{:S(2)}) collective-permute-start(f32[72,128]{1,0:T(8,128)S(1)} %add.67), channel_id=1, source_target_pairs={{0,6},{1,7},{2,4},{3,5},{4,2},{5,3},{6,0},{7,1},{8,14},{9,15},{10,... | collective-permute-start | bytes 110600 | tf_op jit(solution)/shard_map/ppermute | solution.py:46
  46.4 0.8 collective-permute-start.9
  47.1 1.4 %collective-permute-done.11 = f32[72,128]{1,0:T(8,128)S(1)} collective-permute-done((f32[72,128]{1,0:T(8,128)S(1)}, f32[72,128]{1,0:T(8,128)S(1)}, u32[]{:S(2)}, u32[]{:S(2)}) %collective-permute-start.11) | collective-permute-done | bytes 36896 | tf_op jit(solution)/shard_map/ppermute | solution.py:46
  48.5 2.7 %collective-permute-done.10 = f32[72,128]{1,0:T(8,128)S(1)} collective-permute-done((f32[72,128]{1,0:T(8,128)S(1)}, f32[72,128]{1,0:T(8,128)S(1)}, u32[]{:S(2)}, u32[]{:S(2)}) %collective-permute-start.10) | collective-permute-done | bytes 36896 | tf_op jit(solution)/shard_map/ppermute | solution.py:46
  51.3 0.1 collective-permute-start.12
  51.4 0.9 collective-permute-start.13
  52.3 9.0 %mixing.1.mixing_ref = bf16[128,128]{1,0:T(8,128)(2,1)S(1)} custom-call(f32[72,128]{1,0:T(8,128)S(1)} %get-tuple-element.48.gram_ref, f32[64,128]{1,0:T(8,128)S(1)} %bitcast.16), custom_call_target="tpu_custom_call" | custom-call | bytes 38160000 | tf_op jit(solution)/shard_map/mixing/pallas_call | solution.py:187
  61.3 1.6 %spread.1 = (bf16[1,26,16,512]{3,2,1,0:T(8,128)(2,1)S(1)}, bf16[1,26,16,512]{3,2,1,0:T(8,128)(2,1)S(1)}, bf16[1,26,16,512]{3,2,1,0:T(8,128)(2,1)S(1)}, bf16[1,26...) custom-call(s32[11]{0:T(128)S(1)} %copy-done.6, ...), custom_call_target="tpu_custom_call" | custom-call | bytes 5760000 | tf_op jit(solution)/shard_map/spread/pallas_call | solution.py:389
  62.9 0.6 collective-permute-start.14
  63.5 1.4 %collective-permute-start.15 = (bf16[1,26,16,512]{3,2,1,0:T(8,128)(2,1)S(1)}, bf16[1,26,16,512]{3,2,1,0:T(8,128)(2,1)S(1)}, u32[]{:S(2)}, u32[]{:S(2)}) collective-permute-start(bf16[1,26,16,512]{3,2,1,0:T(8,128)(2,1)S(1)} %get-tuple-element.54), channel_id=1, source_target_pairs={{0,16},{8,24},{16,0},{24,8},{1,17},{9,25},{17,1},{25,9},{2,18},{10... | collective-permute-start | bytes 1277960 | tf_op jit(solution)/shard_map/ppermute | solution.py:46
  64.9 4.5 %variation.6 = (bf16[32,4,16,512]{3,2,1,0:T(8,128)(2,1)}, bf16[32,4,16,512]{3,2,1,0:T(8,128)(2,1)}, f32[8,128]{1,0:T(8,128)S(1)}) custom-call(s32[11]{0:T(128)S(1)} %copy-done.6, f32[4]{0:T(128)S(1)} %copy-done.8, bf16[512,512]{1,0:T(8,128)(2,1)S(1)} %fusion.order_ref, bf16[5,16,32,512]{3,2,1,0:T(8,128)(2,1)S(1)} %get-tuple-element.42.refs_0_, ...), custom_call_target="tpu_custom_call" | custom-call | bytes 15480000 | tf_op jit(solution)/shard_map/variation/pallas_call | solution.py:544
  69.4 1.6 %collective-permute-start.16 = (bf16[1,26,16,512]{3,2,1,0:T(8,128)(2,1)S(1)}, bf16[1,26,16,512]{3,2,1,0:T(8,128)(2,1)S(1)}, u32[]{:S(2)}, u32[]{:S(2)}) collective-permute-start(bf16[1,26,16,512]{3,2,1,0:T(8,128)(2,1)S(1)} %gate.6), channel_id=1, source_target_pairs={{0,8},{8,0},{16,24},{24,16},{1,9},{9,1},{17,25},{25,17},{2,10},{10... | collective-permute-start | bytes 1277960 | tf_op jit(solution)/shard_map/ppermute | solution.py:46
  71.0 0.7 collective-permute-start.17
  71.7 5.3 %variation.7 = (bf16[32,4,16,512]{3,2,1,0:T(8,128)(2,1)}, bf16[32,4,16,512]{3,2,1,0:T(8,128)(2,1)}, f32[8,128]{1,0:T(8,128)}) custom-call(s32[11]{0:T(128)S(1)} %copy-done.6, f32[4]{0:T(128)S(1)} %copy-done.8, bf16[512,512]{1,0:T(8,128)(2,1)S(1)} %fusion.order_ref, ...), custom_call_target="tpu_custom_call", output_to_operand_aliasing={{0}: (7, {}), {1}: (8, {})} | custom-call | bytes 15480000 | tf_op jit(solution)/shard_map/variation/pallas_call | solution.py:544
  77.0 7.8 %variation.8 = (bf16[32,4,16,512]{3,2,1,0:T(8,128)(2,1)}, bf16[32,4,16,512]{3,2,1,0:T(8,128)(2,1)}, f32[8,128]{1,0:T(8,128)S(1)}) custom-call(s32[11]{0:T(128)S(1)} %copy-done.6, f32[4]{0:T(128)S(1)} %copy-done.8, bf16[512,512]{1,0:T(8,128)(2,1)S(1)} %fusion.order_ref, ...), custom_call_target="tpu_custom_call", output_to_operand_aliasing={{0}: (8, {}), {1}: (9, {})} | custom-call | bytes 30960000 | tf_op jit(solution)/shard_map/variation/pallas_call | solution.py:544
  84.9 1.5 %collective-permute-start.19 = (bf16[1,26,16,512]{3,2,1,0:T(8,128)(2,1)S(1)}, bf16[1,26,16,512]{3,2,1,0:T(8,128)(2,1)S(1)}, u32[]{:S(2)}, u32[]{:S(2)}) collective-permute-start(bf16[1,26,16,512]{3,2,1,0:T(8,128)(2,1)S(1)} %gate.9), channel_id=1, source_target_pairs={{0,24},{8,16},{16,8},{24,0},{1,25},{9,17},{17,9},{25,1},{2,26},{10... | collective-permute-start | bytes 1277960 | tf_op jit(solution)/shard_map/ppermute | solution.py:46
  86.4 1.5 %collective-permute-start.18 = (bf16[1,26,16,512]{3,2,1,0:T(8,128)(2,1)S(1)}, bf16[1,26,16,512]{3,2,1,0:T(8,128)(2,1)S(1)}, u32[]{:S(2)}, u32[]{:S(2)}) collective-permute-start(bf16[1,26,16,512]{3,2,1,0:T(8,128)(2,1)S(1)} %gate.8), channel_id=1, source_target_pairs={{0,24},{8,16},{16,8},{24,0},{1,25},{9,17},{17,9},{25,1},{2,26},{10... | collective-permute-start | bytes 1277960 | tf_op jit(solution)/shard_map/ppermute | solution.py:46
  87.9 8.4 %variation.9 = (bf16[32,4,16,512]{3,2,1,0:T(8,128)(2,1)}, bf16[32,4,16,512]{3,2,1,0:T(8,128)(2,1)}, f32[8,128]{1,0:T(8,128)}) custom-call(s32[11]{0:T(128)S(1)} %copy-done.6, f32[4]{0:T(128)S(1)} %copy-done.8, bf16[512,512]{1,0:T(8,128)(2,1)S(1)} %fusion.order_ref, ...), custom_call_target="tpu_custom_call", output_to_operand_aliasing={{0}: (8, {}), {1}: (9, {})} | custom-call | bytes 30960000 | tf_op jit(solution)/shard_map/variation/pallas_call | solution.py:544
  96.3 2.0 %collective-permute-done.19.refs_3_ = bf16[1,26,16,512]{3,2,1,0:T(8,128)(2,1)S(1)} collective-permute-done((bf16[1,26,16,512]{3,2,1,0:T(8,128)(2,1)S(1)}, bf16[1,26,16,512]{3,2,1,0:T(8,128)(2,1)S(1)}, u32[]{:S(2)}, u32[]{:S(2)}) %collective-permute-start.19) | collective-permute-done | bytes 426016 | tf_op jit(solution)/shard_map/ppermute | solution.py:46
  98.3 5.4 %variation.10 = (bf16[32,4,16,512]{3,2,1,0:T(8,128)(2,1)}, bf16[32,4,16,512]{3,2,1,0:T(8,128)(2,1)}, f32[8,128]{1,0:T(8,128)}) custom-call(s32[11]{0:T(128)S(1)} %copy-done.6, f32[4]{0:T(128)S(1)} %copy-done.8, bf16[512,512]{1,0:T(8,128)(2,1)S(1)} %fusion.order_ref, ...), custom_call_target="tpu_custom_call", output_to_operand_aliasing={{0}: (7, {}), {1}: (8, {})} | custom-call | bytes 15480000 | tf_op jit(solution)/shard_map/variation/pallas_call | solution.py:544
  103.7 3.7 %collective-permute-done.18.refs_3_ = bf16[1,26,16,512]{3,2,1,0:T(8,128)(2,1)S(1)} collective-permute-done((bf16[1,26,16,512]{3,2,1,0:T(8,128)(2,1)S(1)}, bf16[1,26,16,512]{3,2,1,0:T(8,128)(2,1)S(1)}, u32[]{:S(2)}, u32[]{:S(2)}) %collective-permute-start.18) | collective-permute-done | bytes 426016 | tf_op jit(solution)/shard_map/ppermute | solution.py:46
  107.4 5.2 %variation.11 = (bf16[32,4,16,512]{3,2,1,0:T(8,128)(2,1)}, bf16[32,4,16,512]{3,2,1,0:T(8,128)(2,1)}, f32[8,128]{1,0:T(8,128)}) custom-call(s32[11]{0:T(128)S(1)} %copy-done.6, f32[4]{0:T(128)S(1)} %copy-done.8, bf16[512,512]{1,0:T(8,128)(2,1)S(1)} %fusion.order_ref, ...), custom_call_target="tpu_custom_call", output_to_operand_aliasing={{0}: (7, {}), {1}: (8, {})} | custom-call | bytes 15480000 | tf_op jit(solution)/shard_map/variation/pallas_call | solution.py:544
  (35 shorter events, 0.1 us)
Async XLA Ops:
  5.2 9.2 %copy-start = (bf16[32,4,16,512]{3,2,1,0:T(8,128)(2,1)S(1)}, bf16[32,4,16,512]{3,2,1,0:T(8,128)(2,1)}, u32[]{:S(2)}) copy-start(bf16[32,4,16,512]{3,2,1,0:T(8,128)(2,1)} %frames_ref.5) | copy-start | bytes 6291460
  5.3 9.2 %copy-start.1 = (s32[32,16,512]{2,1,0:T(8,128)S(1)}, s32[32,16,512]{2,1,0:T(8,128)}, u32[]{:S(2)}) copy-start(s32[32,16,512]{2,1,0:T(8,128)} %valid_ref.5) | copy-start | bytes 3145732
  5.3 9.2 %copy-start.2 = (bf16[1,16,32,512]{3,2,1,0:T(8,128)(2,1)S(1)}, bf16[1,16,32,512]{3,2,1,0:T(8,128)(2,1)}, u32[]{:S(2)}) copy-start(bf16[1,16,32,512]{3,2,1,0:T(8,128)(2,1)} %get-tuple-element.41.refs_3_) | copy-start | bytes 1572868
  5.3 9.2 %copy-start.3 = (bf16[1,16,32,512]{3,2,1,0:T(8,128)(2,1)S(1)}, bf16[1,16,32,512]{3,2,1,0:T(8,128)(2,1)}, u32[]{:S(2)}) copy-start(bf16[1,16,32,512]{3,2,1,0:T(8,128)(2,1)} %get-tuple-element.40.refs_2_) | copy-start | bytes 1572868
  5.3 9.2 %copy-start.6 = (s32[11]{0:T(128)S(1)}, s32[11]{0:T(128)}, u32[]{:S(2)}) copy-start(s32[11]{0:T(128)} %stack.43.info_ref.ids_ref) | copy-start | bytes 136
  5.3 17.0 %collective-permute-start.4 = (bf16[1,16,32,512]{3,2,1,0:T(8,128)(2,1)}, bf16[1,16,32,512]{3,2,1,0:T(8,128)(2,1)S(1)}, u32[]{:S(2)}, u32[]{:S(2)}) collective-permute-start(bf16[1,16,32,512]{3,2,1,0:T(8,128)(2,1)} %get-tuple-element.40.refs_2_), channel_id=1, source_target_pairs={{0,24},{8,16},{16,8},{24,0},{1,25},{9,17},{17,9},{25,1},{2,26},{10... | collective-permute-start | bytes 1572872 | tf_op jit(solution)/shard_map/ppermute | solution.py:46
  13.2 19.7 %collective-permute-start.2 = (bf16[1,16,32,512]{3,2,1,0:T(8,128)(2,1)}, bf16[1,16,32,512]{3,2,1,0:T(8,128)(2,1)S(1)}, u32[]{:S(2)}, u32[]{:S(2)}) collective-permute-start(bf16[1,16,32,512]{3,2,1,0:T(8,128)(2,1)} %get-tuple-element.38.refs_0_), channel_id=1, source_target_pairs={{0,8},{8,0},{16,24},{24,16},{1,9},{9,1},{17,25},{25,17},{2,10},{10... | collective-permute-start | bytes 1572872 | tf_op jit(solution)/shard_map/ppermute | solution.py:46
  13.8 19.1 %collective-permute-start.3 = (bf16[1,16,32,512]{3,2,1,0:T(8,128)(2,1)}, bf16[1,16,32,512]{3,2,1,0:T(8,128)(2,1)S(1)}, u32[]{:S(2)}, u32[]{:S(2)}) collective-permute-start(bf16[1,16,32,512]{3,2,1,0:T(8,128)(2,1)} %get-tuple-element.39.refs_1_), channel_id=1, source_target_pairs={{0,16},{8,24},{16,0},{24,8},{1,17},{9,25},{17,1},{25,9},{2,18},{10... | collective-permute-start | bytes 1572872 | tf_op jit(solution)/shard_map/ppermute | solution.py:46
  14.5 1.0 copy-start.4
  15.6 1.0 copy-start.5
  19.2 32.1 %collective-permute-start = (bf16[5,5,32,512]{3,2,1,0:T(8,128)(2,1)S(1)}, bf16[5,5,32,512]{3,2,1,0:T(8,128)(2,1)S(1)}, u32[]{:S(2)}, u32[]{:S(2)}) collective-permute-start(bf16[5,5,32,512]{3,2,1,0:T(8,128)(2,1)S(1)} %get-tuple-element.43), channel_id=1, source_target_pairs={{0,1},{1,0},{2,3},{3,2},{4,5},{5,4},{6,7},{7,6},{8,9},{9,8},{10,11... | collective-permute-start | bytes 2457608 | tf_op jit(solution)/shard_map/ppermute | solution.py:36
  19.2 32.0 %collective-permute-start.1 = (bf16[5,5,32,512]{3,2,1,0:T(8,128)(2,1)S(1)}, bf16[5,5,32,512]{3,2,1,0:T(8,128)(2,1)S(1)}, u32[]{:S(2)}, u32[]{:S(2)}) collective-permute-start(bf16[5,5,32,512]{3,2,1,0:T(8,128)(2,1)S(1)} %get-tuple-element.44), channel_id=1, source_target_pairs={{1,2},{2,1},{3,4},{4,3},{5,6},{6,5},{9,10},{10,9},{11,12},{12,11},... | collective-permute-start | bytes 2457608 | tf_op jit(solution)/shard_map/ppermute | solution.py:36
  34.5 17.8 %copy-start.7 = (f32[128,64]{0,1:T(8,128)S(1)}, f32[128,64]{0,1:T(8,128)}, u32[]{:S(2)}) copy-start(f32[128,64]{0,1:T(8,128)} %param.8) | copy-start | bytes 98308
  34.5 4.9 %collective-permute-start.7 = (f32[72,128]{1,0:T(8,128)S(1)}, f32[72,128]{1,0:T(8,128)S(1)}, u32[]{:S(2)}, u32[]{:S(2)}) collective-permute-start(f32[72,128]{1,0:T(8,128)S(1)} %get-tuple-element.45), channel_id=1, source_target_pairs={{0,24},{8,16},{16,8},{24,0},{1,25},{9,17},{17,9},{25,1},{2,26},{10... | collective-permute-start | bytes 110600 | tf_op jit(solution)/shard_map/ppermute | solution.py:46
  36.9 4.0 %collective-permute-start.6 = (f32[72,128]{1,0:T(8,128)S(1)}, f32[72,128]{1,0:T(8,128)S(1)}, u32[]{:S(2)}, u32[]{:S(2)}) collective-permute-start(f32[72,128]{1,0:T(8,128)S(1)} %get-tuple-element.45), channel_id=1, source_target_pairs={{0,16},{8,24},{16,0},{24,8},{1,17},{9,25},{17,1},{25,9},{2,18},{10... | collective-permute-start | bytes 110600 | tf_op jit(solution)/shard_map/ppermute | solution.py:46
  37.5 4.0 %collective-permute-start.5 = (f32[72,128]{1,0:T(8,128)S(1)}, f32[72,128]{1,0:T(8,128)S(1)}, u32[]{:S(2)}, u32[]{:S(2)}) collective-permute-start(f32[72,128]{1,0:T(8,128)S(1)} %get-tuple-element.45), channel_id=1, source_target_pairs={{0,8},{8,0},{16,24},{24,16},{1,9},{9,1},{17,25},{25,17},{2,10},{10... | collective-permute-start | bytes 110600 | tf_op jit(solution)/shard_map/ppermute | solution.py:46
  41.5 1.3 %collective-permute-start.8 = (f32[72,128]{1,0:T(8,128)S(1)}, f32[72,128]{1,0:T(8,128)S(1)}, u32[]{:S(2)}, u32[]{:S(2)}) collective-permute-start(f32[72,128]{1,0:T(8,128)S(1)} %add_add_fusion.1), channel_id=1, source_target_pairs={{0,1},{1,0},{2,3},{3,2},{4,5},{5,4},{6,7},{7,6},{8,9},{9,8},{10,11... | collective-permute-start | bytes 110600 | tf_op jit(solution)/shard_map/ppermute | solution.py:46
  42.8 5.8 %collective-permute-start.11 = (f32[72,128]{1,0:T(8,128)S(1)}, f32[72,128]{1,0:T(8,128)S(1)}, u32[]{:S(2)}, u32[]{:S(2)}) collective-permute-start(f32[72,128]{1,0:T(8,128)S(1)} %add.67), channel_id=1, source_target_pairs={{0,6},{1,7},{2,4},{3,5},{4,2},{5,3},{6,0},{7,1},{8,14},{9,15},{10,... | collective-permute-start | bytes 110600 | tf_op jit(solution)/shard_map/ppermute | solution.py:46
  46.4 4.9 %collective-permute-start.10 = (f32[72,128]{1,0:T(8,128)S(1)}, f32[72,128]{1,0:T(8,128)S(1)}, u32[]{:S(2)}, u32[]{:S(2)}) collective-permute-start(f32[72,128]{1,0:T(8,128)S(1)} %add.67), channel_id=1, source_target_pairs={{0,4},{1,5},{2,6},{3,7},{4,0},{5,1},{6,2},{7,3},{8,12},{9,13},{10,... | collective-permute-start | bytes 110600 | tf_op jit(solution)/shard_map/ppermute | solution.py:46
  46.4 4.9 %collective-permute-start.9 = (f32[72,128]{1,0:T(8,128)S(1)}, f32[72,128]{1,0:T(8,128)S(1)}, u32[]{:S(2)}, u32[]{:S(2)}) collective-permute-start(f32[72,128]{1,0:T(8,128)S(1)} %add.67), channel_id=1, source_target_pairs={{0,2},{1,3},{2,0},{3,1},{4,6},{5,7},{6,4},{7,5},{8,10},{9,11},{10,... | collective-permute-start | bytes 110600 | tf_op jit(solution)/shard_map/ppermute | solution.py:46
  51.3 13.6 %copy-start.8 = (f32[4]{0:T(128)S(1)}, f32[4]{0:T(128)}, u32[]{:S(2)}) copy-start(f32[4]{0:T(128)} %weight_ref.11) | copy-start | bytes 52
  51.3 10.0 %collective-permute-start.12 = (bf16[1,5,128,512]{3,2,1,0:T(8,128)(2,1)S(1)}, bf16[1,5,128,512]{3,2,1,0:T(8,128)(2,1)S(1)}, u32[]{:S(2)}, u32[]{:S(2)}) collective-permute-start(bf16[1,5,128,512]{3,2,1,0:T(8,128)(2,1)S(1)} %get-tuple-element.50), channel_id=1, source_target_pairs={{0,1},{1,0},{2,3},{3,2},{4,5},{5,4},{6,7},{7,6},{8,9},{9,8},{10,11... | collective-permute-start | bytes 1966088 | tf_op jit(solution)/shard_map/ppermute | solution.py:36
  51.4 9.9 %collective-permute-start.13 = (bf16[1,5,128,512]{3,2,1,0:T(8,128)(2,1)S(1)}, bf16[1,5,128,512]{3,2,1,0:T(8,128)(2,1)S(1)}, u32[]{:S(2)}, u32[]{:S(2)}) collective-permute-start(bf16[1,5,128,512]{3,2,1,0:T(8,128)(2,1)S(1)} %get-tuple-element.51), channel_id=1, source_target_pairs={{1,2},{2,1},{3,4},{4,3},{5,6},{6,5},{9,10},{10,9},{11,12},{12,11},... | collective-permute-start | bytes 1966088 | tf_op jit(solution)/shard_map/ppermute | solution.py:36
  62.9 14.1 %collective-permute-start.14 = (bf16[1,26,16,512]{3,2,1,0:T(8,128)(2,1)S(1)}, bf16[1,26,16,512]{3,2,1,0:T(8,128)(2,1)S(1)}, u32[]{:S(2)}, u32[]{:S(2)}) collective-permute-start(bf16[1,26,16,512]{3,2,1,0:T(8,128)(2,1)S(1)} %get-tuple-element.53), channel_id=1, source_target_pairs={{0,8},{8,0},{16,24},{24,16},{1,9},{9,1},{17,25},{25,17},{2,10},{10... | collective-permute-start | bytes 1277960 | tf_op jit(solution)/shard_map/ppermute | solution.py:46
  63.5 13.5 %collective-permute-start.15 = (bf16[1,26,16,512]{3,2,1,0:T(8,128)(2,1)S(1)}, bf16[1,26,16,512]{3,2,1,0:T(8,128)(2,1)S(1)}, u32[]{:S(2)}, u32[]{:S(2)}) collective-permute-start(bf16[1,26,16,512]{3,2,1,0:T(8,128)(2,1)S(1)} %get-tuple-element.54), channel_id=1, source_target_pairs={{0,16},{8,24},{16,0},{24,8},{1,17},{9,25},{17,1},{25,9},{2,18},{10... | collective-permute-start | bytes 1277960 | tf_op jit(solution)/shard_map/ppermute | solution.py:46
  69.4 15.5 %collective-permute-start.16 = (bf16[1,26,16,512]{3,2,1,0:T(8,128)(2,1)S(1)}, bf16[1,26,16,512]{3,2,1,0:T(8,128)(2,1)S(1)}, u32[]{:S(2)}, u32[]{:S(2)}) collective-permute-start(bf16[1,26,16,512]{3,2,1,0:T(8,128)(2,1)S(1)} %gate.6), channel_id=1, source_target_pairs={{0,8},{8,0},{16,24},{24,16},{1,9},{9,1},{17,25},{25,17},{2,10},{10... | collective-permute-start | bytes 1277960 | tf_op jit(solution)/shard_map/ppermute | solution.py:46
  71.0 13.9 %collective-permute-start.17 = (bf16[1,26,16,512]{3,2,1,0:T(8,128)(2,1)S(1)}, bf16[1,26,16,512]{3,2,1,0:T(8,128)(2,1)S(1)}, u32[]{:S(2)}, u32[]{:S(2)}) collective-permute-start(bf16[1,26,16,512]{3,2,1,0:T(8,128)(2,1)S(1)} %gate.7), channel_id=1, source_target_pairs={{0,16},{8,24},{16,0},{24,8},{1,17},{9,25},{17,1},{25,9},{2,18},{10... | collective-permute-start | bytes 1277960 | tf_op jit(solution)/shard_map/ppermute | solution.py:46
  84.9 13.4 %collective-permute-start.19 = (bf16[1,26,16,512]{3,2,1,0:T(8,128)(2,1)S(1)}, bf16[1,26,16,512]{3,2,1,0:T(8,128)(2,1)S(1)}, u32[]{:S(2)}, u32[]{:S(2)}) collective-permute-start(bf16[1,26,16,512]{3,2,1,0:T(8,128)(2,1)S(1)} %gate.9), channel_id=1, source_target_pairs={{0,24},{8,16},{16,8},{24,0},{1,25},{9,17},{17,9},{25,1},{2,26},{10... | collective-permute-start | bytes 1277960 | tf_op jit(solution)/shard_map/ppermute | solution.py:46
  86.4 21.0 %collective-permute-start.18 = (bf16[1,26,16,512]{3,2,1,0:T(8,128)(2,1)S(1)}, bf16[1,26,16,512]{3,2,1,0:T(8,128)(2,1)S(1)}, u32[]{:S(2)}, u32[]{:S(2)}) collective-permute-start(bf16[1,26,16,512]{3,2,1,0:T(8,128)(2,1)S(1)} %gate.8), channel_id=1, source_target_pairs={{0,24},{8,16},{16,8},{24,0},{1,25},{9,17},{17,9},{25,1},{2,26},{10... | collective-permute-start | bytes 1277960 | tf_op jit(solution)/shard_map/ppermute | solution.py:46

commit v6 on v5

--- a/solution.py
+++ b/solution.py
@@ -218,14 +218,16 @@
     return pl.CostEstimate(flops=0, bytes_accessed=int(micros * 3.6e6), transcendentals=0)
 
 
-def residual_kernel(last, picks, info_ref, frames_ref, prev_ref, valid_ref, *refs):
+def residual_kernel(last, picks, frames_ref, prev_ref, valid_ref, *refs):
     outs, (now, before, ok, sems) = refs[: len(picks)], refs[len(picks) :]
     _, each, count, rows, cols = now.shape
+    me, groups = lax.axis_index("frame"), lax.axis_size("frame")
+    firsts = [partner(me, pick, groups) * each for pick in picks]
     valid_copy = pltpu.make_async_copy(valid_ref, ok, sems.at[0])
     copies = []
-    for n, pick in enumerate(picks):
+    for n in range(len(picks)):
         for c in range(each):
-            chan = info_ref[pick] * each + c
+            chan = firsts[n] + c
             at = 1 + 2 * (n * each + c)
             copies.append(
                 (
@@ -233,18 +235,16 @@
                     pltpu.make_async_copy(prev_ref.at[:, chan], before.at[n, c], sems.at[at + 1]),
                 )
             )
-    for copy in copies[0]:
-        copy.start()
     valid_copy.start()
-    for pair in copies[1:]:
+    for pair in copies:
         for copy in pair:
             copy.start()
     valid_copy.wait()
-    for n, pick in enumerate(picks):
+    for n in range(len(picks)):
         for c in range(each):
             for copy in copies[n * each + c]:
                 copy.wait()
-            keep = jnp.where(info_ref[pick] * each + c == last, 0.0, 1.0)
+            keep = jnp.where(firsts[n] + c == last, 0.0, 1.0)
             for g in range(count // PACK):
                 some = pl.ds(g * PACK, PACK)
                 for j in range(cols // LANE):
@@ -255,12 +255,12 @@
                     outs[n][c, :, some, tile(j)] = turned.astype(jnp.bfloat16)
 
 
-def residual(info, picks, each, frames, prev_fg, depth_valid):
+def residual(picks, each, frames, prev_fg, depth_valid):
     count, chans, rows, cols = frames.shape
     held = pltpu.VMEM((len(picks), each, count, rows, cols), jnp.bfloat16)
     return pl.pallas_call(
         functools.partial(residual_kernel, chans - 1, picks),
-        in_specs=[smem()] + [anywhere()] * 3,
+        in_specs=[anywhere()] * 3,
         out_specs=[vmem()] * len(picks),
         out_shape=[jax.ShapeDtypeStruct((each, rows, count, cols), jnp.bfloat16)] * len(picks),
         scratch_shapes=[
@@ -272,7 +272,7 @@
         compiler_params=pltpu.CompilerParams(vmem_limit_bytes=MOST_BYTES),
         cost_estimate=cost(3.0),
         name="residual",
-    )(info, frames, prev_fg, depth_valid)
+    )(frames, prev_fg, depth_valid)
 
 
 def interleave_kernel(info_ref, frames_ref, valid_ref, order_ref, *refs):
@@ -582,7 +582,7 @@
 
     resid = {}
     for picks in (near, far + [0]):
-        resid.update(zip(picks, residual(info, picks, each, frames, prev_fg, depth_valid)))
+        resid.update(zip(picks, residual(picks, each, frames, prev_fg, depth_valid)))
     blocks = [resid[0]] + [swap(resid[k], "frame", k) for k in range(1, groups)]
     blocks = [block.reshape(each * rows, count, cols) for block in blocks]
 
@@ -593,7 +593,7 @@
     lined_rims = rims_swapped(rims)
 
     terms, pixels, *rims = gram_terms(info, blocks, each, nval, ())
-    gram = all_sum(all_sum(terms, "frame"), "pix")
+    gram = all_sum(all_sum(terms, "pix"), "frame")
     gram, *rims = gate([gram] + rims, lined_rims)
     around = rims_swapped(rims)
     mixing = mixing_matrix(gram, sketch)

time: 113 us -> 113 us (level)
  local copies, waits for them, and re-layouts: 2.75 us -> 4.28 us
    unnamed x18, local copies, waits for them, and re-layouts: 2.12 us -> 4.19 us
    pallas_call x2, Pallas kernels: 7.89 us -> 6.54 us  [residual(): pl.pallas_call(functools.partial(residual_kernel, chans - 1, picks), in_s...]
where the time goes in v6:
time: 113 us; the launch traced here: 112 us
  Pallas kernels  58.7 us (52%)
  waiting for transfers between devices  26.2 us (23%)
  starting transfers between devices  21.8 us (19%)
  local copies, waits for them, and re-layouts  4.28 us (4%)
  between operations  1.16 us (1%)
    pallas_call x6, Pallas kernels, variation(): pl.pallas_call(functools.partial(variation_kernel, units, at, len(outs)),...  36.7 us
    ppermute x16, waiting for transfers between devices, swap(): return lax.ppermute(value, axis, pairs)  26.2 us
    ppermute x16, starting transfers between devices, swap(): return lax.ppermute(value, axis, pairs)  20 us
    pallas_call x1, Pallas kernels, mixing_matrix(): pl.pallas_call(mixing_kernel, out_shape=jax.ShapeDtypeStruct(gram.shape[1...  9 us
    pallas_call x2, Pallas kernels, residual(): pl.pallas_call(functools.partial(residual_kernel, chans - 1, picks), in_s...  6.54 us
    unnamed x18, local copies, waits for them, and re-layouts  4.19 us
    pallas_call x1, Pallas kernels, interleaved(): pl.pallas_call(interleave_kernel, in_specs=[smem()] + [vmem()] * 3 + [any...  2.57 us
    pallas_call x1, Pallas kernels, gram_terms(): pl.pallas_call(functools.partial(gram_kernel, groups, each, nval), in_spe...  2.36 us
  transfers between devices with their start and end apart: 20, of which 10 were waited for; matrix products, arithmetic and copies ran while one was open for 0% of the time, Pallas kernels for 43%

profile of v6, /device:TPU:0, one launch (start us, length us, event | category | flops | bytes accessed | tf_op | source)
XLA Modules:
  0.0 112.4 jit_solution(15153364115507887267)
XLA Ops:
  0.6 3.3 %residual.3 = (bf16[1,16,32,512]{3,2,1,0:T(8,128)(2,1)}, bf16[1,16,32,512]{3,2,1,0:T(8,128)(2,1)}) custom-call(bf16[32,4,16,512]{3,2,1,0:T(8,128)(2,1)} %frames_ref.5, bf16[32,4,16,512]{3,2,1,0:T(8,128)(2,1)} %prev_ref.3, s32[32,16,512]{2,1,0:T(8,128)} %valid_ref.5), custom_call_target="tpu_custom_call" | custom-call | bytes 10800000 | tf_op jit(solution)/shard_map/residual/pallas_call | solution.py:261
  3.9 0.0 copy-start
  3.9 4.0 %collective-permute-start.4 = (bf16[1,16,32,512]{3,2,1,0:T(8,128)(2,1)}, bf16[1,16,32,512]{3,2,1,0:T(8,128)(2,1)}, u32[]{:S(2)}, u32[]{:S(2)}) collective-permute-start(bf16[1,16,32,512]{3,2,1,0:T(8,128)(2,1)} %get-tuple-element.40.refs_2_), channel_id=1, source_target_pairs={{0,24},{8,16},{16,8},{24,0},{1,25},{9,17},{17,9},{25,1},{2,26},{10... | collective-permute-start | bytes 1572872 | tf_op jit(solution)/shard_map/ppermute | solution.py:46
  7.9 3.3 %residual.2 = (bf16[1,16,32,512]{3,2,1,0:T(8,128)(2,1)}, bf16[1,16,32,512]{3,2,1,0:T(8,128)(2,1)}) custom-call(bf16[32,4,16,512]{3,2,1,0:T(8,128)(2,1)} %frames_ref.5, bf16[32,4,16,512]{3,2,1,0:T(8,128)(2,1)} %prev_ref.3, s32[32,16,512]{2,1,0:T(8,128)} %valid_ref.5), custom_call_target="tpu_custom_call" | custom-call | bytes 10800000 | tf_op jit(solution)/shard_map/residual/pallas_call | solution.py:261
  11.2 0.6 collective-permute-start.2
  11.8 0.2 collective-permute-start.3
  12.0 0.1 stack.43.info_ref.ids_ref
  12.1 0.1 fusion.order_ref
  12.3 1.0 copy-done.2
  13.3 1.0 copy-done.4
  14.3 1.0 copy-done.5
  15.4 1.0 copy-done.6
  16.4 2.6 %interleave.1 = (bf16[5,16,32,512]{3,2,1,0:T(8,128)(2,1)S(1)}, bf16[5,5,32,512]{3,2,1,0:T(8,128)(2,1)S(1)}, bf16[5,5,32,512]{3,2,1,0:T(8,128)(2,1)S(1)}) custom-call(s32[11]{0:T(128)S(1)} %stack.43.info_ref.ids_ref, bf16[32,4,16,512]{3,2,1,0:T(8,128)(2,1)S(1)} %copy-done, s32[32,16,512]{2,1,0:T(8,128)S(1)} %copy-done.1, bf16[512,512]{1,0:T(8,128)(2,1)S(1)} %fusion.order_ref, ...), custom_call_target="tpu_custom_call" | custom-call | bytes 11880000 | tf_op jit(solution)/shard_map/interleave/pallas_call | solution.py:306
  19.0 0.1 collective-permute-start
  19.1 0.7 collective-permute-start.1
  19.8 1.2 %collective-permute-done.4 = bf16[1,16,32,512]{3,2,1,0:T(8,128)(2,1)} collective-permute-done((bf16[1,16,32,512]{3,2,1,0:T(8,128)(2,1)}, bf16[1,16,32,512]{3,2,1,0:T(8,128)(2,1)}, u32[]{:S(2)}, u32[]{:S(2)}) %collective-permute-start.4) | collective-permute-done | bytes 524320 | tf_op jit(solution)/shard_map/ppermute | solution.py:46
  21.0 10.7 %collective-permute-done.2 = bf16[1,16,32,512]{3,2,1,0:T(8,128)(2,1)} collective-permute-done((bf16[1,16,32,512]{3,2,1,0:T(8,128)(2,1)}, bf16[1,16,32,512]{3,2,1,0:T(8,128)(2,1)}, u32[]{:S(2)}, u32[]{:S(2)}) %collective-permute-start.2) | collective-permute-done | bytes 524320 | tf_op jit(solution)/shard_map/ppermute | solution.py:46
  31.7 2.4 %gram.1 = (f32[72,128]{1,0:T(8,128)S(1)}, bf16[16,128,512]{2,1,0:T(8,128)(2,1)S(1)}, bf16[1,5,128,512]{3,2,1,0:T(8,128)(2,1)S(1)}, bf16[1,5,128,512]{3,2,1,0:T(8,128)(2,1)S(1)}) custom-call(s32[11]{0:T(128)S(1)} %stack.43.info_ref.ids_ref, bf16[16,32,512]{2,1,0:T(8,128)(2,1)S(1)} %bitcast.12, bf16[16,32,512]{2,1,0:T(8,128)(2,1)} %bitcast.8.refs_1_, ...), custom_call_target="tpu_custom_call" | custom-call | bytes 5040000 | tf_op jit(solution)/shard_map/gram/pallas_call | solution.py:342
  34.1 0.1 collective-permute-start.5
  34.1 1.2 %collective-permute-done.5 = f32[72,128]{1,0:T(8,128)S(1)} collective-permute-done((f32[72,128]{1,0:T(8,128)S(1)}, f32[72,128]{1,0:T(8,128)S(1)}, u32[]{:S(2)}, u32[]{:S(2)}) %collective-permute-start.5) | collective-permute-done | bytes 36896 | tf_op jit(solution)/shard_map/ppermute | solution.py:46
  35.3 3.6 %collective-permute-start.8 = (f32[72,128]{1,0:T(8,128)S(1)}, f32[72,128]{1,0:T(8,128)S(1)}, u32[]{:S(2)}, u32[]{:S(2)}) collective-permute-start(f32[72,128]{1,0:T(8,128)S(1)} %add.64), channel_id=1, source_target_pairs={{0,6},{1,7},{2,4},{3,5},{4,2},{5,3},{6,0},{7,1},{8,14},{9,15},{10,... | collective-permute-start | bytes 110600 | tf_op jit(solution)/shard_map/ppermute | solution.py:46
  38.9 0.8 collective-permute-start.6
  39.7 1.4 %collective-permute-done.8 = f32[72,128]{1,0:T(8,128)S(1)} collective-permute-done((f32[72,128]{1,0:T(8,128)S(1)}, f32[72,128]{1,0:T(8,128)S(1)}, u32[]{:S(2)}, u32[]{:S(2)}) %collective-permute-start.8) | collective-permute-done | bytes 36896 | tf_op jit(solution)/shard_map/ppermute | solution.py:46
  41.1 2.7 %collective-permute-done.7 = f32[72,128]{1,0:T(8,128)S(1)} collective-permute-done((f32[72,128]{1,0:T(8,128)S(1)}, f32[72,128]{1,0:T(8,128)S(1)}, u32[]{:S(2)}, u32[]{:S(2)}) %collective-permute-start.7) | collective-permute-done | bytes 36896 | tf_op jit(solution)/shard_map/ppermute | solution.py:46
  43.8 2.4 %collective-permute-start.11 = (f32[72,128]{1,0:T(8,128)S(1)}, f32[72,128]{1,0:T(8,128)S(1)}, u32[]{:S(2)}, u32[]{:S(2)}) collective-permute-start(f32[72,128]{1,0:T(8,128)S(1)} %add_add_fusion.1), channel_id=1, source_target_pairs={{0,24},{8,16},{16,8},{24,0},{1,25},{9,17},{17,9},{25,1},{2,26},{10... | collective-permute-start | bytes 110600 | tf_op jit(solution)/shard_map/ppermute | solution.py:46
  46.2 0.6 collective-permute-start.10
  46.8 0.5 collective-permute-start.9
  47.4 1.4 %collective-permute-done.11 = f32[72,128]{1,0:T(8,128)S(1)} collective-permute-done((f32[72,128]{1,0:T(8,128)S(1)}, f32[72,128]{1,0:T(8,128)S(1)}, u32[]{:S(2)}, u32[]{:S(2)}) %collective-permute-start.11) | collective-permute-done | bytes 36896 | tf_op jit(solution)/shard_map/ppermute | solution.py:46
  48.7 1.4 %collective-permute-done.10 = f32[72,128]{1,0:T(8,128)S(1)} collective-permute-done((f32[72,128]{1,0:T(8,128)S(1)}, f32[72,128]{1,0:T(8,128)S(1)}, u32[]{:S(2)}, u32[]{:S(2)}) %collective-permute-start.10) | collective-permute-done | bytes 36896 | tf_op jit(solution)/shard_map/ppermute | solution.py:46
  50.2 0.6 collective-permute-done.9
  50.9 0.1 collective-permute-start.12
  50.9 0.9 collective-permute-start.13
  51.8 9.0 %mixing.1.mixing_ref = bf16[128,128]{1,0:T(8,128)(2,1)S(1)} custom-call(f32[72,128]{1,0:T(8,128)S(1)} %get-tuple-element.48.gram_ref, f32[64,128]{1,0:T(8,128)S(1)} %bitcast.13), custom_call_target="tpu_custom_call" | custom-call | bytes 38160000 | tf_op jit(solution)/shard_map/mixing/pallas_call | solution.py:187
  60.9 1.6 %spread.1 = (bf16[1,26,16,512]{3,2,1,0:T(8,128)(2,1)S(1)}, bf16[1,26,16,512]{3,2,1,0:T(8,128)(2,1)S(1)}, bf16[1,26,16,512]{3,2,1,0:T(8,128)(2,1)S(1)}, bf16[1,26...) custom-call(s32[11]{0:T(128)S(1)} %stack.43.info_ref.ids_ref, ...), custom_call_target="tpu_custom_call" | custom-call | bytes 5760000 | tf_op jit(solution)/shard_map/spread/pallas_call | solution.py:389
  62.5 0.6 collective-permute-start.14
  63.1 1.4 %collective-permute-start.15 = (bf16[1,26,16,512]{3,2,1,0:T(8,128)(2,1)S(1)}, bf16[1,26,16,512]{3,2,1,0:T(8,128)(2,1)S(1)}, u32[]{:S(2)}, u32[]{:S(2)}) collective-permute-start(bf16[1,26,16,512]{3,2,1,0:T(8,128)(2,1)S(1)} %get-tuple-element.54), channel_id=1, source_target_pairs={{0,16},{8,24},{16,0},{24,8},{1,17},{9,25},{17,1},{25,9},{2,18},{10... | collective-permute-start | bytes 1277960 | tf_op jit(solution)/shard_map/ppermute | solution.py:46
  64.5 4.5 %variation.6 = (bf16[32,4,16,512]{3,2,1,0:T(8,128)(2,1)}, bf16[32,4,16,512]{3,2,1,0:T(8,128)(2,1)}, f32[8,128]{1,0:T(8,128)S(1)}) custom-call(s32[11]{0:T(128)S(1)} %stack.43.info_ref.ids_ref, f32[4]{0:T(128)S(1)} %copy-done.8, bf16[512,512]{1,0:T(8,128)(2,1)S(1)} %fusion.order_ref, bf16[5,16,32,512]{3,2,1,0:T(8,128)(2,1)S(1)} %get-tuple-element.42.refs_0_, ...), custom_call_target="tpu_custom_call" | custom-call | bytes 15480000 | tf_op jit(solution)/shard_map/variation/pallas_call | solution.py:544
  69.0 1.6 %collective-permute-start.16 = (bf16[1,26,16,512]{3,2,1,0:T(8,128)(2,1)S(1)}, bf16[1,26,16,512]{3,2,1,0:T(8,128)(2,1)S(1)}, u32[]{:S(2)}, u32[]{:S(2)}) collective-permute-start(bf16[1,26,16,512]{3,2,1,0:T(8,128)(2,1)S(1)} %gate.6), channel_id=1, source_target_pairs={{0,8},{8,0},{16,24},{24,16},{1,9},{9,1},{17,25},{25,17},{2,10},{10... | collective-permute-start | bytes 1277960 | tf_op jit(solution)/shard_map/ppermute | solution.py:46
  70.6 0.7 collective-permute-start.17
  71.3 5.3 %variation.7 = (bf16[32,4,16,512]{3,2,1,0:T(8,128)(2,1)}, bf16[32,4,16,512]{3,2,1,0:T(8,128)(2,1)}, f32[8,128]{1,0:T(8,128)}) custom-call(s32[11]{0:T(128)S(1)} %stack.43.info_ref.ids_ref, f32[4]{0:T(128)S(1)} %copy-done.8, bf16[512,512]{1,0:T(8,128)(2,1)S(1)} %fusion.order_ref, ...), custom_call_target="tpu_custom_call", output_to_operand_aliasing={{0}: (7, {}), {1}: (8, {})} | custom-call | bytes 15480000 | tf_op jit(solution)/shard_map/variation/pallas_call | solution.py:544
  76.6 7.8 %variation.8 = (bf16[32,4,16,512]{3,2,1,0:T(8,128)(2,1)}, bf16[32,4,16,512]{3,2,1,0:T(8,128)(2,1)}, f32[8,128]{1,0:T(8,128)S(1)}) custom-call(s32[11]{0:T(128)S(1)} %stack.43.info_ref.ids_ref, f32[4]{0:T(128)S(1)} %copy-done.8, bf16[512,512]{1,0:T(8,128)(2,1)S(1)} %fusion.order_ref, ...), custom_call_target="tpu_custom_call", output_to_operand_aliasing={{0}: (8, {}), {1}: (9, {})} | custom-call | bytes 30960000 | tf_op jit(solution)/shard_map/variation/pallas_call | solution.py:544
  84.5 1.5 %collective-permute-start.19 = (bf16[1,26,16,512]{3,2,1,0:T(8,128)(2,1)S(1)}, bf16[1,26,16,512]{3,2,1,0:T(8,128)(2,1)S(1)}, u32[]{:S(2)}, u32[]{:S(2)}) collective-permute-start(bf16[1,26,16,512]{3,2,1,0:T(8,128)(2,1)S(1)} %gate.9), channel_id=1, source_target_pairs={{0,24},{8,16},{16,8},{24,0},{1,25},{9,17},{17,9},{25,1},{2,26},{10... | collective-permute-start | bytes 1277960 | tf_op jit(solution)/shard_map/ppermute | solution.py:46
  86.0 1.5 %collective-permute-start.18 = (bf16[1,26,16,512]{3,2,1,0:T(8,128)(2,1)S(1)}, bf16[1,26,16,512]{3,2,1,0:T(8,128)(2,1)S(1)}, u32[]{:S(2)}, u32[]{:S(2)}) collective-permute-start(bf16[1,26,16,512]{3,2,1,0:T(8,128)(2,1)S(1)} %gate.8), channel_id=1, source_target_pairs={{0,24},{8,16},{16,8},{24,0},{1,25},{9,17},{17,9},{25,1},{2,26},{10... | collective-permute-start | bytes 1277960 | tf_op jit(solution)/shard_map/ppermute | solution.py:46
  87.5 8.4 %variation.9 = (bf16[32,4,16,512]{3,2,1,0:T(8,128)(2,1)}, bf16[32,4,16,512]{3,2,1,0:T(8,128)(2,1)}, f32[8,128]{1,0:T(8,128)}) custom-call(s32[11]{0:T(128)S(1)} %stack.43.info_ref.ids_ref, f32[4]{0:T(128)S(1)} %copy-done.8, bf16[512,512]{1,0:T(8,128)(2,1)S(1)} %fusion.order_ref, ...), custom_call_target="tpu_custom_call", output_to_operand_aliasing={{0}: (8, {}), {1}: (9, {})} | custom-call | bytes 30960000 | tf_op jit(solution)/shard_map/variation/pallas_call | solution.py:544
  95.9 2.0 %collective-permute-done.19.refs_3_ = bf16[1,26,16,512]{3,2,1,0:T(8,128)(2,1)S(1)} collective-permute-done((bf16[1,26,16,512]{3,2,1,0:T(8,128)(2,1)S(1)}, bf16[1,26,16,512]{3,2,1,0:T(8,128)(2,1)S(1)}, u32[]{:S(2)}, u32[]{:S(2)}) %collective-permute-start.19) | collective-permute-done | bytes 426016 | tf_op jit(solution)/shard_map/ppermute | solution.py:46
  97.9 5.4 %variation.10 = (bf16[32,4,16,512]{3,2,1,0:T(8,128)(2,1)}, bf16[32,4,16,512]{3,2,1,0:T(8,128)(2,1)}, f32[8,128]{1,0:T(8,128)}) custom-call(s32[11]{0:T(128)S(1)} %stack.43.info_ref.ids_ref, f32[4]{0:T(128)S(1)} %copy-done.8, bf16[512,512]{1,0:T(8,128)(2,1)S(1)} %fusion.order_ref, ...), custom_call_target="tpu_custom_call", output_to_operand_aliasing={{0}: (7, {}), {1}: (8, {})} | custom-call | bytes 15480000 | tf_op jit(solution)/shard_map/variation/pallas_call | solution.py:544
  103.3 3.7 %collective-permute-done.18.refs_3_ = bf16[1,26,16,512]{3,2,1,0:T(8,128)(2,1)S(1)} collective-permute-done((bf16[1,26,16,512]{3,2,1,0:T(8,128)(2,1)S(1)}, bf16[1,26,16,512]{3,2,1,0:T(8,128)(2,1)S(1)}, u32[]{:S(2)}, u32[]{:S(2)}) %collective-permute-start.18) | collective-permute-done | bytes 426016 | tf_op jit(solution)/shard_map/ppermute | solution.py:46
  107.0 5.2 %variation.11 = (bf16[32,4,16,512]{3,2,1,0:T(8,128)(2,1)}, bf16[32,4,16,512]{3,2,1,0:T(8,128)(2,1)}, f32[8,128]{1,0:T(8,128)}) custom-call(s32[11]{0:T(128)S(1)} %stack.43.info_ref.ids_ref, f32[4]{0:T(128)S(1)} %copy-done.8, bf16[512,512]{1,0:T(8,128)(2,1)S(1)} %fusion.order_ref, ...), custom_call_target="tpu_custom_call", output_to_operand_aliasing={{0}: (7, {}), {1}: (8, {})} | custom-call | bytes 15480000 | tf_op jit(solution)/shard_map/variation/pallas_call | solution.py:544
  (35 shorter events, 0.1 us)
Async XLA Ops:
  3.9 8.3 %copy-start = (bf16[32,4,16,512]{3,2,1,0:T(8,128)(2,1)S(1)}, bf16[32,4,16,512]{3,2,1,0:T(8,128)(2,1)}, u32[]{:S(2)}) copy-start(bf16[32,4,16,512]{3,2,1,0:T(8,128)(2,1)} %frames_ref.5) | copy-start | bytes 6291460
  3.9 8.3 %copy-start.1 = (s32[32,16,512]{2,1,0:T(8,128)S(1)}, s32[32,16,512]{2,1,0:T(8,128)}, u32[]{:S(2)}) copy-start(s32[32,16,512]{2,1,0:T(8,128)} %valid_ref.5) | copy-start | bytes 3145732
  3.9 17.1 %collective-permute-start.4 = (bf16[1,16,32,512]{3,2,1,0:T(8,128)(2,1)}, bf16[1,16,32,512]{3,2,1,0:T(8,128)(2,1)}, u32[]{:S(2)}, u32[]{:S(2)}) collective-permute-start(bf16[1,16,32,512]{3,2,1,0:T(8,128)(2,1)} %get-tuple-element.40.refs_2_), channel_id=1, source_target_pairs={{0,24},{8,16},{16,8},{24,0},{1,25},{9,17},{17,9},{25,1},{2,26},{10... | collective-permute-start | bytes 1572872 | tf_op jit(solution)/shard_map/ppermute | solution.py:46
  11.2 20.5 %collective-permute-start.2 = (bf16[1,16,32,512]{3,2,1,0:T(8,128)(2,1)}, bf16[1,16,32,512]{3,2,1,0:T(8,128)(2,1)}, u32[]{:S(2)}, u32[]{:S(2)}) collective-permute-start(bf16[1,16,32,512]{3,2,1,0:T(8,128)(2,1)} %get-tuple-element.38.refs_0_), channel_id=1, source_target_pairs={{0,8},{8,0},{16,24},{24,16},{1,9},{9,1},{17,25},{25,17},{2,10},{10... | collective-permute-start | bytes 1572872 | tf_op jit(solution)/shard_map/ppermute | solution.py:46
  11.8 19.9 %collective-permute-start.3 = (bf16[1,16,32,512]{3,2,1,0:T(8,128)(2,1)}, bf16[1,16,32,512]{3,2,1,0:T(8,128)(2,1)}, u32[]{:S(2)}, u32[]{:S(2)}) collective-permute-start(bf16[1,16,32,512]{3,2,1,0:T(8,128)(2,1)} %get-tuple-element.39.refs_1_), channel_id=1, source_target_pairs={{0,16},{8,24},{16,0},{24,8},{1,17},{9,25},{17,1},{25,9},{2,18},{10... | collective-permute-start | bytes 1572872 | tf_op jit(solution)/shard_map/ppermute | solution.py:46
  12.2 1.0 copy-start.2
  13.3 1.0 copy-start.4
  14.3 1.0 copy-start.5
  15.4 1.0 copy-start.6
  16.4 15.3 %copy-start.3 = (bf16[1,16,32,512]{3,2,1,0:T(8,128)(2,1)S(1)}, bf16[1,16,32,512]{3,2,1,0:T(8,128)(2,1)}, u32[]{:S(2)}) copy-start(bf16[1,16,32,512]{3,2,1,0:T(8,128)(2,1)} %get-tuple-element.41.refs_3_) | copy-start | bytes 1572868
  19.0 31.8 %collective-permute-start = (bf16[5,5,32,512]{3,2,1,0:T(8,128)(2,1)S(1)}, bf16[5,5,32,512]{3,2,1,0:T(8,128)(2,1)S(1)}, u32[]{:S(2)}, u32[]{:S(2)}) collective-permute-start(bf16[5,5,32,512]{3,2,1,0:T(8,128)(2,1)S(1)} %get-tuple-element.43), channel_id=1, source_target_pairs={{0,1},{1,0},{2,3},{3,2},{4,5},{5,4},{6,7},{7,6},{8,9},{9,8},{10,11... | collective-permute-start | bytes 2457608 | tf_op jit(solution)/shard_map/ppermute | solution.py:36
  19.1 31.8 %collective-permute-start.1 = (bf16[5,5,32,512]{3,2,1,0:T(8,128)(2,1)S(1)}, bf16[5,5,32,512]{3,2,1,0:T(8,128)(2,1)S(1)}, u32[]{:S(2)}, u32[]{:S(2)}) collective-permute-start(bf16[5,5,32,512]{3,2,1,0:T(8,128)(2,1)S(1)} %get-tuple-element.44), channel_id=1, source_target_pairs={{1,2},{2,1},{3,4},{4,3},{5,6},{6,5},{9,10},{10,9},{11,12},{12,11},... | collective-permute-start | bytes 2457608 | tf_op jit(solution)/shard_map/ppermute | solution.py:36
  34.0 17.8 %copy-start.7 = (f32[128,64]{0,1:T(8,128)S(1)}, f32[128,64]{0,1:T(8,128)}, u32[]{:S(2)}) copy-start(f32[128,64]{0,1:T(8,128)} %param.8) | copy-start | bytes 98308
  34.1 1.3 %collective-permute-start.5 = (f32[72,128]{1,0:T(8,128)S(1)}, f32[72,128]{1,0:T(8,128)S(1)}, u32[]{:S(2)}, u32[]{:S(2)}) collective-permute-start(f32[72,128]{1,0:T(8,128)S(1)} %get-tuple-element.45), channel_id=1, source_target_pairs={{0,1},{1,0},{2,3},{3,2},{4,5},{5,4},{6,7},{7,6},{8,9},{9,8},{10,11... | collective-permute-start | bytes 110600 | tf_op jit(solution)/shard_map/ppermute | solution.py:46
  35.3 5.8 %collective-permute-start.8 = (f32[72,128]{1,0:T(8,128)S(1)}, f32[72,128]{1,0:T(8,128)S(1)}, u32[]{:S(2)}, u32[]{:S(2)}) collective-permute-start(f32[72,128]{1,0:T(8,128)S(1)} %add.64), channel_id=1, source_target_pairs={{0,6},{1,7},{2,4},{3,5},{4,2},{5,3},{6,0},{7,1},{8,14},{9,15},{10,... | collective-permute-start | bytes 110600 | tf_op jit(solution)/shard_map/ppermute | solution.py:46
  38.9 4.9 %collective-permute-start.7 = (f32[72,128]{1,0:T(8,128)S(1)}, f32[72,128]{1,0:T(8,128)S(1)}, u32[]{:S(2)}, u32[]{:S(2)}) collective-permute-start(f32[72,128]{1,0:T(8,128)S(1)} %add.64), channel_id=1, source_target_pairs={{0,4},{1,5},{2,6},{3,7},{4,0},{5,1},{6,2},{7,3},{8,12},{9,13},{10,... | collective-permute-start | bytes 110600 | tf_op jit(solution)/shard_map/ppermute | solution.py:46
  38.9 4.9 %collective-permute-start.6 = (f32[72,128]{1,0:T(8,128)S(1)}, f32[72,128]{1,0:T(8,128)S(1)}, u32[]{:S(2)}, u32[]{:S(2)}) collective-permute-start(f32[72,128]{1,0:T(8,128)S(1)} %add.64), channel_id=1, source_target_pairs={{0,2},{1,3},{2,0},{3,1},{4,6},{5,7},{6,4},{7,5},{8,10},{9,11},{10,... | collective-permute-start | bytes 110600 | tf_op jit(solution)/shard_map/ppermute | solution.py:46
  43.8 4.9 %collective-permute-start.11 = (f32[72,128]{1,0:T(8,128)S(1)}, f32[72,128]{1,0:T(8,128)S(1)}, u32[]{:S(2)}, u32[]{:S(2)}) collective-permute-start(f32[72,128]{1,0:T(8,128)S(1)} %add_add_fusion.1), channel_id=1, source_target_pairs={{0,24},{8,16},{16,8},{24,0},{1,25},{9,17},{17,9},{25,1},{2,26},{10... | collective-permute-start | bytes 110600 | tf_op jit(solution)/shard_map/ppermute | solution.py:46
  46.2 4.0 %collective-permute-start.10 = (f32[72,128]{1,0:T(8,128)S(1)}, f32[72,128]{1,0:T(8,128)S(1)}, u32[]{:S(2)}, u32[]{:S(2)}) collective-permute-start(f32[72,128]{1,0:T(8,128)S(1)} %add_add_fusion.1), channel_id=1, source_target_pairs={{0,16},{8,24},{16,0},{24,8},{1,17},{9,25},{17,1},{25,9},{2,18},{10... | collective-permute-start | bytes 110600 | tf_op jit(solution)/shard_map/ppermute | solution.py:46
  46.8 4.0 %collective-permute-start.9 = (f32[72,128]{1,0:T(8,128)S(1)}, f32[72,128]{1,0:T(8,128)S(1)}, u32[]{:S(2)}, u32[]{:S(2)}) collective-permute-start(f32[72,128]{1,0:T(8,128)S(1)} %add_add_fusion.1), channel_id=1, source_target_pairs={{0,8},{8,0},{16,24},{24,16},{1,9},{9,1},{17,25},{25,17},{2,10},{10... | collective-permute-start | bytes 110600 | tf_op jit(solution)/shard_map/ppermute | solution.py:46
  50.8 13.6 %copy-start.8 = (f32[4]{0:T(128)S(1)}, f32[4]{0:T(128)}, u32[]{:S(2)}) copy-start(f32[4]{0:T(128)} %weight_ref.11) | copy-start | bytes 52
  50.9 10.0 %collective-permute-start.12 = (bf16[1,5,128,512]{3,2,1,0:T(8,128)(2,1)S(1)}, bf16[1,5,128,512]{3,2,1,0:T(8,128)(2,1)S(1)}, u32[]{:S(2)}, u32[]{:S(2)}) collective-permute-start(bf16[1,5,128,512]{3,2,1,0:T(8,128)(2,1)S(1)} %get-tuple-element.50), channel_id=1, source_target_pairs={{0,1},{1,0},{2,3},{3,2},{4,5},{5,4},{6,7},{7,6},{8,9},{9,8},{10,11... | collective-permute-start | bytes 1966088 | tf_op jit(solution)/shard_map/ppermute | solution.py:36
  50.9 9.9 %collective-permute-start.13 = (bf16[1,5,128,512]{3,2,1,0:T(8,128)(2,1)S(1)}, bf16[1,5,128,512]{3,2,1,0:T(8,128)(2,1)S(1)}, u32[]{:S(2)}, u32[]{:S(2)}) collective-permute-start(bf16[1,5,128,512]{3,2,1,0:T(8,128)(2,1)S(1)} %get-tuple-element.51), channel_id=1, source_target_pairs={{1,2},{2,1},{3,4},{4,3},{5,6},{6,5},{9,10},{10,9},{11,12},{12,11},... | collective-permute-start | bytes 1966088 | tf_op jit(solution)/shard_map/ppermute | solution.py:36
  62.5 14.1 %collective-permute-start.14 = (bf16[1,26,16,512]{3,2,1,0:T(8,128)(2,1)S(1)}, bf16[1,26,16,512]{3,2,1,0:T(8,128)(2,1)S(1)}, u32[]{:S(2)}, u32[]{:S(2)}) collective-permute-start(bf16[1,26,16,512]{3,2,1,0:T(8,128)(2,1)S(1)} %get-tuple-element.53), channel_id=1, source_target_pairs={{0,8},{8,0},{16,24},{24,16},{1,9},{9,1},{17,25},{25,17},{2,10},{10... | collective-permute-start | bytes 1277960 | tf_op jit(solution)/shard_map/ppermute | solution.py:46
  63.1 13.5 %collective-permute-start.15 = (bf16[1,26,16,512]{3,2,1,0:T(8,128)(2,1)S(1)}, bf16[1,26,16,512]{3,2,1,0:T(8,128)(2,1)S(1)}, u32[]{:S(2)}, u32[]{:S(2)}) collective-permute-start(bf16[1,26,16,512]{3,2,1,0:T(8,128)(2,1)S(1)} %get-tuple-element.54), channel_id=1, source_target_pairs={{0,16},{8,24},{16,0},{24,8},{1,17},{9,25},{17,1},{25,9},{2,18},{10... | collective-permute-start | bytes 1277960 | tf_op jit(solution)/shard_map/ppermute | solution.py:46
  69.0 15.5 %collective-permute-start.16 = (bf16[1,26,16,512]{3,2,1,0:T(8,128)(2,1)S(1)}, bf16[1,26,16,512]{3,2,1,0:T(8,128)(2,1)S(1)}, u32[]{:S(2)}, u32[]{:S(2)}) collective-permute-start(bf16[1,26,16,512]{3,2,1,0:T(8,128)(2,1)S(1)} %gate.6), channel_id=1, source_target_pairs={{0,8},{8,0},{16,24},{24,16},{1,9},{9,1},{17,25},{25,17},{2,10},{10... | collective-permute-start | bytes 1277960 | tf_op jit(solution)/shard_map/ppermute | solution.py:46
  70.6 13.9 %collective-permute-start.17 = (bf16[1,26,16,512]{3,2,1,0:T(8,128)(2,1)S(1)}, bf16[1,26,16,512]{3,2,1,0:T(8,128)(2,1)S(1)}, u32[]{:S(2)}, u32[]{:S(2)}) collective-permute-start(bf16[1,26,16,512]{3,2,1,0:T(8,128)(2,1)S(1)} %gate.7), channel_id=1, source_target_pairs={{0,16},{8,24},{16,0},{24,8},{1,17},{9,25},{17,1},{25,9},{2,18},{10... | collective-permute-start | bytes 1277960 | tf_op jit(solution)/shard_map/ppermute | solution.py:46
  84.5 13.4 %collective-permute-start.19 = (bf16[1,26,16,512]{3,2,1,0:T(8,128)(2,1)S(1)}, bf16[1,26,16,512]{3,2,1,0:T(8,128)(2,1)S(1)}, u32[]{:S(2)}, u32[]{:S(2)}) collective-permute-start(bf16[1,26,16,512]{3,2,1,0:T(8,128)(2,1)S(1)} %gate.9), channel_id=1, source_target_pairs={{0,24},{8,16},{16,8},{24,0},{1,25},{9,17},{17,9},{25,1},{2,26},{10... | collective-permute-start | bytes 1277960 | tf_op jit(solution)/shard_map/ppermute | solution.py:46
  86.0 21.0 %collective-permute-start.18 = (bf16[1,26,16,512]{3,2,1,0:T(8,128)(2,1)S(1)}, bf16[1,26,16,512]{3,2,1,0:T(8,128)(2,1)S(1)}, u32[]{:S(2)}, u32[]{:S(2)}) collective-permute-start(bf16[1,26,16,512]{3,2,1,0:T(8,128)(2,1)S(1)} %gate.8), channel_id=1, source_target_pairs={{0,24},{8,16},{16,8},{24,0},{1,25},{9,17},{17,9},{25,1},{2,26},{10... | collective-permute-start | bytes 1277960 | tf_op jit(solution)/shard_map/ppermute | solution.py:46
